TPU v7x, 32 devices: a whole 2x2x4 slice. The times are simulated.
32 devices in a mesh: dp: 16 (over z, y, x), ctx: 2 (over core).
Axes of the slice: x: 2, y: 2, z: 4, core: 2. Of those that a mesh axis runs over, the one named last changes fastest.
Arguments:
- tokens: bfloat16 [16, 256, 1152], P('dp', 'ctx'), may hold values from -6 to 6
- cotangent: bfloat16 [16, 256, 1152], P('dp', 'ctx'), may hold values from -6 to 6
- segment: int32 [16, 256], P('dp'), may hold values from 0 to 3, as said below
- rows: int32 [16, 256], P('dp'), may hold values from 0 to 31, as said below
- columns: int32 [16, 256], P('dp'), may hold values from 0 to 7, as said below
- padding: int32 [16, 256], P('dp'), may hold values from 0 to 1, as said below
- timesteps: int32 [16, 4], P('dp'), may hold values from 0 to 999
- encoder_modulate: bfloat16 [1152, 6912], P('dp'), may hold values from -0.1875 to 0.1875
- encoder_offset: bfloat16 [6912], P('dp'), may hold values from -3 to 3
- encoder_triple: bfloat16 [1152, 3456], P('dp'), may hold values from -0.1875 to 0.1875
- encoder_gains: bfloat16 [2, 1152], P(None, 'dp'), may hold values from 0.25 to 1.75
- encoder_mixing: bfloat16 [1152, 1152], P('dp'), may hold values from -1.5 to 1.5
- encoder_expand: bfloat16 [1152, 6144], P('dp'), may hold values from -0.1875 to 0.1875
- encoder_reduce: bfloat16 [3072, 1152], P('dp'), may hold values from -0.109375 to 0.109375
- decoder_modulate: bfloat16 [1152, 6912], P('dp'), may hold values from -0.1875 to 0.1875
- decoder_offset: bfloat16 [6912], P('dp'), may hold values from -3 to 3
- decoder_triple: bfloat16 [1152, 3456], P('dp'), may hold values from -0.1875 to 0.1875
- decoder_gains: bfloat16 [2, 1152], P(None, 'dp'), may hold values from 0.25 to 1.75
- decoder_mixing: bfloat16 [1152, 1152], P('dp'), may hold values from -1.5 to 1.5
- decoder_expand: bfloat16 [1152, 6144], P('dp'), may hold values from -0.1875 to 0.1875
- decoder_reduce: bfloat16 [3072, 1152], P('dp'), may hold values from -0.109375 to 0.109375
Outputs:
- velocity: bfloat16 [16, 256, 1152], P('dp', 'ctx')
- latent: bfloat16 [16, 256, 1152], P('dp', 'ctx')
- token_grad: float32 [16, 256, 1152], P('dp', 'ctx')
- encoder_modulate_grad: float32 [1152, 6912], P('dp')
- encoder_offset_grad: float32 [6912], P('dp')
- encoder_triple_grad: float32 [1152, 3456], P('dp')
- encoder_gains_grad: float32 [2, 1152], P(None, 'dp')
- encoder_mixing_grad: float32 [1152, 1152], P('dp')
- encoder_expand_grad: float32 [1152, 6144], P('dp')
- encoder_reduce_grad: float32 [3072, 1152], P('dp')
- decoder_modulate_grad: float32 [1152, 6912], P('dp')
- decoder_offset_grad: float32 [6912], P('dp')
- decoder_triple_grad: float32 [1152, 3456], P('dp')
- decoder_gains_grad: float32 [2, 1152], P(None, 'dp')
- decoder_mixing_grad: float32 [1152, 1152], P('dp')
- decoder_expand_grad: float32 [1152, 6144], P('dp')
- decoder_reduce_grad: float32 [3072, 1152], P('dp')
Inputs may be any that keep to these rules, and one draw needn't show every extreme that they name: `segment`: each sequence holds image 0 from slot 0, then image 1, then image 2 (which may be empty), each a full rectangle of patches in row-major order of width 2 to 8; all later slots are padding with number 3, at least one in each sequence. Image 1 covers slots 256/2 - 1 and 128. `rows`: row of the slot's patch in its image; 0 on padding. `columns`: column of the slot's patch in its image; 0 on padding. `padding`: 1 exactly where segment is 3.
All inputs are finite; a program needn't handle non-finite values.
Results may differ from a plain program's by a relative error of at most 0.04.
Values may be sent and summed in bfloat16 or wider, within the bound.
A program may use at most 576 MiB of HBM per device.

v0:
```python
import math

import jax
import jax.numpy as jnp
from jax import lax
from jax.sharding import PartitionSpec as P

HEADS = 16
HD = 72


def layer_norm(values):
    center = values - jnp.mean(values, axis=-1, keepdims=True)
    spread = jnp.mean(center * center, axis=-1, keepdims=True)
    return center * lax.rsqrt(spread + 1e-06)


def head_norm(values, gain):
    shaped = values.reshape(values.shape[:-1] + (HEADS, HD))
    scaled = shaped * lax.rsqrt(jnp.mean(shaped * shaped, axis=-1, keepdims=True) + 1e-06)
    return scaled * gain.reshape(HEADS, HD)


def rope_tables(rows, columns):
    quarter = HD // 4
    freqs = jnp.exp(jnp.arange(quarter, dtype=jnp.float32) * (-math.log(10000.0) / quarter))
    places = jnp.stack([rows, columns], axis=-1).astype(jnp.float32)
    angles = places[..., None] * freqs
    return (jnp.cos(angles), jnp.sin(angles))


def rotate(values, cosine, sine):
    shaped = values.reshape(values.shape[:-1] + (2, 2, HD // 4))
    first = shaped[..., 0, :]
    second = shaped[..., 1, :]
    cosine = cosine[..., None, :, :]
    sine = sine[..., None, :, :]
    turned = jnp.stack([first * cosine - second * sine, first * sine + second * cosine], axis=-2)
    return turned.reshape(values.shape)


def time_embed(timesteps, segment, width):
    half_width = width // 2
    freqs = jnp.exp(jnp.arange(half_width, dtype=jnp.float32) * (-math.log(10000.0) / half_width))
    picks = (segment[..., None] == jnp.arange(timesteps.shape[-1], dtype=jnp.int32)).astype(
        jnp.float32
    )
    times = jnp.sum(picks * timesteps[:, None, :].astype(jnp.float32), axis=-1)
    angles = times[..., None] * freqs
    return jnp.concatenate([jnp.cos(angles), jnp.sin(angles)], axis=-1)


def qk_prepare(query_raw, key_raw, gains, cosine, sine):
    return (
        rotate(head_norm(query_raw, gains[0]), cosine, sine),
        rotate(head_norm(key_raw, gains[1]), cosine, sine),
    )


def swish_product(gate, up):
    return jax.nn.silu(gate) * up


def attention_scores(queries, keys, allowed):
    scores = jnp.einsum("sqhd,skhd->shqk", queries, keys, preferred_element_type=jnp.float32) * (
        1.0 / math.sqrt(HD)
    )
    return jnp.where(allowed[:, None], scores, -1e30)


def dense(values, weight):
    return jnp.dot(values, weight, preferred_element_type=jnp.float32)


def dense_back(grads, weight):
    return lax.dot_general(
        grads, weight, (((1,), (1,)), ((), ())), preferred_element_type=jnp.float32
    )


def outer_sum(values, grads):
    return lax.dot_general(
        values, grads, (((0,), (0,)), ((), ())), preferred_element_type=jnp.float32
    )


def block_forward(flat, act_low, weights, context):
    batch, half, allowed, cosine, sine = context
    modulate, triple, mixing, expand, reduce_w, offset, gains = (
        lax.all_gather(weights[0], "dp", axis=0, tiled=True),
        lax.all_gather(weights[1], "dp", axis=0, tiled=True),
        lax.all_gather(weights[2], "dp", axis=0, tiled=True),
        lax.all_gather(weights[3], "dp", axis=0, tiled=True),
        lax.all_gather(weights[4], "dp", axis=0, tiled=True),
        lax.all_gather(weights[5], "dp", axis=0, tiled=True),
        lax.all_gather(weights[6], "dp", axis=1, tiled=True),
    )
    gains = gains.astype(jnp.float32)
    width = flat.shape[1]
    modulation = dense(act_low, modulate) + offset.astype(jnp.float32)
    shift1, scale1, gate1, shift2, scale2, gate2 = jnp.split(modulation, 6, axis=1)
    lifted1 = (layer_norm(flat) * (1.0 + scale1) + shift1).astype(jnp.bfloat16)
    projected = dense(lifted1, triple)
    query_raw, key_raw, value_raw = jnp.split(projected, 3, axis=1)
    queries, keys = qk_prepare(query_raw, key_raw, gains, cosine, sine)
    queries = queries.astype(jnp.bfloat16).reshape(batch, half, HEADS, HD)
    keys_local = keys.astype(jnp.bfloat16).reshape(batch, half, width)
    values_local = value_raw.astype(jnp.bfloat16).reshape(batch, half, width)
    key_whole, value_whole = (
        lax.all_gather(keys_local, "ctx", axis=1, tiled=True),
        lax.all_gather(values_local, "ctx", axis=1, tiled=True),
    )
    key_heads = key_whole.reshape(batch, -1, HEADS, HD)
    value_heads = value_whole.reshape(batch, -1, HEADS, HD)
    scores = attention_scores(queries, key_heads, allowed)
    top = jnp.max(scores, axis=-1, keepdims=True)
    raised = jnp.exp(scores - top)
    total = jnp.sum(raised, axis=-1, keepdims=True)
    softmax_low = (raised / total).astype(jnp.bfloat16)
    logsum = top + jnp.log(total)
    mixed = jnp.einsum(
        "shqk,skhd->sqhd", softmax_low, value_heads, preferred_element_type=jnp.float32
    )
    mixed_low = mixed.reshape(-1, width).astype(jnp.bfloat16)
    attended = dense(mixed_low, mixing)
    resid = flat + gate1 * attended
    lifted2 = (layer_norm(resid) * (1.0 + scale2) + shift2).astype(jnp.bfloat16)
    expanded = dense(lifted2, expand)
    gate, up = jnp.split(expanded, 2, axis=1)
    hidden = swish_product(gate, up).astype(jnp.bfloat16)
    feed = dense(hidden, reduce_w)
    output = resid + gate2 * feed
    kept = (
        act_low,
        modulation,
        flat,
        lifted1,
        query_raw,
        key_raw,
        gains,
        queries,
        key_heads,
        value_heads,
        logsum,
        mixed_low,
        attended,
        resid,
        lifted2,
        expanded,
        hidden,
        feed,
    )
    return (output, kept)


def reduce_grads(grads):
    return (
        lax.psum_scatter(grads[0], "dp", scatter_dimension=0, tiled=True),
        lax.psum_scatter(grads[1], "dp", scatter_dimension=0, tiled=True),
        lax.psum_scatter(grads[2], "dp", scatter_dimension=0, tiled=True),
        lax.psum_scatter(grads[3], "dp", scatter_dimension=1, tiled=True),
        lax.psum_scatter(grads[4], "dp", scatter_dimension=0, tiled=True),
        lax.psum_scatter(grads[5], "dp", scatter_dimension=0, tiled=True),
        lax.psum_scatter(grads[6], "dp", scatter_dimension=0, tiled=True),
    )


def block_backward(grad_out, kept, weights, context, need_act):
    batch, half, allowed, cosine, sine = context
    modulate, triple, mixing, expand, reduce_w = (
        lax.all_gather(weights[0], "dp", axis=0, tiled=True),
        lax.all_gather(weights[1], "dp", axis=0, tiled=True),
        lax.all_gather(weights[2], "dp", axis=0, tiled=True),
        lax.all_gather(weights[3], "dp", axis=0, tiled=True),
        lax.all_gather(weights[4], "dp", axis=0, tiled=True),
    )
    (
        act_low,
        modulation,
        flat,
        lifted1,
        query_raw,
        key_raw,
        gains,
        queries,
        key_heads,
        value_heads,
        logsum,
        mixed_low,
        attended,
        resid,
        lifted2,
        expanded,
        hidden,
        feed,
    ) = kept
    width = flat.shape[1]
    shift1, scale1, gate1, shift2, scale2, gate2 = jnp.split(modulation, 6, axis=1)
    grad_feed = (grad_out * gate2).astype(jnp.bfloat16)
    reduce_grad = outer_sum(hidden, grad_feed)
    grad_hidden = dense_back(grad_feed, reduce_w)
    gate, up = jnp.split(expanded, 2, axis=1)
    unused_out, swish_pull = jax.vjp(swish_product, gate, up)
    grad_gate, grad_up = swish_pull(grad_hidden)
    grad_expanded = jnp.concatenate([grad_gate, grad_up], axis=1).astype(jnp.bfloat16)
    expand_grad = outer_sum(lifted2, grad_expanded)
    grad_lifted2 = dense_back(grad_expanded, expand)
    normed_second, second_pull = jax.vjp(layer_norm, resid)
    grad_resid = grad_out + second_pull(grad_lifted2 * (1.0 + scale2))[0]
    grad_attended = (grad_resid * gate1).astype(jnp.bfloat16)
    mixing_grad = outer_sum(mixed_low, grad_attended)
    grad_mixed = (
        dense_back(grad_attended, mixing).astype(jnp.bfloat16).reshape(batch, half, HEADS, HD)
    )
    scores = attention_scores(queries, key_heads, allowed)
    chances = jnp.exp(scores - logsum)
    grad_chances = jnp.einsum(
        "sqhd,skhd->shqk", grad_mixed, value_heads, preferred_element_type=jnp.float32
    )
    grad_values = jnp.einsum(
        "shqk,sqhd->skhd",
        chances.astype(jnp.bfloat16),
        grad_mixed,
        preferred_element_type=jnp.float32,
    )
    grad_scores = (
        chances * (grad_chances - jnp.sum(chances * grad_chances, axis=-1, keepdims=True))
    ).astype(jnp.bfloat16)
    scale = 1.0 / math.sqrt(HD)
    grad_queries = (
        jnp.einsum("shqk,skhd->sqhd", grad_scores, key_heads, preferred_element_type=jnp.float32)
        * scale
    )
    grad_keys = (
        jnp.einsum("shqk,sqhd->skhd", grad_scores, queries, preferred_element_type=jnp.float32)
        * scale
    )
    grad_keys, grad_values = (
        lax.psum_scatter(
            grad_keys.reshape(batch, -1, width).astype(jnp.bfloat16),
            "ctx",
            scatter_dimension=1,
            tiled=True,
        ).astype(jnp.float32),
        lax.psum_scatter(
            grad_values.reshape(batch, -1, width).astype(jnp.bfloat16),
            "ctx",
            scatter_dimension=1,
            tiled=True,
        ).astype(jnp.float32),
    )

    def prepare(query_in, key_in, gain_in):
        return qk_prepare(query_in, key_in, gain_in, cosine, sine)

    unused_pair, prepare_pull = jax.vjp(prepare, query_raw, key_raw, gains)
    grad_query_raw, grad_key_raw, gains_grad = prepare_pull(
        (grad_queries.reshape(-1, HEADS, HD), grad_keys.reshape(-1, HEADS, HD))
    )
    grad_projected = jnp.concatenate(
        [grad_query_raw, grad_key_raw, grad_values.reshape(-1, width)], axis=1
    ).astype(jnp.bfloat16)
    triple_grad = outer_sum(lifted1, grad_projected)
    grad_lifted1 = dense_back(grad_projected, triple)
    normed_first, first_pull = jax.vjp(layer_norm, flat)
    grad_flat = grad_resid + first_pull(grad_lifted1 * (1.0 + scale1))[0]
    grad_modulation = jnp.concatenate(
        [
            grad_lifted1,
            grad_lifted1 * normed_first,
            grad_resid * attended,
            grad_lifted2,
            grad_lifted2 * normed_second,
            grad_out * feed,
        ],
        axis=1,
    ).astype(jnp.bfloat16)
    modulate_grad = outer_sum(act_low, grad_modulation)
    offset_grad = jnp.sum(grad_modulation, axis=0, dtype=jnp.float32)
    grad_act = dense_back(grad_modulation, modulate) if need_act else None
    summed = reduce_grads(
        (modulate_grad, offset_grad, triple_grad, gains_grad, mixing_grad, expand_grad, reduce_grad)
    )
    return (grad_flat, grad_act, summed)


def sum_cores(grads):
    return (
        lax.psum(grads[0].astype(jnp.bfloat16), "ctx").astype(jnp.float32),
        lax.psum(grads[1].astype(jnp.bfloat16), "ctx").astype(jnp.float32),
        lax.psum(grads[2].astype(jnp.bfloat16), "ctx").astype(jnp.float32),
        lax.psum(grads[3].astype(jnp.bfloat16), "ctx").astype(jnp.float32),
        lax.psum(grads[4].astype(jnp.bfloat16), "ctx").astype(jnp.float32),
        lax.psum(grads[5].astype(jnp.bfloat16), "ctx").astype(jnp.float32),
        lax.psum(grads[6].astype(jnp.bfloat16), "ctx").astype(jnp.float32),
    )


def local(
    tokens,
    cotangent,
    segment,
    rows,
    columns,
    padding,
    timesteps,
    encoder_modulate,
    encoder_offset,
    encoder_triple,
    encoder_gains,
    encoder_mixing,
    encoder_expand,
    encoder_reduce,
    decoder_modulate,
    decoder_offset,
    decoder_triple,
    decoder_gains,
    decoder_mixing,
    decoder_expand,
    decoder_reduce,
):
    batch, half, width = tokens.shape
    start = lax.axis_index("ctx") * half
    segment_local = lax.dynamic_slice_in_dim(segment, start, half, 1)
    rows_local = lax.dynamic_slice_in_dim(rows, start, half, 1)
    columns_local = lax.dynamic_slice_in_dim(columns, start, half, 1)
    padding_local = lax.dynamic_slice_in_dim(padding, start, half, 1)
    place_query = start + jnp.arange(half, dtype=jnp.int32)
    place_key = jnp.arange(segment.shape[1], dtype=jnp.int32)
    allowed = (segment_local[:, :, None] == segment[:, None, :]) & (
        (padding[:, None, :] == 0) | (place_query[None, :, None] == place_key[None, None, :])
    )
    cosine, sine = rope_tables(rows_local.reshape(-1), columns_local.reshape(-1))
    context = (batch, half, allowed, cosine, sine)
    cond = time_embed(timesteps, segment_local, width).reshape(-1, width)
    valid = (1 - padding_local).astype(jnp.float32).reshape(-1, 1)
    flat = tokens.reshape(-1, width).astype(jnp.float32)
    encoder_set = (
        encoder_modulate,
        encoder_triple,
        encoder_mixing,
        encoder_expand,
        encoder_reduce,
        encoder_offset,
        encoder_gains,
    )
    decoder_set = (
        decoder_modulate,
        decoder_triple,
        decoder_mixing,
        decoder_expand,
        decoder_reduce,
        decoder_offset,
        decoder_gains,
    )
    encoder_act = jax.nn.silu(cond).astype(jnp.bfloat16)
    encoder_out, encoder_kept = block_forward(flat, encoder_act, encoder_set, context)
    latent_full = valid * encoder_out
    decoder_pre = latent_full + cond
    decoder_act = jax.nn.silu(decoder_pre).astype(jnp.bfloat16)
    decoder_out, decoder_kept = block_forward(flat, decoder_act, decoder_set, context)
    velocity = (valid * decoder_out).astype(jnp.bfloat16).reshape(batch, half, width)
    grad_out = valid * cotangent.reshape(-1, width).astype(jnp.float32)
    decoder_flat_grad, grad_act, decoder_grads = block_backward(
        grad_out, decoder_kept, decoder_set, context, True
    )
    decoder_grads = sum_cores(decoder_grads)
    unused_silu, silu_pull = jax.vjp(jax.nn.silu, decoder_pre)
    grad_latent = valid * silu_pull(grad_act)[0]
    unused_again, encoder_again = block_forward(flat, encoder_act, encoder_set, context)
    encoder_flat_grad, unused_act, encoder_grads = block_backward(
        grad_latent, encoder_again, encoder_set, context, False
    )
    encoder_grads = sum_cores(encoder_grads)
    token_grad = (decoder_flat_grad + encoder_flat_grad).reshape(batch, half, width)
    latent = latent_full.astype(jnp.bfloat16).reshape(batch, half, width)
    return (
        velocity,
        latent,
        token_grad,
        encoder_grads[0],
        encoder_grads[1],
        encoder_grads[2],
        encoder_grads[3],
        encoder_grads[4],
        encoder_grads[5],
        encoder_grads[6],
        decoder_grads[0],
        decoder_grads[1],
        decoder_grads[2],
        decoder_grads[3],
        decoder_grads[4],
        decoder_grads[5],
        decoder_grads[6],
    )


def solution(mesh):
    return jax.shard_map(
        local,
        mesh=mesh,
        in_specs=(
            P("dp", "ctx", None),
            P("dp", "ctx", None),
            P("dp", None),
            P("dp", None),
            P("dp", None),
            P("dp", None),
            P("dp", None),
            P("dp", None),
            P("dp"),
            P("dp", None),
            P(None, "dp"),
            P("dp", None),
            P("dp", None),
            P("dp", None),
            P("dp", None),
            P("dp"),
            P("dp", None),
            P(None, "dp"),
            P("dp", None),
            P("dp", None),
            P("dp", None),
        ),
        out_specs=(
            P("dp", "ctx", None),
            P("dp", "ctx", None),
            P("dp", "ctx", None),
            P("dp", None),
            P("dp"),
            P("dp", None),
            P(None, "dp"),
            P("dp", None),
            P("dp", None),
            P("dp", None),
            P("dp", None),
            P("dp"),
            P("dp", None),
            P(None, "dp"),
            P("dp", None),
            P("dp", None),
            P("dp", None),
        ),
        check_vma=False,
    )
```

profile of v0, /device:TPU:0, one launch (start us, length us, event | category | flops | bytes accessed | tf_op | source)
XLA Modules:
  0.0 4595.2 jit_solution(2632357616696663817)
XLA Ops:
  16.5 80.7 %all-reduce.23 = (bf16[6912]{0:T(1024)(128)(2,1)S(1)}, bf16[6912]{0:T(1024)(128)(2,1)S(1)}) all-reduce(bf16[6912]{0:T(1024)(128)(2,1)S(1)} %dynamic-update-slice, bf16[6912]{0:T(1024)(128)(2,1)S(1)} %dynamic-update-slice.1), channel_id=1, replica_groups=mesh['dp'=16,'ctx'=2] {'dp'}, use_global_device_ids=true, to_apply=%add.12 | all-reduce | flops 13824 | bytes 55296
  97.6 35.8 all-gather.2
  134.9 37.7 all-gather.3
  176.6 22.5 all-gather.15.cloned.1.call-done
  209.3 99.7 %all-gather.17.cloned.1.call-done = bf16[1152,3456]{1,0:T(8,128)(2,1)} async-done(((bf16[72,3456]{1,0:T(8,128)(2,1)}), bf16[1152,3456]{1,0:T(8,128)(2,1)}) %all-gather.17.cloned.1.call-update) | async-done | bytes 7962640 | tf_op jit(solution)/shard_map/all_gather | solution.py:91
  328.7 45.5 all-gather.19.cloned.1.call-done
  380.0 162.7 %all-gather.21.cloned.1.call-done = bf16[1152,6144]{1,0:T(8,128)(2,1)} async-done(((bf16[72,6144]{1,0:T(8,128)(2,1)}), bf16[1152,6144]{1,0:T(8,128)(2,1)}) %all-gather.21.cloned.1.call-update) | async-done | bytes 14155792 | tf_op jit(solution)/shard_map/all_gather | solution.py:93
  553.0 91.8 %all-gather.23.cloned.1.call-done = bf16[3072,1152]{1,0:T(8,128)(2,1)} async-done(((bf16[192,1152]{1,0:T(8,128)(2,1)}), bf16[3072,1152]{1,0:T(8,128)(2,1)}) %all-gather.23.cloned.1.call-update) | async-done | bytes 7077904 | tf_op jit(solution)/shard_map/all_gather | solution.py:94
  653.9 175.4 %all-gather.25.cloned.1.call-done = bf16[1152,6912]{1,0:T(8,128)(2,1)} async-done(((bf16[72,6912]{1,0:T(8,128)(2,1)}), bf16[1152,6912]{1,0:T(8,128)(2,1)}) %all-gather.25.cloned.1.call-update) | async-done | bytes 15925264 | tf_op jit(solution)/shard_map/all_gather | solution.py:90
  839.6 99.6 %all-gather.27.cloned.1.call-done = bf16[1152,3456]{1,0:T(8,128)(2,1)} async-done(((bf16[72,3456]{1,0:T(8,128)(2,1)}), bf16[1152,3456]{1,0:T(8,128)(2,1)}) %all-gather.27.cloned.1.call-update) | async-done | bytes 7962640 | tf_op jit(solution)/shard_map/all_gather | solution.py:91
  972.8 10.2 convolution_convert_fusion.4
  983.0 21.4 all-gather.29.cloned.1.call-done
  1009.8 163.2 %all-gather.31.cloned.1.call-done = bf16[1152,6144]{1,0:T(8,128)(2,1)} async-done(((bf16[72,6144]{1,0:T(8,128)(2,1)}), bf16[1152,6144]{1,0:T(8,128)(2,1)}) %all-gather.31.cloned.1.call-update) | async-done | bytes 14155792 | tf_op jit(solution)/shard_map/all_gather | solution.py:93
  1182.1 93.2 %all-gather.33.cloned.1.call-done = bf16[3072,1152]{1,0:T(8,128)(2,1)} async-done(((bf16[192,1152]{1,0:T(8,128)(2,1)}), bf16[3072,1152]{1,0:T(8,128)(2,1)}) %all-gather.33.cloned.1.call-update) | async-done | bytes 7077904 | tf_op jit(solution)/shard_map/all_gather | solution.py:94
  1283.3 10.3 multiply_reduce_fusion.7
  1380.4 12.4 multiply_convert_fusion.10
  1400.4 10.4 multiply_reduce_fusion.6
  1507.3 11.4 fusion.22
  1520.2 11.5 fusion.20
  1532.6 13.4 fusion.144
  1556.4 13.0 fusion.119
  1569.5 23.3 reduce-scatter.55.cloned.1.call-done
  1594.5 143.5 %reduce-scatter.51.cloned.1.call-done = f32[72,1152]{1,0:T(8,128)} async-done(((f32[1152,1152]{1,0:T(8,128)}), f32[72,1152]{1,0:T(8,128)}) %reduce-scatter.51.cloned.1.call-update) | async-done | bytes 331792
  1739.6 224.1 %reduce-scatter.43.cloned.1.call-done = f32[192,1152]{1,0:T(8,128)} async-done(((f32[3072,1152]{1,0:T(8,128)}), f32[192,1152]{1,0:T(8,128)}) %reduce-scatter.43.cloned.1.call-update) | async-done | bytes 884752 | tf_op jit(solution)/shard_map/reduce_scatter | solution.py:164
  1965.7 225.5 %reduce-scatter.37.cloned.1.call-done = f32[192,1152]{1,0:T(8,128)} async-done(((f32[3072,1152]{1,0:T(8,128)}), f32[192,1152]{1,0:T(8,128)}) %reduce-scatter.37.cloned.1.call-update) | async-done | bytes 884752 | tf_op jit(solution)/shard_map/reduce_scatter | solution.py:164
  2193.2 255.6 %reduce-scatter.53.cloned.1.call-done = f32[72,3456]{1,0:T(8,128)} async-done(((f32[1152,3456]{1,0:T(8,128)}), f32[72,3456]{1,0:T(8,128)}) %reduce-scatter.53.cloned.1.call-update) | async-done | bytes 995344
  2450.8 255.5 %reduce-scatter.49.cloned.1.call-done = f32[72,3456]{1,0:T(8,128)} async-done(((f32[1152,3456]{1,0:T(8,128)}), f32[72,3456]{1,0:T(8,128)}) %reduce-scatter.49.cloned.1.call-update) | async-done | bytes 995344
  2708.4 401.8 %reduce-scatter.41.cloned.1.call-done = f32[72,6144]{1,0:T(8,128)} async-done(((f32[1152,6144]{1,0:T(8,128)}), f32[72,6144]{1,0:T(8,128)}) %reduce-scatter.41.cloned.1.call-update) | async-done | bytes 1769488 | tf_op jit(solution)/shard_map/reduce_scatter | solution.py:163
  3112.6 400.9 %reduce-scatter.35.cloned.1.call-done = f32[72,6144]{1,0:T(8,128)} async-done(((f32[1152,6144]{1,0:T(8,128)}), f32[72,6144]{1,0:T(8,128)}) %reduce-scatter.35.cloned.1.call-update) | async-done | bytes 1769488 | tf_op jit(solution)/shard_map/reduce_scatter | solution.py:163
  3516.0 482.0 %reduce-scatter.39.cloned.1.call-done = f32[72,6912]{1,0:T(8,128)} async-done(((f32[1152,6912]{1,0:T(8,128)}), f32[72,6912]{1,0:T(8,128)}) %reduce-scatter.39.cloned.1.call-update) | async-done | bytes 1990672 | tf_op jit(solution)/shard_map/reduce_scatter | solution.py:158
  4000.6 482.4 %reduce-scatter.33.cloned.1.call-done = f32[72,6912]{1,0:T(8,128)} async-done(((f32[1152,6912]{1,0:T(8,128)}), f32[72,6912]{1,0:T(8,128)}) %reduce-scatter.33.cloned.1.call-update) | async-done | bytes 1990672 | tf_op jit(solution)/shard_map/reduce_scatter | solution.py:158
  4491.3 76.6 %all-reduce.22 = (bf16[6912]{0:T(1024)(128)(2,1)S(1)}, bf16[2,1152]{1,0:T(2,128)(2,1)S(1)}, bf16[6912]{0:T(1024)(128)(2,1)S(1)}, bf16[2,1152]{1,0:T(2,128)(2,1)S(1)}) all-reduce(f32[6912]{0:T(1024)S(1)} %convert_reduce_fusion.1, f32[2,1152]{1,0:T(2,128)S(1)} %pad_add_fusion.5, ...), channel_id=9, replica_groups=mesh['dp'=16,'ctx'=2] {'dp'}, use_global_device_ids=true, to_apply=%region_36.37.clone | all-reduce | flops 18432 | bytes 110592
  (632 shorter events, 384.0 us)
Async XLA Ops:
  7.2 191.9 %all-gather.15.cloned.1.call-start = ((), (), s32[]{:S(2)}) async-start(), calls=%async_computation.14 | async-start | bytes 16920576 | tf_op jit(solution)/shard_map/all_gather | solution.py:90
  7.9 301.1 %all-gather.17.cloned.1.call-start = ((), (), s32[]{:S(2)}) async-start(), calls=%async_computation.15 | async-start | bytes 8460288 | tf_op jit(solution)/shard_map/all_gather | solution.py:91
  8.7 365.5 %all-gather.19.cloned.1.call-start = ((), (), s32[]{:S(2)}) async-start(), calls=%async_computation.16 | async-start | bytes 2820096 | tf_op jit(solution)/shard_map/all_gather | solution.py:92
  9.5 533.2 %all-gather.21.cloned.1.call-start = ((), (), s32[]{:S(2)}) async-start(), calls=%async_computation.17 | async-start | bytes 15040512 | tf_op jit(solution)/shard_map/all_gather | solution.py:93
  10.1 634.8 %all-gather.23.cloned.1.call-start = ((), (), s32[]{:S(2)}) async-start(), calls=%async_computation.18 | async-start | bytes 7520256 | tf_op jit(solution)/shard_map/all_gather | solution.py:94
  10.7 818.7 %all-gather.25.cloned.1.call-start = ((), (), s32[]{:S(2)}) async-start(), calls=%async_computation.19 | async-start | bytes 16920576 | tf_op jit(solution)/shard_map/all_gather | solution.py:90
  11.3 928.0 %all-gather.27.cloned.1.call-start = ((), (), s32[]{:S(2)}) async-start(), calls=%async_computation.20 | async-start | bytes 8460288 | tf_op jit(solution)/shard_map/all_gather | solution.py:91
  12.0 992.4 %all-gather.29.cloned.1.call-start = ((), (), s32[]{:S(2)}) async-start(), calls=%async_computation.21 | async-start | bytes 2820096 | tf_op jit(solution)/shard_map/all_gather | solution.py:92
  12.8 1160.3 %all-gather.31.cloned.1.call-start = ((), (), s32[]{:S(2)}) async-start(), calls=%async_computation.22 | async-start | bytes 15040512 | tf_op jit(solution)/shard_map/all_gather | solution.py:93
  13.5 1261.7 %all-gather.33.cloned.1.call-start = ((), (), s32[]{:S(2)}) async-start(), calls=%async_computation.23 | async-start | bytes 7520256 | tf_op jit(solution)/shard_map/all_gather | solution.py:94
  14.1 1318.7 %reduce-scatter.45.cloned.1.call-start = ((), (), s32[]{:S(2)}) async-start(), calls=%async_computation.32 | async-start | bytes 884736
  175.7 476.5 %copy-start.57 = (f32[1,128,576]{2,1,0:T(8,128)}, f32[1,128,576]{2,1,0:T(8,128)S(1)}, u32[]{:S(2)}) copy-start(f32[1,128,576]{2,1,0:T(8,128)S(1)} %get-tuple-element.117) | copy-start | bytes 884740
  377.6 172.4 %copy-start.140 = (f32[128]{0:T(128)}, f32[128]{0:T(128)S(1)}, u32[]{:S(2)}) copy-start(f32[128]{0:T(128)S(1)} %broadcast_multiply_fusion.1) | copy-start | bytes 1540
  377.8 172.2 %copy-start.154 = (f32[128]{0:T(128)}, f32[128]{0:T(128)S(1)}, u32[]{:S(2)}) copy-start(f32[128]{0:T(128)S(1)} %multiply_reduce_fusion.11) | copy-start | bytes 1540
  377.8 172.2 %copy-start.144 = (f32[128]{0:T(128)}, f32[128]{0:T(128)S(1)}, u32[]{:S(2)}) copy-start(f32[128]{0:T(128)S(1)} %fusion.109) | copy-start | bytes 1540
  650.2 179.2 %copy-start.126 = (f32[6912]{0:T(1024)S(1)}, f32[6912]{0:T(1024)}, u32[]{:S(2)}) copy-start(f32[6912]{0:T(1024)} %convert_element_type.390) | copy-start | bytes 82948
  653.9 185.4 %copy-start.139 = (f32[128]{0:T(128)S(1)}, f32[128]{0:T(128)}, u32[]{:S(2)}) copy-start(f32[128]{0:T(128)} %copy-done.138) | copy-start | bytes 1540
  653.9 185.4 %copy-start.143 = (f32[128]{0:T(128)S(1)}, f32[128]{0:T(128)}, u32[]{:S(2)}) copy-start(f32[128]{0:T(128)} %copy-done.142) | copy-start | bytes 1540
  1316.4 52.8 %reduce-scatter.29.cloned.1.call-start = ((), (), s32[]{:S(2)}) async-start(), calls=%async_computation.24 | async-start | bytes 884736 | tf_op jit(solution)/shard_map/reduce_scatter | solution.py:245
  1332.7 139.7 %reduce-scatter.47.cloned.1.call-start = ((), (), s32[]{:S(2)}) async-start(), calls=%async_computation.33 | async-start | bytes 884736
  1427.4 69.5 %reduce-scatter.31.cloned.1.call-start = ((), (), s32[]{:S(2)}) async-start(), calls=%async_computation.25 | async-start | bytes 884736 | tf_op jit(solution)/shard_map/reduce_scatter | solution.py:245
  1431.0 161.8 %reduce-scatter.55.cloned.1.call-start = ((), (), s32[]{:S(2)}) async-start(), calls=%async_computation.37 | async-start | bytes 5640192
  1435.2 302.8 %reduce-scatter.51.cloned.1.call-start = ((), (), s32[]{:S(2)}) async-start(), calls=%async_computation.35 | async-start | bytes 5640192
  1439.4 524.3 %reduce-scatter.43.cloned.1.call-start = ((), (), s32[]{:S(2)}) async-start(), calls=%async_computation.31 | async-start | bytes 15040512 | tf_op jit(solution)/shard_map/reduce_scatter | solution.py:164
  1447.7 743.4 %reduce-scatter.37.cloned.1.call-start = ((), (), s32[]{:S(2)}) async-start(), calls=%async_computation.28 | async-start | bytes 15040512 | tf_op jit(solution)/shard_map/reduce_scatter | solution.py:164
  1455.9 992.9 %reduce-scatter.53.cloned.1.call-start = ((), (), s32[]{:S(2)}) async-start(), calls=%async_computation.36 | async-start | bytes 16920576
  1464.9 1241.5 %reduce-scatter.49.cloned.1.call-start = ((), (), s32[]{:S(2)}) async-start(), calls=%async_computation.34 | async-start | bytes 16920576
  1505.9 1604.3 %reduce-scatter.41.cloned.1.call-start = ((), (), s32[]{:S(2)}) async-start(), calls=%async_computation.30 | async-start | bytes 30081024 | tf_op jit(solution)/shard_map/reduce_scatter | solution.py:163
  1518.7 1994.8 %reduce-scatter.35.cloned.1.call-start = ((), (), s32[]{:S(2)}) async-start(), calls=%async_computation.27 | async-start | bytes 30081024 | tf_op jit(solution)/shard_map/reduce_scatter | solution.py:163
  1531.7 2466.3 %reduce-scatter.39.cloned.1.call-start = ((), (), s32[]{:S(2)}) async-start(), calls=%async_computation.29 | async-start | bytes 33841152 | tf_op jit(solution)/shard_map/reduce_scatter | solution.py:158
  1546.0 2937.0 %reduce-scatter.33.cloned.1.call-start = ((), (), s32[]{:S(2)}) async-start(), calls=%async_computation.26 | async-start | bytes 33841152 | tf_op jit(solution)/shard_map/reduce_scatter | solution.py:158
  1569.5 3006.4 %all-reduce.28.cloned.1.call-start = ((), (), s32[]{:S(2)}) async-start(), calls=%async_computation.38 | async-start | bytes 11943936 | tf_op jit(solution)/shard_map/psum | solution.py:289
  (155 other events, 2424.8 us)
Sparse Core Ops, SparseCore 0:
  10.8 188.1 all-gather.14
  201.8 107.1 all-gather.16
  311.7 62.4 all-gather.18
  376.8 165.8 all-gather.20
  545.3 99.5 all-gather.22
  647.5 181.7 all-gather.24
  832.0 107.1 all-gather.26
  941.9 62.4 all-gather.28
  1007.2 165.8 all-gather.30
  1175.7 99.5 all-gather.32
  1316.5 6.1 reduce-scatter.44
  1332.8 6.1 reduce-scatter.28
  1427.5 6.1 reduce-scatter.46
  1436.5 9.1 reduce-scatter.30
  1450.8 141.9 reduce-scatter.54
  1597.9 140.0 reduce-scatter.50
  1743.6 220.0 reduce-scatter.42
  1970.3 220.7 reduce-scatter.36
  2197.0 251.7 reduce-scatter.52
  2454.4 251.8 reduce-scatter.48
  2712.1 397.9 reduce-scatter.40
  3115.9 397.5 reduce-scatter.34
  3519.6 478.3 reduce-scatter.38
  4003.9 479.0 reduce-scatter.32
  4488.6 32.8 all-reduce.27
where the time goes:
time: 4610 us; the launch traced here: 4600 us
  waiting for transfers between devices  3880 us (84%)
  blocking collectives  244 us (5%)
  matrix products  238 us (5%)
  local copies, waits for them, and re-layouts  126 us (3%)
  other arithmetic  91.1 us (2%)
    reduce_scatter x2, waiting for transfers between devices, reduce_grads(): lax.psum_scatter(grads[0], 'dp', scatter_dimension=0, tiled=True)  964 us
    reduce_scatter x2, waiting for transfers between devices, reduce_grads(): lax.psum_scatter(grads[5], 'dp', scatter_dimension=0, tiled=True)  803 us
    unnamed x31, waiting for transfers between devices  684 us
    reduce_scatter x2, waiting for transfers between devices, reduce_grads(): lax.psum_scatter(grads[6], 'dp', scatter_dimension=0, tiled=True)  450 us
    all_gather x2, waiting for transfers between devices, block_forward(): lax.all_gather(weights[3], 'dp', axis=0, tiled=True)  326 us
    all_gather x2, waiting for transfers between devices, block_forward(): lax.all_gather(weights[1], 'dp', axis=0, tiled=True)  199 us
    all_gather x2, waiting for transfers between devices, block_forward(): lax.all_gather(weights[0], 'dp', axis=0, tiled=True)  198 us
    all_gather x2, waiting for transfers between devices, block_forward(): lax.all_gather(weights[4], 'dp', axis=0, tiled=True)  185 us
  transfers between devices with their start and end apart: 25, of which 20 were waited for; matrix products, arithmetic and copies ran while one was open for 7% of the time, Pallas kernels for 0%

commit v1 on v0

v1 whole, which is shorter than its diff:
```python
import functools
import math

import jax
import jax.numpy as jnp
from jax import lax
from jax.experimental import pallas as pl
from jax.experimental.pallas import tpu as pltpu
from jax.sharding import PartitionSpec as P

HEADS = 16
HD = 72
MESH = pl.DeviceIdType.MESH
GRID = (4, 2, 2)
BF16 = jnp.bfloat16
F32 = jnp.float32


def coords():
    dp = lax.axis_index("dp")
    return (lax.div(dp, 4), lax.rem(lax.div(dp, 2), 2), lax.rem(dp, 2), lax.axis_index("ctx"))


def device(z, y, x, c):
    return (z * 4 + y * 2 + x, c)


def when(cond, body):
    if cond is True:
        body()
    else:
        pl.when(cond)(body)


def greet(z, y, x, c):
    barrier = pltpu.get_barrier_semaphore()

    def signal(target):
        pl.semaphore_signal(barrier, inc=1, device_id=target, device_id_type=MESH)

    signal(device(z, 1 - y, x, c))
    signal(device(z, y, 1 - x, c))
    signal(device(z, y, x, 1 - c))
    pl.when(z < 3)(lambda: signal(device(z + 1, y, x, c)))
    pl.when(z > 0)(lambda: signal(device(z - 1, y, x, c)))
    pl.semaphore_wait(barrier, 3 + lax.div(z + 3, 4) + lax.div(6 - z, 4))


def gather_kernel(units, count, stride, group, lag, *refs):
    w = refs[:count]
    o = refs[count : 2 * count]
    ssem, rsem, lsem, csem, crsem = refs[2 * count :]
    z, y, x, c = coords()
    greet(z, y, x, c)
    up = device(z + 1, y, x, c)
    down = device(z - 1, y, x, c)
    partner = {"y": device(z, 1 - y, x, c), "x": device(z, y, 1 - x, c)}
    every = slice(None)

    def run(mine, other):
        def view(u, index):
            m, first, cols, _ = mine[u]
            return o[m].at[index[0], index[1], index[2], :, pl.ds(first, cols)]

        def copy(u, index, k, target, own=False):
            m, first, cols, _ = mine[u]
            dst = view(u, index)
            src = w[m].at[:, pl.ds(first, cols)] if own else dst
            return pltpu.make_async_remote_copy(
                src, dst, ssem.at[u, k], rsem.at[u, k], device_id=target, device_id_type=MESH
            )

        def local_copy(u):
            m, first, cols, _ = mine[u]
            return pltpu.make_async_copy(
                w[m].at[:, pl.ds(first, cols)], view(u, (z, y, x)), lsem.at[u]
            )

        def plan(u):
            held = {"z": False, "y": False, "x": False}

            def index(zz=z, flip=None):
                return (
                    every if held["z"] else zz,
                    every if held["y"] else (1 - y if flip == "y" else y),
                    every if held["x"] else (1 - x if flip == "x" else x),
                )

            steps = []
            pending = []
            sends = []
            own = True
            pair = 0
            for axis in mine[u][3]:
                if axis != "z":
                    send = [(True, functools.partial(copy, u, index(), pair, partner[axis], own))]
                    steps.append((pending, send))
                    sends += send
                    pending = [
                        (True, functools.partial(copy, u, index(flip=axis), pair, partner[axis]))
                    ]
                    pair += 1
                else:

                    def chain(shift, k, target, first=False):
                        return functools.partial(copy, u, index(zz=z + shift), k, target, first)

                    one = [(z < 3, chain(0, 2, up, own)), (z > 0, chain(0, 5, down, own))]
                    steps.append((pending, one))
                    middle = (z > 0) & (z < 3)
                    two = [(middle, chain(-1, 3, up)), (middle, chain(1, 6, down))]
                    steps.append(([(z > 0, chain(-1, 2, down)), (z < 3, chain(1, 5, up))], two))
                    three = [(z == 2, chain(-2, 4, up)), (z == 1, chain(2, 7, down))]
                    steps.append(([(z > 1, chain(-2, 3, down)), (z < 2, chain(2, 6, up))], three))
                    pending = [(z == 3, chain(-3, 4, down)), (z == 0, chain(3, 7, up))]
                    sends += one + two + three
                held[axis] = True
                own = False
            return steps, pending, sends

        plans = [plan(u) for u in range(len(mine))]

        def to_core(u, which):
            m, first, cols, _ = which[u]
            block = o[m].at[:, :, :, :, pl.ds(first, cols)]
            return pltpu.make_async_remote_copy(
                block,
                block,
                csem.at[u],
                crsem.at[u],
                device_id=device(z, y, x, 1 - c),
                device_id_type=MESH,
            )

        for u in range(len(mine)):
            local_copy(u).start()
        starts = [(u // group) * stride for u in range(len(mine))]
        for turn in range(max(starts) + 6 + lag):
            for u in range(len(mine)):
                steps, pending, _ = plans[u]
                s = turn - starts[u]
                if 0 <= s < 5:
                    if s == 1:
                        local_copy(u).wait()
                    for cond, make in steps[s][0]:
                        when(cond, lambda make=make: make().wait_recv())
                    for cond, make in steps[s][1]:
                        when(cond, lambda make=make: make().start())
                elif s == 5 + lag:
                    for cond, make in pending:
                        when(cond, lambda make=make: make().wait_recv())
                    to_core(u, mine).start()
        for u in range(len(mine)):
            for cond, make in plans[u][2]:
                when(cond, lambda make=make: make().wait_send())
            to_core(u, mine).wait_send()
        for u in range(len(other)):
            to_core(u, other).wait_recv()

    pl.when(c == 0)(lambda: run(units[0], units[1]))
    pl.when(c == 1)(lambda: run(units[1], units[0]))


ANY = pl.BlockSpec(memory_space=pl.ANY)
DMA = pltpu.SemaphoreType.DMA


def gather(shards, units, collective_id, stride, group, lag, name):
    count = len(shards)
    most = max(len(units[0]), len(units[1]))
    return pl.pallas_call(
        functools.partial(gather_kernel, units, count, stride, group, lag),
        name=name,
        out_shape=[jax.ShapeDtypeStruct(GRID + s.shape, s.dtype) for s in shards],
        in_specs=[ANY] * count,
        out_specs=[ANY] * count,
        scratch_shapes=[DMA((most, 8)), DMA((most, 8)), DMA((most,)), DMA((most,)), DMA((most,))],
        compiler_params=pltpu.CompilerParams(collective_id=collective_id, has_side_effects=True),
    )(*shards)


def spans(matrix, tiles, shifts=0):
    orders = ("zyx", "zxy", "yzx", "xzy")
    out = []
    at = 0
    for k, t in enumerate(tiles):
        out.append((matrix, at * 128, t * 128, orders[(k + shifts) % 4]))
        at += t
    return out


def exchange_kernel(broadcast, in_ref, out_ref, ssem, rsem, lsem):
    me = lax.axis_index("dp")
    c = lax.axis_index("ctx")
    barrier = pltpu.get_barrier_semaphore()
    for k in range(1, 16):
        pl.semaphore_signal(
            barrier, inc=1, device_id=(lax.rem(me + k, 16), c), device_id_type=MESH
        )
    pl.semaphore_wait(barrier, 15)

    def source(target):
        return in_ref if broadcast else in_ref.at[target]

    def copy(k):
        target = lax.rem(me + k, 16)
        return pltpu.make_async_remote_copy(
            source(target),
            out_ref.at[me],
            ssem.at[k],
            rsem.at[k],
            device_id=(target, c),
            device_id_type=MESH,
        )

    def arrival(k):
        origin = lax.rem(me + 16 - k, 16)
        return pltpu.make_async_remote_copy(
            source(origin),
            out_ref.at[origin],
            ssem.at[k],
            rsem.at[k],
            device_id=(origin, c),
            device_id_type=MESH,
        )

    for k in range(1, 16):
        copy(k).start()
    own = pltpu.make_async_copy(source(me), out_ref.at[me], lsem.at[0])
    own.start()
    own.wait()
    for k in range(1, 16):
        copy(k).wait_send()
        arrival(k).wait_recv()


def exchange(values, broadcast, collective_id, name):
    shape = values.shape if broadcast else values.shape[1:]
    return pl.pallas_call(
        functools.partial(exchange_kernel, broadcast),
        name=name,
        out_shape=jax.ShapeDtypeStruct((16,) + shape, values.dtype),
        in_specs=[ANY],
        out_specs=ANY,
        scratch_shapes=[DMA((16,)), DMA((16,)), DMA((1,))],
        compiler_params=pltpu.CompilerParams(collective_id=collective_id, has_side_effects=True),
    )(values)


LAG = (0, 3, 5, 7, 9, 11)
RECV_SLOTS = 14
SEND_SLOTS = 13
FIRST_SLOTS = 6
UNIT = 384
ROWS = 72
PADDED = 80


def scatter_kernel(first, cols, source, dy_count, *refs):
    nv = len(first) - 1
    xt = refs[:nv]
    dy = refs[nv : nv + dy_count]
    out = refs[nv + dy_count]
    (
        xts, dys, a_s1, a_s2, a_t, a_su, a_sd, e_s1, e_t, e_su, e_sd, e_sq,
        a_b1, a_b2, a_bu, a_bd, e_b1, e_bu, e_bd, e_bq, outs,
        ssem, rsem, xl, xs, xr, yl, ys, yr, ol, os, orr,
    ) = refs[nv + dy_count + 1 :]
    z, y, x, c = coords()
    total = first[-1] // 2
    sibling = device(z, y, x, 1 - c)
    up = device(z + 1, y, x, c)
    down = device(z - 1, y, x, c)
    greet(z, y, x, c)
    lanes = pl.ds(pl.multiple_of(c * 128, 128), 128)
    offsets = []
    at = 0
    for k in range(dy_count):
        offsets.append(at)
        at += dy[k].shape[1]

    def remote(src, dst, send, recv, target):
        return pltpu.make_async_remote_copy(
            src, dst, send, recv, device_id=target, device_id_type=MESH
        )

    def x_views(v, k):
        o, b = k // 2, k % 2
        src = xt[v].at[:, :, b] if o == 0 else xt[v].at[:, b]
        return src, xts.at[v, o, b, :, :, :, lanes]

    def x_local(v, k):
        return pltpu.make_async_copy(*x_views(v, k), xl.at[v, k])

    def x_remote(v, k):
        return remote(*x_views(v, k), xs.at[v, k], xr.at[v, k], sibling)

    def y_views(k):
        return dy[k], dys.at[lanes, pl.ds(offsets[k], dy[k].shape[1])]

    def y_local(k):
        return pltpu.make_async_copy(*y_views(k), yl.at[k])

    def y_remote(k):
        return remote(*y_views(k), ys.at[k], yr.at[k], sibling)

    fresh = [source[v] not in source[:v] for v in range(nv)]
    for v in range(nv):
        for k in range(4):
            x_local(v, k).start()
            x_remote(v, k).start()
        if fresh[v]:
            y_local(source[v]).start()
            y_remote(source[v]).start()

    def arrive(tick):
        for v in range(nv):

            def wait(v=v):
                for k in range(4):
                    x_local(v, k).wait()
                    x_remote(v, k).wait_recv()
                if fresh[v]:
                    y_local(source[v]).wait()
                    y_remote(source[v]).wait_recv()

            pl.when(tick == (first[v] - c + 1) // 2)(wait)

    def unit(i):
        j = 2 * i + c
        v = jnp.int32(0)
        col = j * UNIT
        for k in range(1, nv):
            past = (j >= first[k]).astype(jnp.int32)
            v = v + past
            col = col + past * ((cols[k] - first[k] * UNIT) - (cols[k - 1] - first[k - 1] * UNIT))
        return v, pl.multiple_of(col, 128)

    def axes(i):
        o = lax.rem(i, 2)
        pb = x * (1 - o) + y * o
        qb = y * (1 - o) + x * o
        dp = z * 4 + y * 2 + x
        return o, pb, qb, (dp + (1 - 2 * pb) * (1 + o), c), (dp + (1 - 2 * qb) * (2 - o), c)

    def slots(i):
        return lax.rem(i, FIRST_SLOTS), lax.rem(i, SEND_SLOTS), lax.rem(i, RECV_SLOTS)

    def send(src, dst, i, k, target):
        return remote(
            src, dst, ssem.at[lax.rem(i, SEND_SLOTS), k], rsem.at[lax.rem(i, RECV_SLOTS), k], target
        )

    def first_copies(i):
        o, pb, qb, pn, qn = axes(i)
        f, s, w = slots(i)
        return [send(a_s1.at[f], a_b1.at[w], i, 0, pn), send(e_s1.at[f], e_b1.at[w], i, 8, pn)]

    def second_copy(i):
        o, pb, qb, pn, qn = axes(i)
        f, s, w = slots(i)
        return send(a_s2.at[s], a_b2.at[w], i, 1, qn)

    def last_copy(i):
        o, pb, qb, pn, qn = axes(i)
        f, s, w = slots(i)
        return send(e_sq.at[s], e_bq.at[w], i, 9, qn)

    def up_copy(i, k, e):
        f, s, w = slots(i)
        src, dst, n = (e_su, e_bu, 10) if e else (a_su, a_bu, 2)
        return send(src.at[s, k], dst.at[w, k], i, n + k, up)

    def down_copy(i, k, e):
        f, s, w = slots(i)
        src, dst, n = (e_sd, e_bd, 13) if e else (a_sd, a_bd, 5)
        return send(src.at[s, k], dst.at[w, k], i, n + k, down)

    def up_sends(k):
        return (z <= k) & (z < 3)

    def down_sends(k):
        return (3 - z <= k) & (z > 0)

    def up_comes(k):
        return (z >= 1) & (z <= k + 1)

    def down_comes(k):
        return (z <= 2) & (3 - z <= k + 1)

    def kept(i, e, d):
        f, s, w = slots(i)
        if e:
            return e_t.at[s, d]
        return a_t.at[s, d, axes(i)[2]]

    def z_send(i, k, e):
        f, s, w = slots(i)

        def pass_on(dest, stage, box, inner, copy):
            value = kept(i, e, dest)[...]
            if k == 0:
                stage[s, k] = value.astype(BF16)
            else:

                def add():
                    stage[s, k] = (value + box[w, k - 1].astype(F32)).astype(BF16)

                def begin():
                    stage[s, k] = value.astype(BF16)

                pl.when(inner)(add)
                pl.when(jnp.logical_not(inner))(begin)
            copy.start()

        pl.when(up_sends(k))(
            lambda: pass_on(
                z + 3 - k, e_su if e else a_su, e_bu if e else a_bu, z > 0, up_copy(i, k, e)
            )
        )
        pl.when(down_sends(k))(
            lambda: pass_on(
                z + k - 3, e_sd if e else a_sd, e_bd if e else a_bd, z < 3, down_copy(i, k, e)
            )
        )

    def z_wait(i, k, e):
        pl.when(up_comes(k))(lambda: up_copy(i, k, e).wait_recv())
        pl.when(down_comes(k))(lambda: down_copy(i, k, e).wait_recv())

    def z_close(i, e):
        f, s, w = slots(i)
        mine = kept(i, e, z)

        def below():
            mine[...] = mine[...] + (e_bu if e else a_bu)[w, 2].astype(F32)

        def above():
            mine[...] = mine[...] + (e_bd if e else a_bd)[w, 2].astype(F32)

        pl.when(z > 0)(below)
        pl.when(z < 3)(above)
        return mine

    def product(i, bit):
        v, col = unit(i)
        lhs = xts[v, axes(i)[0], bit].reshape(8 * PADDED, 256)
        whole = jnp.dot(lhs, dys[:, pl.ds(col, UNIT)], preferred_element_type=F32)
        return whole.reshape(8, PADDED, UNIT)[:, :ROWS]

    def stage0(i):
        f, s, w = slots(i)
        part = product(i, 1 - axes(i)[1])
        a_s1[f] = part[:, :, :128].astype(BF16).reshape(4, 2, ROWS, 128)
        e_s1[f] = part[:, :, 128:].astype(BF16).reshape(4, 2, ROWS, 256)
        for copy in first_copies(i):
            copy.start()

    def stage1(i):
        f, s, w = slots(i)
        o, pb, qb, pn, qn = axes(i)
        part = product(i, pb)
        for copy in first_copies(i):
            copy.wait_recv()
        a_t[s] = part[:, :, :128].reshape(4, 2, ROWS, 128) + a_b1[w].astype(F32)
        a_s2[s] = a_t[s, :, 1 - qb].astype(BF16)
        second_copy(i).start()
        e_t[s] = part[:, :, 128:].reshape(4, 2, ROWS, 256) + e_b1[w].astype(F32)
        z_send(i, 0, True)

    def stage2(i):
        f, s, w = slots(i)
        qb = axes(i)[2]
        second_copy(i).wait_recv()
        a_t[s, :, qb] = a_t[s, :, qb] + a_b2[w].astype(F32)
        z_send(i, 0, False)
        z_wait(i, 0, True)
        z_send(i, 1, True)

    def stage3(i):
        z_wait(i, 0, False)
        z_send(i, 1, False)
        z_wait(i, 1, True)
        z_send(i, 2, True)

    def stage4(i):
        f, s, w = slots(i)
        z_wait(i, 1, False)
        z_send(i, 2, False)
        z_wait(i, 2, True)
        z_close(i, True)
        e_sq[s] = e_t[s, z, 1 - axes(i)[2]].astype(BF16)
        last_copy(i).start()

    def out_view(i):
        return out.at[:, pl.ds(pl.multiple_of((2 * i + c) * UNIT, 128), UNIT)]

    def stage5(i):
        f, s, w = slots(i)
        z_wait(i, 2, False)
        outs[i, :, :128] = z_close(i, False)[...]
        last_copy(i).wait_recv()
        outs[i, :, 128:] = e_t[s, z, axes(i)[2]] + e_bq[w].astype(F32)
        pltpu.make_async_copy(outs.at[i], out_view(i), ol.at[0]).start()
        remote(outs.at[i], out_view(i), os.at[0], orr.at[0], sibling).start()

    def first_sent(i):
        for copy in first_copies(i):
            copy.wait_send()

    def sent(i):
        second_copy(i).wait_send()
        last_copy(i).wait_send()
        for e in (False, True):
            for k in range(3):
                pl.when(up_sends(k))(lambda k=k, e=e: up_copy(i, k, e).wait_send())
                pl.when(down_sends(k))(lambda k=k, e=e: down_copy(i, k, e).wait_send())

    stages = (stage0, stage1, stage2, stage3, stage4, stage5)

    def tick(t, carry):
        arrive(t)
        pl.when((t >= SEND_SLOTS) & (t - SEND_SLOTS < total))(lambda: sent(t - SEND_SLOTS))
        pl.when((t >= FIRST_SLOTS) & (t - FIRST_SLOTS < total))(lambda: first_sent(t - FIRST_SLOTS))
        for k in reversed(range(6)):
            i = t - LAG[k]
            pl.when((i >= 0) & (i < total))(functools.partial(stages[k], i))
        return carry

    lax.fori_loop(0, total + SEND_SLOTS, tick, 0)
    for v in range(nv):
        for k in range(4):
            x_remote(v, k).wait_send()
    for k in range(dy_count):
        y_remote(k).wait_send()
    half = out.at[:, pl.ds(0, total * UNIT)]
    pltpu.make_async_copy(half, half, ol.at[0]).wait()
    everything = remote(half, half, os.at[0], orr.at[0], sibling)
    everything.wait_send()
    everything.wait_recv()


def scatter(xts, dys, source, collective_id, name):
    nv = len(xts)
    starts = []
    width = 0
    for d in dys:
        starts.append(width)
        width += d.shape[1]
    first = [0]
    cols = []
    for v in range(nv):
        cols.append(starts[source[v]])
        first.append(first[-1] + dys[source[v]].shape[1] // UNIT)
    total = first[-1] // 2
    s, f, r = SEND_SLOTS, FIRST_SLOTS, RECV_SLOTS
    vmem = pltpu.VMEM
    return pl.pallas_call(
        functools.partial(scatter_kernel, tuple(first), tuple(cols), tuple(source), len(dys)),
        name=name,
        out_shape=jax.ShapeDtypeStruct((ROWS, first[-1] * UNIT), F32),
        in_specs=[ANY] * (nv + len(dys)),
        out_specs=ANY,
        scratch_shapes=[
            vmem((nv, 2, 2, 4, 2, PADDED, 256), BF16),
            vmem((256, width), BF16),
            vmem((f, 4, 2, ROWS, 128), BF16),
            vmem((s, 4, ROWS, 128), BF16),
            vmem((s, 4, 2, ROWS, 128), F32),
            vmem((s, 3, ROWS, 128), BF16),
            vmem((s, 3, ROWS, 128), BF16),
            vmem((f, 4, 2, ROWS, 256), BF16),
            vmem((s, 4, 2, ROWS, 256), F32),
            vmem((s, 3, 2, ROWS, 256), BF16),
            vmem((s, 3, 2, ROWS, 256), BF16),
            vmem((s, ROWS, 256), BF16),
            vmem((r, 4, 2, ROWS, 128), BF16),
            vmem((r, 4, ROWS, 128), BF16),
            vmem((r, 3, ROWS, 128), BF16),
            vmem((r, 3, ROWS, 128), BF16),
            vmem((r, 4, 2, ROWS, 256), BF16),
            vmem((r, 3, 2, ROWS, 256), BF16),
            vmem((r, 3, 2, ROWS, 256), BF16),
            vmem((r, ROWS, 256), BF16),
            vmem((total, ROWS, UNIT), F32),
            DMA((s, 16)),
            DMA((r, 16)),
            DMA((nv, 4)),
            DMA((nv, 4)),
            DMA((nv, 4)),
            DMA((len(dys),)),
            DMA((len(dys),)),
            DMA((len(dys),)),
            DMA((1,)),
            DMA((1,)),
            DMA((1,)),
        ],
        compiler_params=pltpu.CompilerParams(
            collective_id=collective_id, has_side_effects=True, vmem_limit_bytes=60 * 1024 * 1024
        ),
    )(*xts, *dys)


def layer_norm(values):
    center = values - jnp.mean(values, axis=-1, keepdims=True)
    spread = jnp.mean(center * center, axis=-1, keepdims=True)
    return center * lax.rsqrt(spread + 1e-06)


def head_norm(values, gain):
    shaped = values.reshape(values.shape[:-1] + (HEADS, HD))
    scaled = shaped * lax.rsqrt(jnp.mean(shaped * shaped, axis=-1, keepdims=True) + 1e-06)
    return scaled * gain.reshape(HEADS, HD)


def rope_tables(rows, columns):
    quarter = HD // 4
    freqs = jnp.exp(jnp.arange(quarter, dtype=F32) * (-math.log(10000.0) / quarter))
    places = jnp.stack([rows, columns], axis=-1).astype(F32)
    angles = places[..., None] * freqs
    return (jnp.cos(angles), jnp.sin(angles))


def rotate(values, cosine, sine):
    shaped = values.reshape(values.shape[:-1] + (2, 2, HD // 4))
    first = shaped[..., 0, :]
    second = shaped[..., 1, :]
    cosine = cosine[..., None, :, :]
    sine = sine[..., None, :, :]
    turned = jnp.stack([first * cosine - second * sine, first * sine + second * cosine], axis=-2)
    return turned.reshape(values.shape)


def embed_times(times, width):
    half_width = width // 2
    freqs = jnp.exp(jnp.arange(half_width, dtype=F32) * (-math.log(10000.0) / half_width))
    angles = times[..., None] * freqs
    return jnp.concatenate([jnp.cos(angles), jnp.sin(angles)], axis=-1)


def qk_prepare(query_raw, key_raw, gains, cosine, sine):
    return (
        rotate(head_norm(query_raw, gains[0]), cosine, sine),
        rotate(head_norm(key_raw, gains[1]), cosine, sine),
    )


def swish_product(gate, up):
    return jax.nn.silu(gate) * up


def attention_scores(queries, keys, allowed):
    scores = jnp.einsum("sqhd,skhd->shqk", queries, keys, preferred_element_type=F32) * (
        1.0 / math.sqrt(HD)
    )
    return jnp.where(allowed[:, None], scores, -1e30)


def dense(values, weight):
    return jnp.dot(values, weight, preferred_element_type=F32)


def dense_back(grads, weight):
    return lax.dot_general(grads, weight, (((1,), (1,)), ((), ())), preferred_element_type=F32)


def outer_sum(values, grads):
    return lax.dot_general(values, grads, (((0,), (0,)), ((), ())), preferred_element_type=F32)


def block_forward(flat, modulation, weights, context):
    batch, half, allowed, cosine, sine = context
    triple, mixing, expand, reduce_w, gains = weights
    width = flat.shape[1]
    shift1, scale1, gate1, shift2, scale2, gate2 = jnp.split(modulation, 6, axis=1)
    lifted1 = (layer_norm(flat) * (1.0 + scale1) + shift1).astype(BF16)
    projected = dense(lifted1, triple)
    query_raw, key_raw, value_raw = jnp.split(projected, 3, axis=1)
    queries, keys = qk_prepare(query_raw, key_raw, gains, cosine, sine)
    queries = queries.astype(BF16).reshape(batch, half, HEADS, HD)
    keys_local = keys.astype(BF16).reshape(batch, half, width)
    values_local = value_raw.astype(BF16).reshape(batch, half, width)
    key_heads = lax.all_gather(keys_local, "ctx", axis=1, tiled=True).reshape(batch, -1, HEADS, HD)
    value_heads = lax.all_gather(values_local, "ctx", axis=1, tiled=True)
    value_heads = value_heads.reshape(batch, -1, HEADS, HD)
    scores = attention_scores(queries, key_heads, allowed)
    top = jnp.max(scores, axis=-1, keepdims=True)
    raised = jnp.exp(scores - top)
    total = jnp.sum(raised, axis=-1, keepdims=True)
    softmax_low = (raised / total).astype(BF16)
    logsum = top + jnp.log(total)
    mixed = jnp.einsum("shqk,skhd->sqhd", softmax_low, value_heads, preferred_element_type=F32)
    mixed_low = mixed.reshape(-1, width).astype(BF16)
    attended = dense(mixed_low, mixing)
    resid = flat + gate1 * attended
    lifted2 = (layer_norm(resid) * (1.0 + scale2) + shift2).astype(BF16)
    expanded = dense(lifted2, expand)
    gate, up = jnp.split(expanded, 2, axis=1)
    hidden = swish_product(gate, up).astype(BF16)
    feed = dense(hidden, reduce_w)
    output = resid + gate2 * feed
    kept = (
        modulation,
        flat,
        lifted1,
        query_raw,
        key_raw,
        queries,
        key_heads,
        value_heads,
        logsum,
        mixed_low,
        attended,
        resid,
        lifted2,
        expanded,
        hidden,
        feed,
    )
    return (output, kept)


def block_backward(grad_out, kept, weights, context):
    batch, half, allowed, cosine, sine = context
    triple, mixing, expand, reduce_w, gains = weights
    (
        modulation,
        flat,
        lifted1,
        query_raw,
        key_raw,
        queries,
        key_heads,
        value_heads,
        logsum,
        mixed_low,
        attended,
        resid,
        lifted2,
        expanded,
        hidden,
        feed,
    ) = kept
    width = flat.shape[1]
    shift1, scale1, gate1, shift2, scale2, gate2 = jnp.split(modulation, 6, axis=1)
    grad_feed = (grad_out * gate2).astype(BF16)
    grad_hidden = dense_back(grad_feed, reduce_w)
    gate, up = jnp.split(expanded, 2, axis=1)
    unused_out, swish_pull = jax.vjp(swish_product, gate, up)
    grad_gate, grad_up = swish_pull(grad_hidden)
    grad_expanded = jnp.concatenate([grad_gate, grad_up], axis=1).astype(BF16)
    grad_lifted2 = dense_back(grad_expanded, expand)
    normed_second, second_pull = jax.vjp(layer_norm, resid)
    grad_resid = grad_out + second_pull(grad_lifted2 * (1.0 + scale2))[0]
    grad_attended = (grad_resid * gate1).astype(BF16)
    grad_mixed = dense_back(grad_attended, mixing).astype(BF16).reshape(batch, half, HEADS, HD)
    scores = attention_scores(queries, key_heads, allowed)
    chances = jnp.exp(scores - logsum)
    grad_chances = jnp.einsum(
        "sqhd,skhd->shqk", grad_mixed, value_heads, preferred_element_type=F32
    )
    grad_values = jnp.einsum(
        "shqk,sqhd->skhd", chances.astype(BF16), grad_mixed, preferred_element_type=F32
    )
    grad_scores = (
        chances * (grad_chances - jnp.sum(chances * grad_chances, axis=-1, keepdims=True))
    ).astype(BF16)
    scale = 1.0 / math.sqrt(HD)
    grad_queries = (
        jnp.einsum("shqk,skhd->sqhd", grad_scores, key_heads, preferred_element_type=F32) * scale
    )
    grad_keys = (
        jnp.einsum("shqk,sqhd->skhd", grad_scores, queries, preferred_element_type=F32) * scale
    )
    pair = jnp.stack(
        [grad_keys.reshape(batch, -1, width), grad_values.reshape(batch, -1, width)]
    ).astype(BF16)
    place = lax.axis_index("ctx")
    theirs = lax.dynamic_slice_in_dim(pair, (1 - place) * half, half, 2)
    theirs = lax.ppermute(theirs, "ctx", [(0, 1), (1, 0)])
    mine = lax.dynamic_slice_in_dim(pair, place * half, half, 2)
    pair = mine.astype(F32) + theirs.astype(F32)
    grad_keys, grad_values = pair[0], pair[1]

    def prepare(query_in, key_in, gain_in):
        return qk_prepare(query_in, key_in, gain_in, cosine, sine)

    unused_pair, prepare_pull = jax.vjp(prepare, query_raw, key_raw, gains)
    grad_query_raw, grad_key_raw, gains_grad = prepare_pull(
        (grad_queries.reshape(-1, HEADS, HD), grad_keys.reshape(-1, HEADS, HD))
    )
    grad_projected = jnp.concatenate(
        [grad_query_raw, grad_key_raw, grad_values.reshape(-1, width)], axis=1
    ).astype(BF16)
    grad_lifted1 = dense_back(grad_projected, triple)
    normed_first, first_pull = jax.vjp(layer_norm, flat)
    grad_flat = grad_resid + first_pull(grad_lifted1 * (1.0 + scale1))[0]
    grad_modulation = jnp.concatenate(
        [
            grad_lifted1,
            grad_lifted1 * normed_first,
            grad_resid * attended,
            grad_lifted2,
            grad_lifted2 * normed_second,
            grad_out * feed,
        ],
        axis=1,
    ).astype(BF16)
    factors = (
        (lifted1, grad_projected),
        (mixed_low, grad_attended),
        (lifted2, grad_expanded),
        (hidden, grad_feed),
    )
    return (grad_flat, grad_modulation, factors, gains_grad)


def shard_rows(values, groups):
    turned = values.T.reshape(16, groups, -1, values.shape[0])
    rows = turned.shape[2]
    turned = jnp.pad(turned, ((0, 0), (0, 0), (0, PADDED - rows), (0, 0)))
    return [turned[:, g].reshape(GRID + turned.shape[2:]) for g in range(groups)]


def fast_reduce(factors, extra, collective_id, name):
    tokens = factors[0][0].shape[0]
    xts = []
    dys = []
    source = []
    for k, (left, right) in enumerate(factors):
        groups = 3 if k == len(factors) - 1 else 1
        xts += shard_rows(left, groups)
        dys.append(right)
        source += [k] * groups
    count = extra.shape[1]
    lines = -(-count // tokens)
    packed = jnp.pad(extra, ((0, 0), (0, lines * tokens - count))).reshape(16, lines, tokens)
    packed = jnp.pad(packed, ((0, 0), (0, PADDED - lines), (0, 0))).astype(BF16)
    xts.append(packed.reshape(GRID + packed.shape[1:]))
    dys.append(jnp.eye(tokens, UNIT, dtype=BF16))
    source.append(len(factors))
    out = scatter(xts, dys, source, collective_id, name)
    grads = []
    at = 0
    for left, right in factors[:-1]:
        grads.append(out[:, at : at + right.shape[1]])
        at += right.shape[1]
    width = factors[-1][1].shape[1]
    rows = factors[-1][0].shape[1] // 48
    parts = [out[:rows, at + g * width : at + (g + 1) * width] for g in range(3)]
    grads.append(jnp.concatenate(parts, axis=0))
    at += 3 * width
    small = out[:lines, at : at + tokens].reshape(-1)[:count]
    return grads, small


def whole_rows(gathered):
    return gathered.reshape((-1,) + gathered.shape[4:])


def fast_step(flat, cotangent, context, segment_local, valid, timesteps, encoder, decoder):
    width = flat.shape[1]
    offset_size = encoder[1].shape[0]
    gain_size = 2 * encoder[3].shape[1]
    small = jnp.concatenate(
        [
            encoder[1].astype(F32),
            decoder[1].astype(F32),
            encoder[3].astype(F32).reshape(-1),
            decoder[3].astype(F32).reshape(-1),
            timesteps.astype(F32).reshape(-1),
        ]
    )
    size = small.shape[0]
    small = jnp.pad(small, (0, 2048 - size)).reshape(16, 128)
    small = exchange(small, True, 0, "small").reshape(16, -1)
    encoder_offset = small[:, :offset_size].reshape(-1)
    decoder_offset = small[:, offset_size : 2 * offset_size].reshape(-1)
    at = 2 * offset_size
    encoder_gains = small[:, at : at + gain_size].reshape(16, 2, -1).swapaxes(0, 1).reshape(2, -1)
    at += gain_size
    decoder_gains = small[:, at : at + gain_size].reshape(16, 2, -1).swapaxes(0, 1).reshape(2, -1)
    at += gain_size
    all_times = small[:, at : at + timesteps.size]
    segments = timesteps.shape[1]
    picks = (segment_local[..., None] == jnp.arange(segments, dtype=jnp.int32)).astype(F32)
    picks = picks.reshape(-1, segments)

    all_cond = embed_times(all_times, width).reshape(-1, width)
    act_rows = jax.nn.silu(all_cond).astype(BF16)
    me = lax.axis_index("dp")
    rows = encoder[0].shape[0]
    act_mine = lax.dynamic_slice_in_dim(act_rows, me * rows, rows, 1)
    partial = dense(act_mine, encoder[0]).reshape(16, -1, 1152)
    partial = exchange(partial, False, 1, "partial")
    modulation_rows = jnp.sum(partial, axis=0).reshape(segments, -1) + encoder_offset
    exact = lax.Precision.HIGHEST
    encoder_modulation = jnp.dot(picks, modulation_rows, precision=exact)
    cond_rows = lax.dynamic_slice_in_dim(all_cond, me * segments, segments, 0)
    cond = jnp.dot(picks, cond_rows, precision=exact)

    encoder_units = (
        tuple(spans(2, (6,) * 8) + spans(0, (6,))),
        tuple(
            [(0, 768 + at, n, o) for _, at, n, o in spans(0, (7, 7, 7))]
            + spans(1, (4, 5), 3)
            + spans(3, (2, 2, 2, 3), 1)
        ),
    )
    triple, mixing, expand, reduce_w = gather(
        [encoder[2], encoder[4], encoder[5], encoder[6]], encoder_units, 2, 1, 2, 1, "gather_encoder"
    )
    encoder_weights = (
        whole_rows(triple),
        whole_rows(mixing),
        whole_rows(expand),
        whole_rows(reduce_w),
        encoder_gains,
    )
    encoder_out, encoder_kept = block_forward(flat, encoder_modulation, encoder_weights, context)
    latent_full = valid * encoder_out
    decoder_pre = latent_full + cond
    decoder_act = jax.nn.silu(decoder_pre).astype(BF16)

    decoder_units = (
        tuple(spans(0, (7, 7, 7, 7, 7, 7, 6, 6)) + spans(1, (7, 7, 7, 6))),
        tuple(spans(3, (6,) * 8) + spans(4, (2, 2, 2, 3)) + spans(2, (2, 2, 2, 3))),
    )
    shards = (decoder[0], decoder[2], decoder[4], decoder[5], decoder[6])
    shards, decoder_act = lax.optimization_barrier((shards, decoder_act))
    modulate, triple, mixing, expand, reduce_w = gather(
        shards, decoder_units, 3, 1, 2, 1, "gather_decoder"
    )
    modulate = whole_rows(modulate)
    decoder_weights = (
        whole_rows(triple),
        whole_rows(mixing),
        whole_rows(expand),
        whole_rows(reduce_w),
        decoder_gains,
    )
    decoder_modulation = dense(decoder_act, modulate) + decoder_offset
    decoder_out, decoder_kept = block_forward(flat, decoder_modulation, decoder_weights, context)
    velocity = valid * decoder_out

    grad_out = valid * cotangent
    decoder_flat, grad_modulation, factors, gains_grad = block_backward(
        grad_out, decoder_kept, decoder_weights, context
    )
    grad_act = dense_back(grad_modulation, modulate)
    unused_silu, silu_pull = jax.vjp(jax.nn.silu, decoder_pre)
    grad_latent = valid * silu_pull(grad_act)[0]
    offset_grad = jnp.sum(grad_modulation, axis=0, dtype=F32)
    extra = jnp.concatenate(
        [
            offset_grad.reshape(16, -1),
            gains_grad.reshape(2, 16, -1).swapaxes(0, 1).reshape(16, -1),
        ],
        axis=1,
    )
    grads, small = fast_reduce(
        ((decoder_act, grad_modulation),) + factors, extra, 4, "scatter_decoder"
    )
    decoder_grads = (
        grads[0],
        small[:offset_size],
        grads[1],
        small[offset_size:].reshape(2, -1),
        grads[2],
        grads[3],
        grads[4],
    )

    encoder_flat, grad_modulation, factors, gains_grad = block_backward(
        grad_latent, encoder_kept, encoder_weights, context
    )
    grad_rows = lax.dot_general(
        picks.astype(BF16), grad_modulation, (((0,), (0,)), ((), ())), preferred_element_type=F32
    )
    grad_rows = grad_rows + lax.ppermute(grad_rows, "ctx", [(0, 1), (1, 0)])
    extra = gains_grad.reshape(2, 16, -1).swapaxes(0, 1).reshape(16, -1)
    grads, small = fast_reduce(factors, extra, 5, "scatter_encoder")
    grad_rows, grads = lax.optimization_barrier((grad_rows, grads))
    all_rows = exchange(grad_rows.reshape(-1, 1152), True, 6, "rows")
    all_rows = all_rows.reshape(16 * segments, -1)
    modulate_grad = lax.dot_general(
        act_mine.astype(F32), all_rows, (((0,), (0,)), ((), ())), precision=exact
    )
    offset_grad = lax.dynamic_slice_in_dim(
        jnp.sum(all_rows, axis=0), me * offset_size, offset_size, 0
    )
    encoder_grads = (
        modulate_grad,
        offset_grad,
        grads[0],
        small.reshape(2, -1),
        grads[1],
        grads[2],
        grads[3],
    )
    return velocity, latent_full, decoder_flat + encoder_flat, encoder_grads, decoder_grads


def plain_gather(block):
    parts = [lax.all_gather(block[k], "dp", axis=0, tiled=True) for k in (0, 1, 2, 4, 5, 6)]
    gains = lax.all_gather(block[3], "dp", axis=1, tiled=True).astype(F32)
    modulate, offset, triple, mixing, expand, reduce_w = parts
    return modulate, offset.astype(F32), (triple, mixing, expand, reduce_w, gains)


def plain_reduce(factors, grad_modulation, gains_grad):
    def rows(values, dim=0):
        part = lax.psum_scatter(values, "dp", scatter_dimension=dim, tiled=True)
        return lax.psum(part.astype(BF16), "ctx").astype(F32)

    offset = rows(jnp.sum(grad_modulation, axis=0, dtype=F32))
    modulate, triple, mixing, expand, reduce_w = [rows(outer_sum(a, b)) for a, b in factors]
    return modulate, offset, triple, rows(gains_grad, 1), mixing, expand, reduce_w


def plain_step(flat, cotangent, context, segment_local, valid, timesteps, encoder, decoder):
    picks = (
        segment_local[..., None] == jnp.arange(timesteps.shape[-1], dtype=jnp.int32)
    ).astype(F32)
    times = jnp.sum(picks * timesteps[:, None, :].astype(F32), axis=-1)
    cond = embed_times(times, flat.shape[1]).reshape(flat.shape)
    modulate, offset, encoder_weights = plain_gather(encoder)
    encoder_act = jax.nn.silu(cond).astype(BF16)
    encoder_out, encoder_kept = block_forward(
        flat, dense(encoder_act, modulate) + offset, encoder_weights, context
    )
    latent_full = valid * encoder_out
    decoder_pre = latent_full + cond
    decoder_act = jax.nn.silu(decoder_pre).astype(BF16)
    modulate, offset, decoder_weights = plain_gather(decoder)
    decoder_out, decoder_kept = block_forward(
        flat, dense(decoder_act, modulate) + offset, decoder_weights, context
    )
    decoder_flat, grad_modulation, factors, gains_grad = block_backward(
        valid * cotangent, decoder_kept, decoder_weights, context
    )
    grad_act = dense_back(grad_modulation, modulate)
    decoder_grads = plain_reduce(
        ((decoder_act, grad_modulation),) + factors, grad_modulation, gains_grad
    )
    unused_silu, silu_pull = jax.vjp(jax.nn.silu, decoder_pre)
    encoder_flat, grad_modulation, factors, gains_grad = block_backward(
        valid * silu_pull(grad_act)[0], encoder_kept, encoder_weights, context
    )
    encoder_grads = plain_reduce(
        ((encoder_act, grad_modulation),) + factors, grad_modulation, gains_grad
    )
    return valid * decoder_out, latent_full, decoder_flat + encoder_flat, encoder_grads, decoder_grads


def local(fast, tokens, cotangent, segment, rows, columns, padding, timesteps, *weights):
    batch, half, width = tokens.shape
    start = lax.axis_index("ctx") * half
    segment_local = lax.dynamic_slice_in_dim(segment, start, half, 1)
    rows_local = lax.dynamic_slice_in_dim(rows, start, half, 1)
    columns_local = lax.dynamic_slice_in_dim(columns, start, half, 1)
    padding_local = lax.dynamic_slice_in_dim(padding, start, half, 1)
    place_query = start + jnp.arange(half, dtype=jnp.int32)
    place_key = jnp.arange(segment.shape[1], dtype=jnp.int32)
    allowed = (segment_local[:, :, None] == segment[:, None, :]) & (
        (padding[:, None, :] == 0) | (place_query[None, :, None] == place_key[None, None, :])
    )
    cosine, sine = rope_tables(rows_local.reshape(-1), columns_local.reshape(-1))
    context = (batch, half, allowed, cosine, sine)
    valid = (1 - padding_local).astype(F32).reshape(-1, 1)
    flat = tokens.reshape(-1, width).astype(F32)
    step = fast_step if fast else plain_step
    velocity, latent, token_grad, encoder_grads, decoder_grads = step(
        flat,
        cotangent.reshape(-1, width).astype(F32),
        context,
        segment_local,
        valid,
        timesteps,
        weights[:7],
        weights[7:],
    )
    return (
        velocity.astype(BF16).reshape(batch, half, width),
        latent.astype(BF16).reshape(batch, half, width),
        token_grad.reshape(batch, half, width),
        *encoder_grads,
        *decoder_grads,
    )


def solution(mesh):
    fast = dict(mesh.shape) == {"dp": math.prod(GRID), "ctx": 2}
    block = (
        P("dp", None),
        P("dp"),
        P("dp", None),
        P(None, "dp"),
        P("dp", None),
        P("dp", None),
        P("dp", None),
    )
    slots = P("dp", "ctx", None)
    return jax.shard_map(
        functools.partial(local, fast),
        mesh=mesh,
        in_specs=(slots, slots) + (P("dp", None),) * 5 + block + block,
        out_specs=(slots, slots, slots) + block + block,
        check_vma=False,
    )
```

time: 4610 us -> 1130 us (0.25)
  waiting for transfers between devices: 3880 us -> 0.01 us
  Pallas kernels: 0 us -> 795 us
  blocking collectives: 244 us -> 11.1 us
  matrix products: 238 us -> 115 us
    reduce_scatter x8 -> x0, waiting for transfers between devices: 2220 us -> none  [the longest x2 964 us: reduce_grads(): lax.psum_scatter(grads[0], 'dp', scatter_dimension=0, tiled=True)]
    all_gather x10 -> x0, waiting for transfers between devices: 975 us -> none  [the longest x2 326 us: block_forward(): lax.all_gather(weights[3], 'dp', axis=0, tiled=True)]
    pallas_call x0 -> x7, Pallas kernels: none -> 795 us  [the longest x2 373 us: gather(): pl.pallas_call(functools.partial(gather_kernel, units, count, stride, gro...]
    unnamed x31 -> x0, waiting for transfers between devices: 684 us -> none
    unnamed x2 -> x0, blocking collectives: 157 us -> none
    dot_general x24 -> x18, matrix products: 152 us -> 46 us  [the longest x10 36.2 us: dense(): return jnp.dot(values, weight, preferred_element_type=F32)]
    all_gather x4 -> x2, blocking collectives: 79.6 us -> 6.46 us  [block_forward(): value_heads = lax.all_gather(values_local, 'ctx', axis=1, tiled=True)]
  transfers between devices with their start and end apart: 25 -> 3, of which waited for: 20 -> 0; matrix products, arithmetic and copies ran while one was open for 7% -> 4% of each run, Pallas kernels for 0% -> 0%
where the time goes in v1:
time: 1130 us; the launch traced here: 1110 us
  Pallas kernels  795 us (70%)
  local copies, waits for them, and re-layouts  121 us (11%)
  matrix products  115 us (10%)
  other arithmetic  67 us (6%)
    pallas_call x2, Pallas kernels, gather(): pl.pallas_call(functools.partial(gather_kernel, units, count, stride, gro...  373 us
    pallas_call x2, Pallas kernels, scatter(): pl.pallas_call(functools.partial(scatter_kernel, tuple(first), tuple(cols...  345 us
    pallas_call x3, Pallas kernels, exchange(): pl.pallas_call(functools.partial(exchange_kernel, broadcast), name=name,...  77.3 us
    dot_general x9, matrix products, dense_back(): lax.dot_general(grads, weight, (((1,), (1,)), ((), ())), preferred_elemen...  58.5 us
    dot_general x10, matrix products, dense(): return jnp.dot(values, weight, preferred_element_type=F32)  36.2 us
  transfers between devices with their start and end apart: 3, of which 0 were waited for; matrix products, arithmetic and copies ran while one was open for 4% of the time, Pallas kernels for 0%

profile of v1, /device:TPU:0, one launch (start us, length us, event | category | flops | bytes accessed | tf_op | source)
XLA Modules:
  0.0 1113.5 jit_solution(17758238252679309796)
XLA Ops:
  5.0 10.7 small.1
  20.2 33.3 %partial.1 = f32[16,24,1152]{2,1,0:T(8,128)} custom-call(f32[16,24,1152]{2,1,0:T(8,128)} %reshape.1010.in_ref), custom_call_target="tpu_custom_call" | custom-call | tf_op jit(solution)/shard_map/partial/pallas_call | solution.py:239
  62.3 175.5 %gather_encoder.1 = (bf16[4,2,2,72,3456]{4,3,2,1,0:T(8,128)(2,1)}, bf16[4,2,2,72,1152]{4,3,2,1,0:T(8,128)(2,1)}, bf16[4,2,2,72,6144]{4,3,2,1,0:T(8,128)(2,1)}, bf16[4,2,2,192,1152]{4,3,2,1,0:T(8,128)(2,1)}) custom-call(bf16[72,3456]{1,0:T(8,128)(2,1)} %refs_0_.1, bf16[72,1152]{1,0:T(8,128)(2,1)} %refs_1_.1, bf16[72,6144]{1,0:T(8,128)(2,1)} %refs_2_.1, ...), custom_call_target="tpu_custom_call" | custom-call | tf_op jit(solution)/shard_map/gather_encoder/pallas_call | solution.py:171
  237.8 4.6 fusion.149
  247.9 2.2 all_gather.13
  250.1 2.4 all-gather
  259.7 7.5 fusion.150
  267.2 5.6 fusion.151
  277.0 197.4 %gather_decoder.1 = (bf16[4,2,2,72,6912]{4,3,2,1,0:T(8,128)(2,1)}, bf16[4,2,2,72,3456]{4,3,2,1,0:T(8,128)(2,1)}, bf16[4,2,2,72,1152]{4,3,2,1,0:T(8,128)(2,1)}, b...) custom-call(bf16[72,6912]{1,0:T(8,128)(2,1)} %refs_0_.2, bf16[72,3456]{1,0:T(8,128)(2,1)} %refs_1_.2, ...), custom_call_target="tpu_custom_call" | custom-call | tf_op jit(solution)/shard_map/gather_decoder/pallas_call | solution.py:171
  474.5 8.2 convolution_add_fusion
  493.8 2.4 all_gather.15
  496.2 4.0 all-gather.1
  506.7 3.5 fusion.135
  514.0 3.5 fusion.6
  520.3 10.1 multiply_reduce_fusion.7
  536.7 3.2 multiply_reduce_fusion.1
  543.4 2.4 multiply_convert_fusion.1
  554.1 3.2 fusion.207
  584.3 2.6 pad_maximum_fusion.refs_11_
  609.7 6.7 convert_dynamic-update-slice_fusion.3
  627.0 198.8 %scatter_decoder.1 = f32[72,21504]{1,0:T(8,128)} custom-call(bf16[4,2,2,80,128]{4,3,2,1,0:T(8,128)(2,1)} %bitcast.399, bf16[4,2,2,80,128]{4,3,2,1,0:T(8,128)(2,1)} %bitcast.398, bf16[4,2,2,80,128]{4,3,2,1,0:T(8,128)(2,1)} %bitcast.397, bf16[4,2,2,80,128]{4,3,2,1,0:T(8,128)(2,1)} %bitcast.396, bf16[4,2,2,80,128]{4,3,2,1,0:T(8,128)(2,1)} %bitcast.394, ...), custom_call_target="tpu_custom_call" | custom-call | tf_op jit(solution)/shard_map/scatter_decoder/pallas_call | solution.py:558
  827.9 3.0 slice.183
  830.9 2.9 slice.189
  839.1 11.8 %multiply_convert_fusion.10 = (bf16[128,1152]{1,0:T(8,128)(2,1)}, f32[128,1152]{1,0:T(8,128)S(1)}) fusion(f32[128,6912]{1,0:T(8,128)S(1)} %copy-done.12, f32[128,1152]{1,0:T(8,128)} %get-tuple-element.165, f32[128]{0:T(128)} %get-tuple-element.180, bf16[128,6912]{1,0:T(8,128)(2,1)} %fusion.84.refs_8_, bf16[1152,6912]{1,0:T(8,128)(2,1)} %bitcast.324), kind=kOutput, calls=%fused_computation.165 | convolution fusion | flops 2040201216 | bytes 19759616 | tf_op jit(solution)/shard_map/dot_general | solution.py:664
  850.9 6.6 fusion.9
  857.6 10.3 multiply_reduce_fusion.6
  904.1 2.3 fusion.47
  907.4 6.1 fusion.40
  914.8 145.7 %scatter_encoder.1 = f32[72,14592]{1,0:T(8,128)} custom-call(bf16[4,2,2,80,128]{4,3,2,1,0:T(8,128)(2,1)} %bitcast.391, bf16[4,2,2,80,128]{4,3,2,1,0:T(8,128)(2,1)} %bitcast.390, bf16[4,2,2,80,128]{4,3,2,1,0:T(8,128)(2,1)} %bitcast.389, bf16[4,2,2,80,128]{4,3,2,1,0:T(8,128)(2,1)} %bitcast.387, bf16[4,2,2,80,128]{4,3,2,1,0:T(8,128)(2,1)} %bitcast.386, ...), custom_call_target="tpu_custom_call" | custom-call | tf_op jit(solution)/shard_map/scatter_encoder/pallas_call | solution.py:558
  1065.1 2.3 fusion.130
  1074.7 33.4 %rows.1 = f32[16,24,1152]{2,1,0:T(8,128)} custom-call(f32[24,1152]{1,0:T(8,128)} %reshape.1059.in_ref), custom_call_target="tpu_custom_call" | custom-call | tf_op jit(solution)/shard_map/rows/pallas_call | solution.py:239
  1109.9 2.4 fusion.125
  (620 shorter events, 195.1 us)
Async XLA Ops:
  0.7 17.5 %copy-start = (bf16[72,6912]{1,0:T(8,128)(2,1)S(1)}, bf16[72,6912]{1,0:T(8,128)(2,1)}, u32[]{:S(2)}) copy-start(bf16[72,6912]{1,0:T(8,128)(2,1)} %param.28) | copy-start | bytes 2985988
  18.1 257.5 %copy-start.100 = (f32[64,576]{1,0:T(8,128)}, f32[64,576]{1,0:T(8,128)S(1)}, u32[]{:S(2)}) copy-start(f32[64,576]{1,0:T(8,128)S(1)} %get-tuple-element.157) | copy-start | bytes 442372
  18.1 257.5 %copy-start.102 = (f32[64,576]{1,0:T(8,128)}, f32[64,576]{1,0:T(8,128)S(1)}, u32[]{:S(2)}) copy-start(f32[64,576]{1,0:T(8,128)S(1)} %get-tuple-element.158) | copy-start | bytes 442372
  56.9 425.9 %copy-start.142 = (f32[128]{0:T(128)}, f32[128]{0:T(128)S(1)}, u32[]{:S(2)}) copy-start(f32[128]{0:T(128)S(1)} %fusion.120) | copy-start | bytes 1540
  57.9 217.7 %copy-start.145 = (s32[128]{0:T(128)}, s32[128]{0:T(128)S(1)}, u32[]{:S(2)}) copy-start(s32[128]{0:T(128)S(1)} %get-tuple-element.181) | copy-start | bytes 1540
  62.2 180.1 %copy-start.62 = (bf16[128,1152]{1,0:T(8,128)(2,1)}, bf16[128,1152]{1,0:T(8,128)(2,1)S(1)}, u32[]{:S(2)}) copy-start(bf16[128,1152]{1,0:T(8,128)(2,1)S(1)} %fusion.34) | copy-start | bytes 884740
  258.7 8.5 copy-start.140
  259.4 7.7 copy-start.147
  259.7 7.5 copy-start.74
  277.0 205.8 %copy-start.104 = (bf16[128,1152]{1,0:T(8,128)(2,1)}, bf16[128,1152]{1,0:T(8,128)(2,1)S(1)}, u32[]{:S(2)}) copy-start(bf16[128,1152]{1,0:T(8,128)(2,1)S(1)} %get-tuple-element.41) | copy-start | bytes 884740
  474.5 9.3 slice-start.6
  474.5 9.3 slice-start.7
  492.9 9.5 copy-start.82
  492.9 18.7 %slice-start = ((s8[14155776]{0:T(1024)(128)(4,1)}), s8[1572864]{0:T(1024)(128)(4,1)S(1)}, s32[]{:S(2)}) async-start(s8[14155776]{0:T(1024)(128)(4,1)} %bitcast.314), calls=%async_computation | async-start | bytes 3145728
  496.2 6.8 copy-start.59
  502.4 9.2 slice-start.1
  503.7 7.9 slice-start.2
  510.2 20.2 %copy-start.13 = (f32[128,1152]{1,0:T(8,128)}, f32[128,1152]{1,0:T(8,128)S(1)}, u32[]{:S(2)}) copy-start(f32[128,1152]{1,0:T(8,128)S(1)} %get-tuple-element.76) | copy-start | bytes 1769476
  518.8 11.6 %copy-start.53 = (f32[128,1152]{1,0:T(8,128)}, f32[128,1152]{1,0:T(8,128)S(1)}, u32[]{:S(2)}) copy-start(f32[128,1152]{1,0:T(8,128)S(1)} %fusion.154) | copy-start | bytes 1769476
  550.4 36.6 %collective-permute-start = (bf16[2,1,128,1152]{3,2,1,0:T(8,128)(2,1)}, bf16[2,1,128,1152]{3,2,1,0:T(8,128)(2,1)}, u32[]{:S(2)}, u32[]{:S(2)}) collective-permute-start(bf16[2,1,128,1152]{3,2,1,0:T(8,128)(2,1)} %fusion.51), channel_id=1, source_target_pairs={{0,1},{1,0},{2,3},{3,2},{4,5},{5,4},{6,7},{7,6},{8,9},{9,8},{10,11... | collective-permute-start | bytes 1769480 | tf_op jit(solution)/shard_map/ppermute | solution.py:780
  609.7 7.3 copy-start.143
  609.7 9.3 copy-start.26
  609.7 9.3 copy-start.41
  609.7 9.3 copy-start.151
  830.8 8.2 copy-start.12
  850.9 17.4 %copy-start.94 = (f32[128,1152]{1,0:T(8,128)}, f32[128,1152]{1,0:T(8,128)S(1)}, u32[]{:S(2)}) copy-start(f32[128,1152]{1,0:T(8,128)S(1)} %get-tuple-element.70) | copy-start | bytes 1769476
  857.6 10.4 copy-start.69
  857.6 10.4 copy-start.71
  857.6 10.4 copy-start.157
  857.6 10.4 copy-start.148
  881.0 3.6 collective-permute-start.1
  1064.7 9.3 collective-permute-start.2
  (142 other events, 389.3 us)

commit v2 on v1

--- a/solution.py
+++ b/solution.py
@@ -32,26 +32,63 @@
         pl.when(cond)(body)
 
 
-def greet(z, y, x, c):
+def greet():
     barrier = pltpu.get_barrier_semaphore()
-
-    def signal(target):
-        pl.semaphore_signal(barrier, inc=1, device_id=target, device_id_type=MESH)
-
-    signal(device(z, 1 - y, x, c))
-    signal(device(z, y, 1 - x, c))
-    signal(device(z, y, x, 1 - c))
-    pl.when(z < 3)(lambda: signal(device(z + 1, y, x, c)))
-    pl.when(z > 0)(lambda: signal(device(z - 1, y, x, c)))
-    pl.semaphore_wait(barrier, 3 + lax.div(z + 3, 4) + lax.div(6 - z, 4))
+    me = lax.axis_index("dp")
+    c = lax.axis_index("ctx")
+    for k in range(1, 16):
+        pl.semaphore_signal(
+            barrier, inc=1, device_id=(lax.rem(me + k, 16), c), device_id_type=MESH
+        )
+    pl.semaphore_signal(barrier, inc=1, device_id=(me, 1 - c), device_id_type=MESH)
+    pl.semaphore_wait(barrier, 16)
+
+
+class Exchange:
+    def __init__(self, broadcast, in_ref, out_ref, ssem, rsem, lsem):
+        self.refs = (in_ref, out_ref, ssem, rsem, lsem)
+        self.broadcast = broadcast
+        self.me = lax.axis_index("dp")
+
+    def source(self, target):
+        return self.refs[0] if self.broadcast else self.refs[0].at[target]
+
+    def copy(self, k, target, slot):
+        return pltpu.make_async_remote_copy(
+            self.source(target),
+            self.refs[1].at[slot],
+            self.refs[2].at[k],
+            self.refs[3].at[k],
+            device_id=(target, lax.axis_index("ctx")),
+            device_id_type=MESH,
+        )
+
+    def own(self):
+        return pltpu.make_async_copy(
+            self.source(self.me), self.refs[1].at[self.me], self.refs[4].at[0]
+        )
+
+    def start(self):
+        for k in range(1, 16):
+            self.copy(k, lax.rem(self.me + k, 16), self.me).start()
+        self.own().start()
+
+    def wait(self):
+        self.own().wait()
+        for k in range(1, 16):
+            self.copy(k, lax.rem(self.me + k, 16), self.me).wait_send()
+            origin = lax.rem(self.me + 16 - k, 16)
+            self.copy(k, origin, origin).wait_recv()
 
 
 def gather_kernel(units, count, stride, group, lag, *refs):
     w = refs[:count]
-    o = refs[count : 2 * count]
-    ssem, rsem, lsem, csem, crsem = refs[2 * count :]
+    o = refs[count + 1 : 2 * count + 1]
+    ssem, rsem, lsem, csem, crsem, es, er, el = refs[2 * count + 2 :]
     z, y, x, c = coords()
-    greet(z, y, x, c)
+    greet()
+    side = Exchange(False, refs[count], refs[2 * count + 1], es, er, el)
+    side.start()
     up = device(z + 1, y, x, c)
     down = device(z - 1, y, x, c)
     partner = {"y": device(z, 1 - y, x, c), "x": device(z, y, 1 - x, c)}
@@ -159,98 +196,77 @@
 
     pl.when(c == 0)(lambda: run(units[0], units[1]))
     pl.when(c == 1)(lambda: run(units[1], units[0]))
+    side.wait()
 
 
 ANY = pl.BlockSpec(memory_space=pl.ANY)
 DMA = pltpu.SemaphoreType.DMA
 
 
-def gather(shards, units, collective_id, stride, group, lag, name):
+SIDE = [DMA((16,)), DMA((16,)), DMA((1,))]
+
+
+def gather(shards, rows, units, collective_id, stride, group, lag, name):
     count = len(shards)
     most = max(len(units[0]), len(units[1]))
+    shapes = [jax.ShapeDtypeStruct(GRID + s.shape, s.dtype) for s in shards]
     return pl.pallas_call(
         functools.partial(gather_kernel, units, count, stride, group, lag),
         name=name,
-        out_shape=[jax.ShapeDtypeStruct(GRID + s.shape, s.dtype) for s in shards],
-        in_specs=[ANY] * count,
-        out_specs=[ANY] * count,
-        scratch_shapes=[DMA((most, 8)), DMA((most, 8)), DMA((most,)), DMA((most,)), DMA((most,))],
+        out_shape=shapes + [jax.ShapeDtypeStruct(rows.shape, rows.dtype)],
+        in_specs=[ANY] * (count + 1),
+        out_specs=[ANY] * (count + 1),
+        scratch_shapes=[DMA((most, 8)), DMA((most, 8)), DMA((most,)), DMA((most,)), DMA((most,))]
+        + SIDE,
         compiler_params=pltpu.CompilerParams(collective_id=collective_id, has_side_effects=True),
-    )(*shards)
-
-
-def spans(matrix, tiles, shifts=0):
-    orders = ("zyx", "zxy", "yzx", "xzy")
-    out = []
-    at = 0
-    for k, t in enumerate(tiles):
-        out.append((matrix, at * 128, t * 128, orders[(k + shifts) % 4]))
-        at += t
-    return out
-
-
-def exchange_kernel(broadcast, in_ref, out_ref, ssem, rsem, lsem):
-    me = lax.axis_index("dp")
-    c = lax.axis_index("ctx")
-    barrier = pltpu.get_barrier_semaphore()
-    for k in range(1, 16):
-        pl.semaphore_signal(
-            barrier, inc=1, device_id=(lax.rem(me + k, 16), c), device_id_type=MESH
-        )
-    pl.semaphore_wait(barrier, 15)
-
-    def source(target):
-        return in_ref if broadcast else in_ref.at[target]
-
-    def copy(k):
-        target = lax.rem(me + k, 16)
-        return pltpu.make_async_remote_copy(
-            source(target),
-            out_ref.at[me],
-            ssem.at[k],
-            rsem.at[k],
-            device_id=(target, c),
-            device_id_type=MESH,
-        )
-
-    def arrival(k):
-        origin = lax.rem(me + 16 - k, 16)
-        return pltpu.make_async_remote_copy(
-            source(origin),
-            out_ref.at[origin],
-            ssem.at[k],
-            rsem.at[k],
-            device_id=(origin, c),
-            device_id_type=MESH,
-        )
-
-    for k in range(1, 16):
-        copy(k).start()
-    own = pltpu.make_async_copy(source(me), out_ref.at[me], lsem.at[0])
-    own.start()
-    own.wait()
-    for k in range(1, 16):
-        copy(k).wait_send()
-        arrival(k).wait_recv()
-
-
-def exchange(values, broadcast, collective_id, name):
-    shape = values.shape if broadcast else values.shape[1:]
+    )(*shards, rows)
+
+
+def gather_units(shards, size):
+    orders = (
+        ("xzy", "yzx", "zyx", "yzx", "xzy", "zxy"),
+        ("yzx", "xzy", "zxy", "xzy", "yzx", "zyx"),
+    )
+    units = ([], [])
+    load = [0, 0]
+    for m, shard in enumerate(shards):
+        rows, columns = shard.shape
+        tiles = columns // 128
+        cuts = max(1, round(tiles * rows / 72 / size))
+        at = 0
+        for k in range(cuts):
+            n = tiles // cuts + (1 if k < tiles % cuts else 0)
+            core = 0 if load[0] <= load[1] else 1
+            order = orders[core][len(units[core]) % 6]
+            units[core].append((m, at * 128, n * 128, order))
+            load[core] += n * rows
+            at += n
+    return tuple(units[0]), tuple(units[1])
+
+
+def exchange_kernel(in_ref, out_ref, *sems):
+    greet()
+    side = Exchange(True, in_ref, out_ref, *sems)
+    side.start()
+    side.wait()
+
+
+def exchange(values, collective_id, name):
     return pl.pallas_call(
-        functools.partial(exchange_kernel, broadcast),
+        exchange_kernel,
         name=name,
-        out_shape=jax.ShapeDtypeStruct((16,) + shape, values.dtype),
+        out_shape=jax.ShapeDtypeStruct((16,) + values.shape, values.dtype),
         in_specs=[ANY],
         out_specs=ANY,
-        scratch_shapes=[DMA((16,)), DMA((16,)), DMA((1,))],
+        scratch_shapes=SIDE,
         compiler_params=pltpu.CompilerParams(collective_id=collective_id, has_side_effects=True),
     )(values)
 
 
-LAG = (0, 3, 5, 7, 9, 11)
-RECV_SLOTS = 14
-SEND_SLOTS = 13
-FIRST_SLOTS = 6
+LAG = (0, 2, 3, 4, 5, 6)
+RECV_SLOTS = 9
+SEND_SLOTS = 8
+FIRST_SLOTS = 4
 UNIT = 384
 ROWS = 72
 PADDED = 80
@@ -260,18 +276,19 @@
     nv = len(first) - 1
     xt = refs[:nv]
     dy = refs[nv : nv + dy_count]
-    out = refs[nv + dy_count]
+    out = refs[nv + dy_count + 1]
     (
         xts, dys, a_s1, a_s2, a_t, a_su, a_sd, e_s1, e_t, e_su, e_sd, e_sq,
         a_b1, a_b2, a_bu, a_bd, e_b1, e_bu, e_bd, e_bq, outs,
-        ssem, rsem, xl, xs, xr, yl, ys, yr, ol, os, orr,
-    ) = refs[nv + dy_count + 1 :]
+        ssem, rsem, xl, xs, xr, yl, ys, yr, ol, os, orr, es, er, el,
+    ) = refs[nv + dy_count + 3 :]
     z, y, x, c = coords()
     total = first[-1] // 2
     sibling = device(z, y, x, 1 - c)
     up = device(z + 1, y, x, c)
     down = device(z - 1, y, x, c)
-    greet(z, y, x, c)
+    greet()
+    side = Exchange(True, refs[nv + dy_count], refs[nv + dy_count + 2], es, er, el)
     lanes = pl.ds(pl.multiple_of(c * 128, 128), 128)
     offsets = []
     at = 0
@@ -284,16 +301,14 @@
             src, dst, send, recv, device_id=target, device_id_type=MESH
         )
 
-    def x_views(v, k):
-        o, b = k // 2, k % 2
-        src = xt[v].at[:, :, b] if o == 0 else xt[v].at[:, b]
-        return src, xts.at[v, o, b, :, :, :, lanes]
-
-    def x_local(v, k):
-        return pltpu.make_async_copy(*x_views(v, k), xl.at[v, k])
-
-    def x_remote(v, k):
-        return remote(*x_views(v, k), xs.at[v, k], xr.at[v, k], sibling)
+    def x_views(v):
+        return xt[v], xts.at[v, :, :, lanes]
+
+    def x_local(v):
+        return pltpu.make_async_copy(*x_views(v), xl.at[v])
+
+    def x_remote(v):
+        return remote(*x_views(v), xs.at[v], xr.at[v], sibling)
 
     def y_views(k):
         return dy[k], dys.at[lanes, pl.ds(offsets[k], dy[k].shape[1])]
@@ -306,20 +321,20 @@
 
     fresh = [source[v] not in source[:v] for v in range(nv)]
     for v in range(nv):
-        for k in range(4):
-            x_local(v, k).start()
-            x_remote(v, k).start()
+        x_local(v).start()
+        x_remote(v).start()
         if fresh[v]:
             y_local(source[v]).start()
             y_remote(source[v]).start()
+        if v == 0:
+            side.start()
 
     def arrive(tick):
         for v in range(nv):
 
             def wait(v=v):
-                for k in range(4):
-                    x_local(v, k).wait()
-                    x_remote(v, k).wait_recv()
+                x_local(v).wait()
+                x_remote(v).wait_recv()
                 if fresh[v]:
                     y_local(source[v]).wait()
                     y_remote(source[v]).wait_recv()
@@ -444,7 +459,9 @@
 
     def product(i, bit):
         v, col = unit(i)
-        lhs = xts[v, axes(i)[0], bit].reshape(8 * PADDED, 256)
+        o = axes(i)[0]
+        chips = [4 * k + bit * (1 + o) + q * (2 - o) for k in range(4) for q in range(2)]
+        lhs = jnp.concatenate([xts[v, chip] for chip in chips], axis=0)
         whole = jnp.dot(lhs, dys[:, pl.ds(col, UNIT)], preferred_element_type=F32)
         return whole.reshape(8, PADDED, UNIT)[:, :ROWS]
 
@@ -529,8 +546,7 @@
 
     lax.fori_loop(0, total + SEND_SLOTS, tick, 0)
     for v in range(nv):
-        for k in range(4):
-            x_remote(v, k).wait_send()
+        x_remote(v).wait_send()
     for k in range(dy_count):
         y_remote(k).wait_send()
     half = out.at[:, pl.ds(0, total * UNIT)]
@@ -538,9 +554,10 @@
     everything = remote(half, half, os.at[0], orr.at[0], sibling)
     everything.wait_send()
     everything.wait_recv()
-
-
-def scatter(xts, dys, source, collective_id, name):
+    side.wait()
+
+
+def scatter(xts, dys, source, rows, collective_id, name):
     nv = len(xts)
     starts = []
     width = 0
@@ -558,11 +575,14 @@
     return pl.pallas_call(
         functools.partial(scatter_kernel, tuple(first), tuple(cols), tuple(source), len(dys)),
         name=name,
-        out_shape=jax.ShapeDtypeStruct((ROWS, first[-1] * UNIT), F32),
-        in_specs=[ANY] * (nv + len(dys)),
-        out_specs=ANY,
+        out_shape=[
+            jax.ShapeDtypeStruct((ROWS, first[-1] * UNIT), F32),
+            jax.ShapeDtypeStruct((16,) + rows.shape, rows.dtype),
+        ],
+        in_specs=[ANY] * (nv + len(dys) + 1),
+        out_specs=[ANY] * 2,
         scratch_shapes=[
-            vmem((nv, 2, 2, 4, 2, PADDED, 256), BF16),
+            vmem((nv, 16, PADDED, 256), BF16),
             vmem((256, width), BF16),
             vmem((f, 4, 2, ROWS, 128), BF16),
             vmem((s, 4, ROWS, 128), BF16),
@@ -585,20 +605,21 @@
             vmem((total, ROWS, UNIT), F32),
             DMA((s, 16)),
             DMA((r, 16)),
-            DMA((nv, 4)),
-            DMA((nv, 4)),
-            DMA((nv, 4)),
+            DMA((nv,)),
+            DMA((nv,)),
+            DMA((nv,)),
             DMA((len(dys),)),
             DMA((len(dys),)),
             DMA((len(dys),)),
             DMA((1,)),
             DMA((1,)),
             DMA((1,)),
-        ],
+        ]
+        + SIDE,
         compiler_params=pltpu.CompilerParams(
-            collective_id=collective_id, has_side_effects=True, vmem_limit_bytes=60 * 1024 * 1024
+            collective_id=collective_id, has_side_effects=True, vmem_limit_bytes=62 * 1024 * 1024
         ),
-    )(*xts, *dys)
+    )(*xts, *dys, rows)
 
 
 def layer_norm(values):
@@ -819,39 +840,44 @@
     turned = values.T.reshape(16, groups, -1, values.shape[0])
     rows = turned.shape[2]
     turned = jnp.pad(turned, ((0, 0), (0, 0), (0, PADDED - rows), (0, 0)))
-    return [turned[:, g].reshape(GRID + turned.shape[2:]) for g in range(groups)]
-
-
-def fast_reduce(factors, extra, collective_id, name):
-    tokens = factors[0][0].shape[0]
+    return [turned[:, g] for g in range(groups)]
+
+
+def fast_reduce(blocks, rows, collective_id, name):
     xts = []
     dys = []
     source = []
-    for k, (left, right) in enumerate(factors):
-        groups = 3 if k == len(factors) - 1 else 1
-        xts += shard_rows(left, groups)
-        dys.append(right)
-        source += [k] * groups
-    count = extra.shape[1]
-    lines = -(-count // tokens)
-    packed = jnp.pad(extra, ((0, 0), (0, lines * tokens - count))).reshape(16, lines, tokens)
-    packed = jnp.pad(packed, ((0, 0), (0, PADDED - lines), (0, 0))).astype(BF16)
-    xts.append(packed.reshape(GRID + packed.shape[1:]))
-    dys.append(jnp.eye(tokens, UNIT, dtype=BF16))
-    source.append(len(factors))
-    out = scatter(xts, dys, source, collective_id, name)
-    grads = []
+    for factors, extra in blocks:
+        for k, (left, right) in enumerate(factors):
+            groups = 3 if k == len(factors) - 1 else 1
+            source += [len(dys)] * groups
+            xts += shard_rows(left, groups)
+            dys.append(right)
+        tokens = left.shape[0]
+        lines = -(-extra.shape[1] // tokens)
+        packed = jnp.pad(extra, ((0, 0), (0, lines * tokens - extra.shape[1])))
+        packed = packed.reshape(16, lines, tokens).astype(BF16)
+        xts.append(jnp.pad(packed, ((0, 0), (0, PADDED - lines), (0, 0))))
+        source.append(len(dys))
+        dys.append(jnp.eye(tokens, UNIT, dtype=BF16))
+    out, rows = scatter(xts, dys, source, rows, collective_id, name)
+    results = []
     at = 0
-    for left, right in factors[:-1]:
-        grads.append(out[:, at : at + right.shape[1]])
-        at += right.shape[1]
-    width = factors[-1][1].shape[1]
-    rows = factors[-1][0].shape[1] // 48
-    parts = [out[:rows, at + g * width : at + (g + 1) * width] for g in range(3)]
-    grads.append(jnp.concatenate(parts, axis=0))
-    at += 3 * width
-    small = out[:lines, at : at + tokens].reshape(-1)[:count]
-    return grads, small
+    for factors, extra in blocks:
+        grads = []
+        for left, right in factors[:-1]:
+            grads.append(out[:, at : at + right.shape[1]])
+            at += right.shape[1]
+        width = factors[-1][1].shape[1]
+        count = factors[-1][0].shape[1] // 48
+        parts = [out[:count, at + g * width : at + (g + 1) * width] for g in range(3)]
+        grads.append(jnp.concatenate(parts, axis=0))
+        at += 3 * width
+        lines = -(-extra.shape[1] // tokens)
+        small = out[:lines, at : at + tokens].reshape(-1)[: extra.shape[1]]
+        at += UNIT
+        results.append((grads, small))
+    return results, rows
 
 
 def whole_rows(gathered):
@@ -873,7 +899,7 @@
     )
     size = small.shape[0]
     small = jnp.pad(small, (0, 2048 - size)).reshape(16, 128)
-    small = exchange(small, True, 0, "small").reshape(16, -1)
+    small = exchange(small, 0, "small").reshape(16, -1)
     encoder_offset = small[:, :offset_size].reshape(-1)
     decoder_offset = small[:, offset_size : 2 * offset_size].reshape(-1)
     at = 2 * offset_size
@@ -891,54 +917,25 @@
     me = lax.axis_index("dp")
     rows = encoder[0].shape[0]
     act_mine = lax.dynamic_slice_in_dim(act_rows, me * rows, rows, 1)
-    partial = dense(act_mine, encoder[0]).reshape(16, -1, 1152)
-    partial = exchange(partial, False, 1, "partial")
+    partial = dense(act_mine, encoder[0]).reshape(16, 8, -1)
+    shards = (encoder[2], encoder[4], encoder[5], encoder[6])
+    shards += (decoder[0], decoder[2], decoder[4], decoder[5], decoder[6])
+    *wholes, partial = gather(shards, partial, gather_units(shards, 7), 1, 1, 3, 1, "gather")
+    wholes = [whole_rows(w) for w in wholes]
+    encoder_weights = (*wholes[:4], encoder_gains)
+    modulate = wholes[4]
+    decoder_weights = (*wholes[5:], decoder_gains)
     modulation_rows = jnp.sum(partial, axis=0).reshape(segments, -1) + encoder_offset
     exact = lax.Precision.HIGHEST
     encoder_modulation = jnp.dot(picks, modulation_rows, precision=exact)
     cond_rows = lax.dynamic_slice_in_dim(all_cond, me * segments, segments, 0)
     cond = jnp.dot(picks, cond_rows, precision=exact)
 
-    encoder_units = (
-        tuple(spans(2, (6,) * 8) + spans(0, (6,))),
-        tuple(
-            [(0, 768 + at, n, o) for _, at, n, o in spans(0, (7, 7, 7))]
-            + spans(1, (4, 5), 3)
-            + spans(3, (2, 2, 2, 3), 1)
-        ),
-    )
-    triple, mixing, expand, reduce_w = gather(
-        [encoder[2], encoder[4], encoder[5], encoder[6]], encoder_units, 2, 1, 2, 1, "gather_encoder"
-    )
-    encoder_weights = (
-        whole_rows(triple),
-        whole_rows(mixing),
-        whole_rows(expand),
-        whole_rows(reduce_w),
-        encoder_gains,
-    )
     encoder_out, encoder_kept = block_forward(flat, encoder_modulation, encoder_weights, context)
     latent_full = valid * encoder_out
     decoder_pre = latent_full + cond
     decoder_act = jax.nn.silu(decoder_pre).astype(BF16)
 
-    decoder_units = (
-        tuple(spans(0, (7, 7, 7, 7, 7, 7, 6, 6)) + spans(1, (7, 7, 7, 6))),
-        tuple(spans(3, (6,) * 8) + spans(4, (2, 2, 2, 3)) + spans(2, (2, 2, 2, 3))),
-    )
-    shards = (decoder[0], decoder[2], decoder[4], decoder[5], decoder[6])
-    shards, decoder_act = lax.optimization_barrier((shards, decoder_act))
-    modulate, triple, mixing, expand, reduce_w = gather(
-        shards, decoder_units, 3, 1, 2, 1, "gather_decoder"
-    )
-    modulate = whole_rows(modulate)
-    decoder_weights = (
-        whole_rows(triple),
-        whole_rows(mixing),
-        whole_rows(expand),
-        whole_rows(reduce_w),
-        decoder_gains,
-    )
     decoder_modulation = dense(decoder_act, modulate) + decoder_offset
     decoder_out, decoder_kept = block_forward(flat, decoder_modulation, decoder_weights, context)
     velocity = valid * decoder_out
@@ -958,9 +955,20 @@
         ],
         axis=1,
     )
-    grads, small = fast_reduce(
-        ((decoder_act, grad_modulation),) + factors, extra, 4, "scatter_decoder"
-    )
+    decoder_block = (((decoder_act, grad_modulation),) + factors, extra)
+
+    encoder_flat, grad_modulation, factors, gains_grad = block_backward(
+        grad_latent, encoder_kept, encoder_weights, context
+    )
+    grad_rows = lax.dot_general(
+        picks.astype(BF16), grad_modulation, (((0,), (0,)), ((), ())), preferred_element_type=F32
+    )
+    grad_rows = grad_rows + lax.ppermute(grad_rows, "ctx", [(0, 1), (1, 0)])
+    extra = gains_grad.reshape(2, 16, -1).swapaxes(0, 1).reshape(16, -1)
+    results, all_rows = fast_reduce(
+        (decoder_block, (factors, extra)), grad_rows.astype(BF16).reshape(16, -1), 2, "scatter"
+    )
+    (grads, small), (encoder_parts, encoder_small) = results
     decoder_grads = (
         grads[0],
         small[:offset_size],
@@ -970,33 +978,19 @@
         grads[3],
         grads[4],
     )
-
-    encoder_flat, grad_modulation, factors, gains_grad = block_backward(
-        grad_latent, encoder_kept, encoder_weights, context
-    )
-    grad_rows = lax.dot_general(
-        picks.astype(BF16), grad_modulation, (((0,), (0,)), ((), ())), preferred_element_type=F32
-    )
-    grad_rows = grad_rows + lax.ppermute(grad_rows, "ctx", [(0, 1), (1, 0)])
-    extra = gains_grad.reshape(2, 16, -1).swapaxes(0, 1).reshape(16, -1)
-    grads, small = fast_reduce(factors, extra, 5, "scatter_encoder")
-    grad_rows, grads = lax.optimization_barrier((grad_rows, grads))
-    all_rows = exchange(grad_rows.reshape(-1, 1152), True, 6, "rows")
     all_rows = all_rows.reshape(16 * segments, -1)
-    modulate_grad = lax.dot_general(
-        act_mine.astype(F32), all_rows, (((0,), (0,)), ((), ())), precision=exact
-    )
+    modulate_grad = outer_sum(act_mine, all_rows)
     offset_grad = lax.dynamic_slice_in_dim(
-        jnp.sum(all_rows, axis=0), me * offset_size, offset_size, 0
+        jnp.sum(all_rows.astype(F32), axis=0), me * offset_size, offset_size, 0
     )
     encoder_grads = (
         modulate_grad,
         offset_grad,
-        grads[0],
-        small.reshape(2, -1),
-        grads[1],
-        grads[2],
-        grads[3],
+        encoder_parts[0],
+        encoder_small.reshape(2, -1),
+        encoder_parts[1],
+        encoder_parts[2],
+        encoder_parts[3],
     )
     return velocity, latent_full, decoder_flat + encoder_flat, encoder_grads, decoder_grads
 

time: 1130 us -> 1030 us (0.912); the launches traced: 1110 us -> 1030 us
  Pallas kernels: 795 us -> 705 us
    pallas_call x3 -> x1, Pallas kernels: 77.3 us -> 10.7 us  [exchange(): pl.pallas_call(exchange_kernel, name=name, out_shape=jax.ShapeDtypeStruct...]
    pallas_call x2 -> x1, Pallas kernels: 373 us -> 353 us  [gather(): pl.pallas_call(functools.partial(gather_kernel, units, count, stride, gro...]
    pallas_call x2 -> x1, Pallas kernels: 345 us -> 342 us  [scatter(): pl.pallas_call(functools.partial(scatter_kernel, tuple(first), tuple(cols...]
where the time goes in v2:
time: 1030 us
  Pallas kernels  705 us (68%)
  local copies, waits for them, and re-layouts  122 us (12%)
  matrix products  115 us (11%)
  other arithmetic  60.3 us (6%)
  blocking collectives  21.2 us (2%)
    pallas_call x1, Pallas kernels, gather(): pl.pallas_call(functools.partial(gather_kernel, units, count, stride, gro...  353 us
    pallas_call x1, Pallas kernels, scatter(): pl.pallas_call(functools.partial(scatter_kernel, tuple(first), tuple(cols...  342 us
    dot_general x9, matrix products, dense_back(): lax.dot_general(grads, weight, (((1,), (1,)), ((), ())), preferred_elemen...  58.6 us
    dot_general x10, matrix products, dense(): return jnp.dot(values, weight, preferred_element_type=F32)  36.3 us
    unnamed x341, local copies, waits for them, and re-layouts  20.8 us
  transfers between devices with their start and end apart: 3, of which 0 were waited for; matrix products, arithmetic and copies ran while one was open for 4% of the time, Pallas kernels for 0%

profile of v2, /device:TPU:0, one launch (start us, length us, event | category | flops | bytes accessed | tf_op | source)
XLA Modules:
  0.0 1027.3 jit_solution(16682604356498421625)
XLA Ops:
  5.0 10.7 %small.1 = f32[16,16,128]{2,1,0:T(8,128)} custom-call(f32[16,128]{1,0:T(8,128)} %pad_bitcast_fusion.7.in_ref), custom_call_target="tpu_custom_call" | custom-call | tf_op jit(solution)/shard_map/small/pallas_call | solution.py:255
  20.3 352.6 %gather.1 = (bf16[4,2,2,72,3456]{4,3,2,1,0:T(8,128)(2,1)}, bf16[4,2,2,72,1152]{4,3,2,1,0:T(8,128)(2,1)}, bf16[4,2,2,72,6144]{4,3,2,1,0:T(8,128)(2,1)}, bf16[4,2,...) custom-call(bf16[72,3456]{1,0:T(8,128)(2,1)} %refs_0_.1, ...), custom_call_target="tpu_custom_call" | custom-call | tf_op jit(solution)/shard_map/gather/pallas_call | solution.py:213
  380.7 4.7 fusion.158
  390.9 2.2 all_gather.13
  393.2 2.5 all-gather
  402.3 7.4 fusion.159
  409.8 5.6 fusion.160
  418.0 8.3 convolution_add_fusion
  438.1 2.4 all_gather.15
  440.6 14.1 %all-gather.1 = bf16[256,1152]{1,0:T(8,128)(2,1)} all-gather(bf16[128,1152]{1,0:T(8,128)(2,1)} %split.200), channel_id=3, replica_groups=mesh['dp'=16,'ctx'=2] {'ctx'}, dimensions={0}, use_global_device_ids=true | all-gather | bytes 884736 | tf_op jit(solution)/shard_map/all_gather | solution.py:705
  461.1 3.5 fusion.142
  465.3 2.2 fusion.162
  468.2 3.5 fusion.6
  474.5 10.1 multiply_reduce_fusion.7
  490.0 3.2 multiply_reduce_fusion.1
  496.8 2.2 multiply_convert_fusion.1
  506.8 3.2 fusion.215
  513.7 2.2 copy.157
  523.0 2.2 fusion.80
  527.9 2.3 copy.187
  535.1 2.6 pad_maximum_fusion.refs_18_
  559.6 6.0 convert_dynamic-update-slice_fusion.3
  568.2 12.7 %multiply_convert_fusion.10 = (bf16[128,1152]{1,0:T(8,128)(2,1)}, f32[128,1152]{1,0:T(8,128)}, bf16[1152,128]{0,1:T(8,128)(2,1)}) fusion(f32[128,6912]{1,0:T(8,128)} %copy-done.10, f32[128,1152]{1,0:T(8,128)S(1)} %copy-done.89, f32[128]{0:T(128)S(1)} %get-tuple-element.169, bf16[128,6912]{1,0:T(8,128)(2,1)S(1)} %fusion.90.refs_15_, ...), kind=kOutput, calls=%fused_computation.166 | convolution fusion | flops 2040496128 | bytes 20054528 | tf_op jit(solution)/shard_map/dot_general | solution.py:685
  580.9 6.6 fusion.9
  587.5 10.3 %multiply_reduce_fusion.6 = (f32[128]{0:T(128)S(1)}, f32[128,1152]{1,0:T(8,128)S(1)}) fusion(f32[128,1152]{1,0:T(8,128)S(1)} %get-tuple-element.62, f32[128]{0:T(128)S(1)} %copy-done.143, f32[128,6912]{1,0:T(8,128)S(1)} %copy-done.12, bf16[1152,6144]{1,0:T(8,128)(2,1)} %bitcast.323, bf16[128,3072]{1,0:T(8,128)(2,1)S(1)} %get-tuple-element.76, ...), kind=kOutput, calls=%fused_computation.165 | convolution fusion | flops 1815822208 | bytes 17499136 | tf_op jit(solution)/shard_map/dot_general | solution.py:685
  626.7 2.3 fusion.75
  644.1 2.3 fusion.47
  646.4 6.2 fusion.40
  661.8 341.6 %scatter.1 = (f32[72,36096]{1,0:T(8,128)}, bf16[16,16,1728]{2,1,0:T(8,128)(2,1)}) custom-call(bf16[16,80,128]{2,1,0:T(8,128)(2,1)} %pad_bitcast_fusion.6.refs_0_, bf16[16,80,128]{2,1,0:T(8,128)(2,1)} %pad_bitcast_fusion.5.refs_1_, bf16[16,80,128]{2,1,0:T(8,128)(2,1)} %pad_bitcast_fusion.4.refs_2_, bf16[16,80,128]{2,1,0:T(8,128)(2,1)} %pad_bitcast_fusion.3.refs_3_, ...), custom_call_target="tpu_custom_call" | custom-call | tf_op jit(solution)/shard_map/scatter/pallas_call | solution.py:575
  1005.0 4.1 fusion.147
  1009.1 2.9 fusion.149
  1012.0 3.0 slice.183
  (609 shorter events, 178.0 us)
Async XLA Ops:
  0.7 17.5 %copy-start = (bf16[72,6912]{1,0:T(8,128)(2,1)S(1)}, bf16[72,6912]{1,0:T(8,128)(2,1)}, u32[]{:S(2)}) copy-start(bf16[72,6912]{1,0:T(8,128)(2,1)} %param.28) | copy-start | bytes 2985988
  18.1 399.4 %copy-start.90 = (f32[64,576]{1,0:T(8,128)}, f32[64,576]{1,0:T(8,128)S(1)}, u32[]{:S(2)}) copy-start(f32[64,576]{1,0:T(8,128)S(1)} %get-tuple-element.148) | copy-start | bytes 442372
  18.1 399.4 %copy-start.92 = (f32[64,576]{1,0:T(8,128)}, f32[64,576]{1,0:T(8,128)S(1)}, u32[]{:S(2)}) copy-start(f32[64,576]{1,0:T(8,128)S(1)} %get-tuple-element.149) | copy-start | bytes 442372
  376.2 50.1 %copy-start.146 = (f32[128]{0:T(128)}, f32[128]{0:T(128)S(1)}, u32[]{:S(2)}) copy-start(f32[128]{0:T(128)S(1)} %fusion.126) | copy-start | bytes 1540
  376.3 41.2 %copy-start.144 = (s32[128]{0:T(128)}, s32[128]{0:T(128)S(1)}, u32[]{:S(2)}) copy-start(s32[128]{0:T(128)S(1)} %get-tuple-element.170) | copy-start | bytes 1540
  401.7 8.0 copy-start.142
  401.9 7.8 copy-start.157
  402.0 7.8 copy-start.150
  402.2 7.5 copy-start.77
  415.4 11.0 %copy-start.101 = (f32[128,1152]{1,0:T(8,128)}, f32[128,1152]{1,0:T(8,128)S(1)}, u32[]{:S(2)}) copy-start(f32[128,1152]{1,0:T(8,128)S(1)} %fusion.160) | copy-start | bytes 1769476
  418.0 8.4 copy-start.88
  418.0 9.4 slice-start.6
  418.0 9.4 slice-start.7
  437.2 19.6 %copy-start.86 = (bf16[128,16,2,2,18]{0,1,4,3,2:T(8,128)(2,1)}, bf16[128,16,2,2,18]{0,1,4,3,2:T(8,128)(2,1)S(1)}, u32[]{:S(2)}) copy-start(bf16[128,16,2,2,18]{0,1,4,3,2:T(8,128)(2,1)S(1)} %copy.139) | copy-start | bytes 884740
  437.2 28.0 %slice-start = ((s8[14155776]{0:T(1024)(128)(4,1)}), s8[1572864]{0:T(1024)(128)(4,1)S(1)}, s32[]{:S(2)}) async-start(s8[14155776]{0:T(1024)(128)(4,1)} %bitcast.325), calls=%async_computation | async-start | bytes 3145728
  440.6 16.8 %copy-start.62 = (bf16[1,256,1152]{1,2,0:T(8,128)(2,1)}, bf16[1,256,1152]{1,2,0:T(8,128)(2,1)S(1)}, u32[]{:S(2)}) copy-start(bf16[1,256,1152]{1,2,0:T(8,128)(2,1)S(1)} %all_gather.15) | copy-start | bytes 1769476
  456.8 8.4 slice-start.1
  464.6 20.0 %copy-start.13 = (f32[128,1152]{1,0:T(8,128)}, f32[128,1152]{1,0:T(8,128)S(1)}, u32[]{:S(2)}) copy-start(f32[128,1152]{1,0:T(8,128)S(1)} %get-tuple-element.60) | copy-start | bytes 1769476
  464.9 19.7 %copy-start.148 = (f32[128]{0:T(128)}, f32[128]{0:T(128)S(1)}, u32[]{:S(2)}) copy-start(f32[128]{0:T(128)S(1)} %fusion.128) | copy-start | bytes 1540
  473.0 11.7 %copy-start.55 = (f32[128,1152]{1,0:T(8,128)}, f32[128,1152]{1,0:T(8,128)S(1)}, u32[]{:S(2)}) copy-start(f32[128,1152]{1,0:T(8,128)S(1)} %fusion.163) | copy-start | bytes 1769476
  503.6 34.2 %collective-permute-start = (bf16[2,1,128,1152]{3,2,1,0:T(8,128)(2,1)}, bf16[2,1,128,1152]{3,2,1,0:T(8,128)(2,1)}, u32[]{:S(2)}, u32[]{:S(2)}) collective-permute-start(bf16[2,1,128,1152]{3,2,1,0:T(8,128)(2,1)} %fusion.51), channel_id=1, source_target_pairs={{0,1},{1,0},{2,3},{3,2},{4,5},{5,4},{6,7},{7,6},{8,9},{9,8},{10,11... | collective-permute-start | bytes 1769480 | tf_op jit(solution)/shard_map/ppermute | solution.py:801
  513.7 8.2 copy-start.54
  559.6 7.2 copy-start.26
  559.6 7.2 copy-start.41
  568.2 12.7 %copy-start.51 = (bf16[128,6912]{1,0:T(8,128)(2,1)}, bf16[128,6912]{1,0:T(8,128)(2,1)S(1)}, u32[]{:S(2)}) copy-start(bf16[128,6912]{1,0:T(8,128)(2,1)S(1)} %fusion.90.refs_15_) | copy-start | bytes 5308420
  587.5 10.4 %copy-start.73 = (bf16[128,3072]{1,0:T(8,128)(2,1)}, bf16[128,3072]{1,0:T(8,128)(2,1)S(1)}, u32[]{:S(2)}) copy-start(bf16[128,3072]{1,0:T(8,128)(2,1)S(1)} %get-tuple-element.75) | copy-start | bytes 2359300
  587.5 10.4 %copy-start.75 = (bf16[128,3072]{1,0:T(8,128)(2,1)}, bf16[128,3072]{1,0:T(8,128)(2,1)S(1)}, u32[]{:S(2)}) copy-start(bf16[128,3072]{1,0:T(8,128)(2,1)S(1)} %get-tuple-element.76) | copy-start | bytes 2359300
  587.5 10.4 %copy-start.158 = (f32[128]{0:T(128)S(1)}, f32[128]{0:T(128)}, u32[]{:S(2)}) copy-start(f32[128]{0:T(128)} %copy-done.157) | copy-start | bytes 1540
  587.5 10.4 %copy-start.151 = (f32[128]{0:T(128)S(1)}, f32[128]{0:T(128)}, u32[]{:S(2)}) copy-start(f32[128]{0:T(128)} %copy-done.150) | copy-start | bytes 1540
  618.0 6.1 collective-permute-start.1
  656.4 4.6 collective-permute-start.2
  1019.1 7.9 copy-start.1
  (141 other events, 413.6 us)

commit v3 on v2

--- a/solution.py
+++ b/solution.py
@@ -836,11 +836,420 @@
     return (grad_flat, grad_modulation, factors, gains_grad)
 
 
-def shard_rows(values, groups):
-    turned = values.T.reshape(16, groups, -1, values.shape[0])
-    rows = turned.shape[2]
-    turned = jnp.pad(turned, ((0, 0), (0, 0), (0, PADDED - rows), (0, 0)))
-    return [turned[:, g] for g in range(groups)]
+def meet_sibling():
+    barrier = pltpu.get_barrier_semaphore()
+    sibling = (lax.axis_index("dp"), 1 - lax.axis_index("ctx"))
+    pl.semaphore_signal(barrier, inc=1, device_id=sibling, device_id_type=MESH)
+    pl.semaphore_wait(barrier, 1)
+    return sibling
+
+
+def head_sum_matrix(width):
+    channel = lax.broadcasted_iota(jnp.int32, (width, 128), 0)
+    head = lax.broadcasted_iota(jnp.int32, (width, 128), 1)
+    inside = (channel >= head * HD) & (channel < (head + 1) * HD)
+    return jnp.where(inside, 1.0, 0.0).astype(F32)
+
+
+def exact_dot(left, right):
+    return jnp.dot(left, right, preferred_element_type=F32, precision=lax.Precision.HIGHEST)
+
+
+def spread_heads(values, heads):
+    return lax.dot_general(
+        values,
+        heads,
+        (((1,), (1,)), ((), ())),
+        preferred_element_type=F32,
+        precision=lax.Precision.HIGHEST,
+    )
+
+
+def swap_pairs(values):
+    width = values.shape[1]
+    lane = lax.broadcasted_iota(jnp.int32, values.shape, 1)
+    quarter = HD // 4
+    early = lax.rem(lane, 2 * quarter) < quarter
+    return jnp.where(
+        early, pltpu.roll(values, width - quarter, 1), pltpu.roll(values, quarter, 1)
+    )
+
+
+def normalize(values):
+    mean = jnp.mean(values, axis=1, keepdims=True)
+    center = values - mean
+    spread = jnp.mean(center * center, axis=1, keepdims=True)
+    inverse = lax.rsqrt(spread + 1e-06)
+    return center * inverse, inverse
+
+
+def norm_back(normed, inverse, grad):
+    mean = jnp.mean(grad, axis=1, keepdims=True)
+    along = jnp.mean(grad * normed, axis=1, keepdims=True)
+    return (grad - mean - normed * along) * inverse
+
+
+def window(h, width):
+    first = min((h * HD) // 128 * 128, width - 256)
+    return first, h * HD - first
+
+
+def head_mask(h, width, rows):
+    first, at = window(h, width)
+    lane = lax.broadcasted_iota(jnp.int32, (rows, 256), 1)
+    return (lane >= at) & (lane < at + HD)
+
+
+def turned(values):
+    tokens, width = values.shape
+    rows = values.T.reshape(-1, ROWS, tokens)
+    return jnp.concatenate(
+        [rows, jnp.zeros((width // ROWS, PADDED - ROWS, tokens), F32)], axis=1
+    ).astype(BF16)
+
+
+FF_TILE = 768
+KV_TILE = 1152
+
+
+def allowed_mask(seg_q, seg_k, pad_k, half):
+    place_q = lax.axis_index("ctx") * half + lax.broadcasted_iota(jnp.int32, (half, 2 * half), 0)
+    place_k = lax.broadcasted_iota(jnp.int32, (half, 2 * half), 1)
+    return (seg_q[...] == seg_k[...]) & ((pad_k[...] == 0) | (place_q == place_k))
+
+
+def forward_kernel(
+    flat, mod, gains, cosine, sine, seg_q, seg_k, pad_k, triple_h, mixing_h, expand_h, reduce_h,
+    output, raw, queries, kv, lse, attended, resid, expanded, feed, xt1, xtm, xt2, xth,
+    triple, mixing, expand, reduce_w, mixed, wsem, ssem, rsem,
+):
+    half, width = flat.shape
+    loads = [
+        pltpu.make_async_copy(src, dst, wsem.at[k])
+        for k, (src, dst) in enumerate(
+            ((triple_h, triple), (mixing_h, mixing), (expand_h, expand), (reduce_h, reduce_w))
+        )
+    ]
+    for load in loads:
+        load.start()
+    sibling = meet_sibling()
+    c = lax.axis_index("ctx")
+    mine = pl.ds(pl.multiple_of(c * half, 128), half)
+
+    def part(k):
+        return mod[:, k * width : (k + 1) * width]
+
+    normed, unused = normalize(flat[...])
+    lifted = normed * (1.0 + part(1)) + part(0)
+    lifted_low = lifted.astype(BF16)
+    xt1[...] = turned(lifted_low.astype(F32))
+    heads = head_sum_matrix(width)
+    loads[0].wait()
+
+    def prepared(k):
+        values = raw[:, k * width : (k + 1) * width]
+        mean = exact_dot(values * values, heads) * (1.0 / HD)
+        scaled = values * spread_heads(lax.rsqrt(mean + 1e-06), heads) * gains[k : k + 1, :]
+        return scaled * cosine[...] + swap_pairs(scaled) * sine[...]
+
+    def project(k):
+        return jnp.dot(
+            lifted_low, triple[:, k * width : (k + 1) * width], preferred_element_type=F32
+        )
+
+    raw[:, width:] = project(1)
+    kv[0, mine] = prepared(1).astype(BF16)
+    kv[1, mine] = project(2).astype(BF16)
+    share = pltpu.make_async_remote_copy(
+        kv.at[:, mine], kv.at[:, mine], ssem.at[0], rsem.at[0], device_id=sibling,
+        device_id_type=MESH,
+    )
+    share.start()
+    raw[:, :width] = project(0)
+    queries[...] = prepared(0).astype(BF16)
+    allowed = allowed_mask(seg_q, seg_k, pad_k, half)
+    mixed[...] = jnp.zeros_like(mixed)
+    lane = lax.broadcasted_iota(jnp.int32, (half, 128), 1)
+    sums = jnp.zeros((half, 128), F32)
+    theirs = pl.ds(pl.multiple_of((1 - c) * half, 128), half)
+    pltpu.make_async_remote_copy(
+        kv.at[:, theirs], kv.at[:, theirs], ssem.at[0], rsem.at[0], device_id=sibling,
+        device_id_type=MESH,
+    ).wait_recv()
+    for h in range(width // HD):
+        first, unused = window(h, width)
+        span = slice(first, first + 256)
+        mask = head_mask(h, width, half)
+        query = jnp.where(mask, queries[:, span].astype(F32), 0.0).astype(BF16)
+        scores = dense_back(query, kv[0, :, span]) * (1.0 / math.sqrt(HD))
+        scores = jnp.where(allowed, scores, -1e30)
+        top = jnp.max(scores, axis=1, keepdims=True)
+        raised = jnp.exp(scores - top)
+        total = jnp.sum(raised, axis=1, keepdims=True)
+        low = (raised / total).astype(BF16)
+        out = jnp.dot(low, kv[1, :, span], preferred_element_type=F32)
+        mixed[:, span] = mixed[:, span] + jnp.where(mask, out, 0.0)
+        sums = jnp.where(lane == h, top + jnp.log(total), sums)
+    lse[...] = sums
+    mixed_low = mixed[...].astype(BF16)
+    xtm[...] = turned(mixed_low.astype(F32))
+    loads[1].wait()
+    attended[...] = jnp.dot(mixed_low, mixing[...], preferred_element_type=F32)
+    resid[...] = flat[...] + part(2) * attended[...]
+    normed, unused = normalize(resid[...])
+    lifted_low = (normed * (1.0 + part(4)) + part(3)).astype(BF16)
+    xt2[...] = turned(lifted_low.astype(F32))
+    feed[...] = jnp.zeros_like(feed)
+    loads[2].wait()
+    loads[3].wait()
+    hidden_size = reduce_w.shape[0]
+    xth[...] = jnp.zeros_like(xth)
+    for t in range(hidden_size // FF_TILE):
+        gate = jnp.dot(
+            lifted_low, expand[:, t * FF_TILE : (t + 1) * FF_TILE], preferred_element_type=F32
+        )
+        up = jnp.dot(
+            lifted_low,
+            expand[:, hidden_size + t * FF_TILE : hidden_size + (t + 1) * FF_TILE],
+            preferred_element_type=F32,
+        )
+        expanded[:, t * FF_TILE : (t + 1) * FF_TILE] = gate
+        expanded[:, hidden_size + t * FF_TILE : hidden_size + (t + 1) * FF_TILE] = up
+        hidden = (gate * jax.nn.sigmoid(gate) * up).astype(BF16)
+        pieces = hidden.astype(F32).T.astype(BF16).reshape(FF_TILE // 192, 3, 64, half)
+        for g in range(3):
+            xth[g, t * (FF_TILE // 192) : (t + 1) * (FF_TILE // 192), :64] = pieces[:, g]
+        feed[...] = feed[...] + jnp.dot(
+            hidden, reduce_w[t * FF_TILE : (t + 1) * FF_TILE], preferred_element_type=F32
+        )
+    output[...] = resid[...] + part(5) * feed[...]
+    share.wait_send()
+
+
+def backward_kernel(
+    grad_out, flat, mod, gains, cosine, sine, seg_q, seg_k, pad_k,
+    raw, queries, kv, lse, attended, resid, expanded, feed,
+    triple_h, mixing_h, expand_h, reduce_h,
+    grad_flat, grad_mod, grad_feed, grad_expanded, grad_attended, grad_projected, gains_grad,
+    triple, mixing, expand, reduce_w, grad_q, grad_k, grad_v, lift, outgoing, incoming,
+    wsem, ssem, rsem,
+):
+    half, width = flat.shape
+    loads = [
+        pltpu.make_async_copy(src, dst, wsem.at[k])
+        for k, (src, dst) in enumerate(
+            ((reduce_h, reduce_w), (expand_h, expand), (mixing_h, mixing), (triple_h, triple))
+        )
+    ]
+    for load in loads:
+        load.start()
+    sibling = meet_sibling()
+    c = lax.axis_index("ctx")
+    mine = pl.ds(pl.multiple_of(c * half, 128), half)
+    theirs = pl.ds(pl.multiple_of((1 - c) * half, 128), half)
+
+    def part(k):
+        return mod[:, k * width : (k + 1) * width]
+
+    def keep(k, values):
+        grad_mod[:, k * width : (k + 1) * width] = values.astype(BF16)
+
+    keep(5, grad_out[...] * feed[...])
+    feed_low = (grad_out[...] * part(5)).astype(BF16)
+    grad_feed[...] = feed_low
+    hidden_size = reduce_w.shape[0]
+    lift[...] = jnp.zeros_like(lift)
+    loads[0].wait()
+    loads[1].wait()
+    for t in range(hidden_size // FF_TILE):
+        one = slice(t * FF_TILE, (t + 1) * FF_TILE)
+        two = slice(hidden_size + t * FF_TILE, hidden_size + (t + 1) * FF_TILE)
+        grad_hidden = dense_back(feed_low, reduce_w[one])
+        gate = expanded[:, one]
+        up = expanded[:, two]
+        sig = jax.nn.sigmoid(gate)
+        grad_gate = (grad_hidden * up * (sig * (1.0 + gate * (1.0 - sig)))).astype(BF16)
+        grad_up = (grad_hidden * (gate * sig)).astype(BF16)
+        grad_expanded[:, one] = grad_gate
+        grad_expanded[:, two] = grad_up
+        lift[...] = lift[...] + dense_back(grad_gate, expand[:, one])
+        lift[...] = lift[...] + dense_back(grad_up, expand[:, two])
+    normed, inverse = normalize(resid[...])
+    keep(3, lift[...])
+    keep(4, lift[...] * normed)
+    grad_resid = grad_out[...] + norm_back(normed, inverse, lift[...] * (1.0 + part(4)))
+    keep(2, grad_resid * attended[...])
+    grad_flat[...] = grad_resid
+    attended_low = (grad_resid * part(2)).astype(BF16)
+    grad_attended[...] = attended_low
+    loads[2].wait()
+    lift[...] = dense_back(attended_low, mixing[...])
+    allowed = allowed_mask(seg_q, seg_k, pad_k, half)
+    grad_q[...] = jnp.zeros_like(grad_q)
+    grad_k[...] = jnp.zeros_like(grad_k)
+    grad_v[...] = jnp.zeros_like(grad_v)
+    scale = 1.0 / math.sqrt(HD)
+    lane = lax.broadcasted_iota(jnp.int32, (half, 128), 1)
+    for h in range(width // HD):
+        first, unused = window(h, width)
+        span = slice(first, first + 256)
+        mask = head_mask(h, width, half)
+        query = jnp.where(mask, queries[:, span].astype(F32), 0.0).astype(BF16)
+        grad_mixed = jnp.where(mask, lift[:, span], 0.0).astype(BF16)
+        scores = dense_back(query, kv[0, :, span]) * scale
+        logsum = jnp.sum(jnp.where(lane == h, lse[...], 0.0), axis=1, keepdims=True)
+        chances = jnp.exp(jnp.where(allowed, scores, -1e30) - logsum)
+        grad_chances = dense_back(grad_mixed, kv[1, :, span])
+        along = jnp.sum(chances * grad_chances, axis=1, keepdims=True)
+        grad_scores = chances * (grad_chances - along)
+        scores_low = grad_scores.astype(BF16)
+        out = jnp.dot(scores_low, kv[0, :, span], preferred_element_type=F32)
+        grad_q[:, span] = grad_q[:, span] + jnp.where(mask, out, 0.0)
+        grad_k[:, span] = grad_k[:, span] + outer_sum(scores_low, query)
+        grad_v[:, span] = grad_v[:, span] + outer_sum(chances.astype(BF16), grad_mixed)
+    outgoing[0] = (grad_k[theirs, :] * scale).astype(BF16)
+    outgoing[1] = grad_v[theirs, :].astype(BF16)
+    share = pltpu.make_async_remote_copy(
+        outgoing, incoming, ssem.at[0], rsem.at[0], device_id=sibling, device_id_type=MESH
+    )
+    share.start()
+    heads = head_sum_matrix(width)
+
+    def prepare_back(k, grad):
+        values = raw[:, k * width : (k + 1) * width]
+        gain = gains[k : k + 1, :]
+        mean = exact_dot(values * values, heads) * (1.0 / HD)
+        inverse = spread_heads(lax.rsqrt(mean + 1e-06), heads)
+        scaled = values * inverse
+        turned_back = grad * cosine[...] + swap_pairs(grad * sine[...])
+        gains_grad[k : k + 1, :] = jnp.sum(turned_back * scaled, axis=0, keepdims=True)
+        turned_back = turned_back * gain
+        along = spread_heads(exact_dot(turned_back * scaled, heads) * (1.0 / HD), heads)
+        return (turned_back - scaled * along) * inverse
+
+    grad_projected[:, :width] = prepare_back(0, grad_q[...] * scale).astype(BF16)
+    share.wait()
+    own_k = (grad_k[mine, :] * scale).astype(BF16).astype(F32) + incoming[0].astype(F32)
+    own_v = grad_v[mine, :].astype(BF16).astype(F32) + incoming[1].astype(F32)
+    grad_projected[:, width : 2 * width] = prepare_back(1, own_k).astype(BF16)
+    grad_projected[:, 2 * width :] = own_v.astype(BF16)
+    loads[3].wait()
+    total = dense_back(grad_projected[:, :width], triple[:, :width])
+    for k in (1, 2):
+        span = slice(k * width, (k + 1) * width)
+        total = total + dense_back(grad_projected[:, span], triple[:, span])
+    normed, inverse = normalize(flat[...])
+    keep(0, total)
+    keep(1, total * normed)
+    grad_flat[...] = grad_flat[...] + norm_back(normed, inverse, total * (1.0 + part(1)))
+
+
+IN_VMEM = pl.BlockSpec(memory_space=pltpu.VMEM)
+
+
+def weight_scratch(weights):
+    return [pltpu.VMEM(w.shape, w.dtype) for w in weights]
+
+
+def kernel_forward(flat, modulation, weights, context, name):
+    cosine, sine, seg_q, seg_k, pad_k = context
+    *weights, gains = weights
+    half, width = flat.shape
+    hidden_size = weights[3].shape[0]
+
+    def struct(shape, dtype=F32):
+        return jax.ShapeDtypeStruct(shape, dtype)
+
+    rows = (16, PADDED, half)
+    out_shape = [
+        struct((half, width)),
+        struct((half, 2 * width)),
+        struct((half, width), BF16),
+        struct((2, 2 * half, width), BF16),
+        struct((half, 128)),
+        struct((half, width)),
+        struct((half, width)),
+        struct((half, 2 * hidden_size)),
+        struct((half, width)),
+        struct(rows, BF16),
+        struct(rows, BF16),
+        struct(rows, BF16),
+        struct((3,) + rows, BF16),
+    ]
+    output, *rest = pl.pallas_call(
+        forward_kernel,
+        name=name,
+        out_shape=out_shape,
+        in_specs=[IN_VMEM] * 8 + [ANY] * 4,
+        out_specs=[IN_VMEM] * len(out_shape),
+        scratch_shapes=weight_scratch(weights)
+        + [pltpu.VMEM((half, width), F32), DMA((4,)), DMA((1,)), DMA((1,))],
+        compiler_params=pltpu.CompilerParams(
+            collective_id=5, has_side_effects=True, vmem_limit_bytes=60 * 1024 * 1024
+        ),
+    )(flat, modulation, gains, cosine, sine, seg_q, seg_k, pad_k, *weights)
+    return output, (flat, modulation, rest[:8]), rest[8:]
+
+
+def kernel_backward(grad_out, kept, weights, context, name):
+    cosine, sine, seg_q, seg_k, pad_k = context
+    flat, modulation, saved = kept
+    *weights, gains = weights
+    half, width = flat.shape
+    hidden_size = weights[3].shape[0]
+
+    def struct(columns, dtype=BF16):
+        return jax.ShapeDtypeStruct((half, columns), dtype)
+
+    out_shape = [
+        struct(width, F32),
+        struct(6 * width),
+        struct(width),
+        struct(2 * hidden_size),
+        struct(width),
+        struct(3 * width),
+        jax.ShapeDtypeStruct((2, width), F32),
+    ]
+    vmem = pltpu.VMEM
+    return pl.pallas_call(
+        backward_kernel,
+        name=name,
+        out_shape=out_shape,
+        in_specs=[IN_VMEM] * 17 + [ANY] * 4,
+        out_specs=[IN_VMEM] * len(out_shape),
+        scratch_shapes=weight_scratch(weights)
+        + [
+            vmem((half, width), F32),
+            vmem((2 * half, width), F32),
+            vmem((2 * half, width), F32),
+            vmem((half, width), F32),
+            vmem((2, half, width), BF16),
+            vmem((2, half, width), BF16),
+            DMA((4,)),
+            DMA((1,)),
+            DMA((1,)),
+        ],
+        compiler_params=pltpu.CompilerParams(
+            collective_id=6, has_side_effects=True, vmem_limit_bytes=60 * 1024 * 1024
+        ),
+    )(
+        grad_out, flat, modulation, gains, cosine, sine, seg_q, seg_k, pad_k, *saved, *weights
+    )
+
+
+def shard_rows(values):
+    rows = values.T.reshape(16, -1, values.shape[0])
+    return jnp.pad(rows, ((0, 0), (0, PADDED - rows.shape[1]), (0, 0)))
+
+
+def rope_lanes(cosine, sine):
+    tokens = cosine.shape[0]
+
+    def lanes(table, signs):
+        table = jnp.stack([signs[0] * table, signs[1] * table], axis=2).reshape(tokens, 1, HD)
+        return jnp.broadcast_to(table, (tokens, HEADS, HD)).reshape(tokens, HEADS * HD)
+
+    return lanes(cosine, (1.0, 1.0)), lanes(sine, (-1.0, 1.0))
 
 
 def fast_reduce(blocks, rows, collective_id, name):
@@ -848,12 +1257,11 @@
     dys = []
     source = []
     for factors, extra in blocks:
-        for k, (left, right) in enumerate(factors):
-            groups = 3 if k == len(factors) - 1 else 1
-            source += [len(dys)] * groups
-            xts += shard_rows(left, groups)
+        for lefts, right in factors:
+            source += [len(dys)] * len(lefts)
+            xts += lefts
             dys.append(right)
-        tokens = left.shape[0]
+        tokens = right.shape[0]
         lines = -(-extra.shape[1] // tokens)
         packed = jnp.pad(extra, ((0, 0), (0, lines * tokens - extra.shape[1])))
         packed = packed.reshape(16, lines, tokens).astype(BF16)
@@ -865,12 +1273,11 @@
     at = 0
     for factors, extra in blocks:
         grads = []
-        for left, right in factors[:-1]:
+        for lefts, right in factors[:-1]:
             grads.append(out[:, at : at + right.shape[1]])
             at += right.shape[1]
         width = factors[-1][1].shape[1]
-        count = factors[-1][0].shape[1] // 48
-        parts = [out[:count, at + g * width : at + (g + 1) * width] for g in range(3)]
+        parts = [out[:64, at + g * width : at + (g + 1) * width] for g in range(3)]
         grads.append(jnp.concatenate(parts, axis=0))
         at += 3 * width
         lines = -(-extra.shape[1] // tokens)
@@ -931,19 +1338,34 @@
     cond_rows = lax.dynamic_slice_in_dim(all_cond, me * segments, segments, 0)
     cond = jnp.dot(picks, cond_rows, precision=exact)
 
-    encoder_out, encoder_kept = block_forward(flat, encoder_modulation, encoder_weights, context)
+    encoder_out, encoder_kept, encoder_left = kernel_forward(
+        flat, encoder_modulation, encoder_weights, context, "encoder"
+    )
     latent_full = valid * encoder_out
     decoder_pre = latent_full + cond
     decoder_act = jax.nn.silu(decoder_pre).astype(BF16)
 
     decoder_modulation = dense(decoder_act, modulate) + decoder_offset
-    decoder_out, decoder_kept = block_forward(flat, decoder_modulation, decoder_weights, context)
+    decoder_out, decoder_kept, decoder_left = kernel_forward(
+        flat, decoder_modulation, decoder_weights, context, "decoder"
+    )
     velocity = valid * decoder_out
 
+    def pair_up(lefts, rights):
+        feed, expanded, attended, projected = rights
+        one, mixed, two, hidden = lefts
+        return (
+            ([one], projected),
+            ([mixed], attended),
+            ([two], expanded),
+            ([hidden[g] for g in range(3)], feed),
+        )
+
     grad_out = valid * cotangent
-    decoder_flat, grad_modulation, factors, gains_grad = block_backward(
-        grad_out, decoder_kept, decoder_weights, context
-    )
+    decoder_flat, grad_modulation, *rights, gains_grad = kernel_backward(
+        grad_out, decoder_kept, decoder_weights, context, "decoder_back"
+    )
+    factors = pair_up(decoder_left, rights)
     grad_act = dense_back(grad_modulation, modulate)
     unused_silu, silu_pull = jax.vjp(jax.nn.silu, decoder_pre)
     grad_latent = valid * silu_pull(grad_act)[0]
@@ -955,11 +1377,13 @@
         ],
         axis=1,
     )
-    decoder_block = (((decoder_act, grad_modulation),) + factors, extra)
-
-    encoder_flat, grad_modulation, factors, gains_grad = block_backward(
-        grad_latent, encoder_kept, encoder_weights, context
-    )
+    first = ([shard_rows(decoder_act)], grad_modulation)
+    decoder_block = ((first,) + factors, extra)
+
+    encoder_flat, grad_modulation, *rights, gains_grad = kernel_backward(
+        grad_latent, encoder_kept, encoder_weights, context, "encoder_back"
+    )
+    factors = pair_up(encoder_left, rights)
     grad_rows = lax.dot_general(
         picks.astype(BF16), grad_modulation, (((0,), (0,)), ((), ())), preferred_element_type=F32
     )
@@ -1061,6 +1485,9 @@
     )
     cosine, sine = rope_tables(rows_local.reshape(-1), columns_local.reshape(-1))
     context = (batch, half, allowed, cosine, sine)
+    if fast:
+        context = rope_lanes(cosine, sine)
+        context += (segment_local.reshape(-1, 1), segment, padding)
     valid = (1 - padding_local).astype(F32).reshape(-1, 1)
     flat = tokens.reshape(-1, width).astype(F32)
     step = fast_step if fast else plain_step

time: 1030 us -> 914 us (0.89)
  Pallas kernels: 705 us -> 826 us
  matrix products: 115 us -> 31.3 us
  local copies, waits for them, and re-layouts: 122 us -> 39.3 us
  other arithmetic: 60.3 us -> 10 us
  blocking collectives: 21.2 us -> 0 us
    pallas_call x0 -> x4, Pallas kernels: none -> 122 us  [the longest x2 72.4 us: kernel_backward(): pl.pallas_call(backward_kernel, name=name, out_shape=out_shape, in_specs=...]
    dot_general x9 -> x1, matrix products: 58.6 us -> 12.2 us  [dense_back(): lax.dot_general(grads, weight, (((1,), (1,)), ((), ())), preferred_elemen...]
    dot_general x10 -> x2, matrix products: 36.3 us -> 10.5 us  [dense(): return jnp.dot(values, weight, preferred_element_type=F32)]
    all_gather x4 -> x0, blocking collectives: 21.2 us -> none  [the longest x2 16.6 us: block_forward(): value_heads = lax.all_gather(values_local, 'ctx', axis=1, tiled=True)]
    unnamed x341 -> x29, local copies, waits for them, and re-layouts: 20.8 us -> 1.02 us
    dot_general x12 -> x0, matrix products: 15.5 us -> none  [the longest x2 5.23 us: block_backward(): jnp.einsum('sqhd,skhd->shqk', grad_mixed, value_heads, preferred_element_...]
    mul x20 -> x0, local copies, waits for them, and re-layouts: 15 us -> none  [the longest x8 10.1 us: head_norm(): shaped * lax.rsqrt(jnp.mean(shaped * shaped, axis=-1, keepdims=True) + 1e...]
    reduce_sum x21 -> x0, other arithmetic: 13.1 us -> none  [the longest x4 5.82 us: head_norm(): shaped * lax.rsqrt(jnp.mean(shaped * shaped, axis=-1, keepdims=True) + 1e...]
  transfers between devices with their start and end apart: 3 -> 1, of which waited for: 0 -> 0; matrix products, arithmetic and copies ran while one was open for 4% -> 1% of each run, Pallas kernels for 0% -> 0%
where the time goes in v3:
time: 914 us; the launch traced here: 908 us
  Pallas kernels  826 us (90%)
  local copies, waits for them, and re-layouts  39.3 us (4%)
  matrix products  31.3 us (3%)
  other arithmetic  10 us (1%)
    pallas_call x1, Pallas kernels, gather(): pl.pallas_call(functools.partial(gather_kernel, units, count, stride, gro...  353 us
    pallas_call x1, Pallas kernels, scatter(): pl.pallas_call(functools.partial(scatter_kernel, tuple(first), tuple(cols...  340 us
    pallas_call x2, Pallas kernels, kernel_backward(): pl.pallas_call(backward_kernel, name=name, out_shape=out_shape, in_specs=...  72.4 us
    pallas_call x2, Pallas kernels, kernel_forward(): pl.pallas_call(forward_kernel, name=name, out_shape=out_shape, in_specs=[...  49.9 us
  transfers between devices with their start and end apart: 1, of which 0 were waited for; matrix products, arithmetic and copies ran while one was open for 1% of the time, Pallas kernels for 0%

profile of v3, /device:TPU:0, one launch (start us, length us, event | category | flops | bytes accessed | tf_op | source)
XLA Modules:
  0.0 908.4 jit_solution(10996680957654807335)
XLA Ops:
  2.9 1.5 concatenate.21
  5.0 10.7 %small.1 = f32[16,16,128]{2,1,0:T(8,128)} custom-call(f32[16,128]{1,0:T(8,128)} %pad_bitcast_fusion.in_ref), custom_call_target="tpu_custom_call" | custom-call | tf_op jit(solution)/shard_map/small/pallas_call | solution.py:255
  15.7 0.9 copy.69
  17.7 1.1 copy.50.sine
  20.0 1.5 reshape.317.refs_9_
  21.7 352.8 %gather.1 = (bf16[4,2,2,72,3456]{4,3,2,1,0:T(8,128)(2,1)}, bf16[4,2,2,72,1152]{4,3,2,1,0:T(8,128)(2,1)}, bf16[4,2,2,72,6144]{4,3,2,1,0:T(8,128)(2,1)}, bf16[4,2,...) custom-call(bf16[72,3456]{1,0:T(8,128)(2,1)} %refs_0_.1, ...), custom_call_target="tpu_custom_call" | custom-call | tf_op jit(solution)/shard_map/gather/pallas_call | solution.py:213
  374.5 1.6 reduce_sum.27
  376.3 1.1 copy.49.cosine
  378.9 0.9 bitcast_convert_fusion.flat
  380.7 3.4 fusion.17.mod
  384.1 0.9 convert_multiply_fusion.grad_out
  385.0 24.9 %encoder.1 = (f32[128,1152]{1,0:T(8,128)}, f32[128,2304]{1,0:T(8,128)}, bf16[128,1152]{1,0:T(8,128)(2,1)}, bf16[2,256,1152]{2,1,0:T(8,128)(2,1)}, f32[128,128]{1...) custom-call(f32[128,1152]{1,0:T(8,128)} %bitcast_convert_fusion.flat, ...), custom_call_target="tpu_custom_call" | custom-call | tf_op jit(solution)/shard_map/encoder/pallas_call | solution.py:1179
  409.9 1.5 convolution_add_fusion.1
  411.4 10.0 %convolution_add_fusion.mod = f32[128,6912]{1,0:T(8,128)} fusion(bf16[1152,6912]{1,0:T(8,128)(2,1)} %bitcast.83, f32[6912]{0:T(1024)S(1)} %add.88, f32[128,1152]{1,0:T(8,128)S(1)} %convolution_add_fusion.1), kind=kOutput, calls=%fused_computation | convolution fusion | flops 2040053760 | bytes 20081664 | tf_op jit(solution)/shard_map/dot_general | solution.py:681
  421.4 25.0 %decoder.1 = (f32[128,1152]{1,0:T(8,128)}, f32[128,2304]{1,0:T(8,128)}, bf16[128,1152]{1,0:T(8,128)(2,1)}, bf16[2,256,1152]{2,1,0:T(8,128)(2,1)}, f32[128,128]{1...) custom-call(f32[128,1152]{1,0:T(8,128)} %bitcast_convert_fusion.flat, ...), custom_call_target="tpu_custom_call" | custom-call | tf_op jit(solution)/shard_map/decoder/pallas_call | solution.py:1179
  446.5 36.1 %decoder_back.1 = (f32[128,1152]{1,0:T(8,128)}, bf16[128,6912]{1,0:T(8,128)(2,1)}, bf16[128,1152]{1,0:T(8,128)(2,1)}, bf16[128,6144]{1,0:T(8,128)(2,1)}, bf16[12...) custom-call(f32[128,1152]{1,0:T(8,128)} %convert_multiply_fusion.grad_out, ...), custom_call_target="tpu_custom_call" | custom-call | tf_op jit(solution)/shard_map/decoder_back/pallas_call | solution.py:1214
  482.6 12.2 %fusion.30 = (bf16[1152,128]{0,1:T(8,128)(2,1)S(1)}, f32[128,1152]{1,0:T(8,128)}, bf16[1,128,1152]{2,1,0:T(8,128)(2,1)}, bf16[1,128,1152]{2,1,0:T(8,128)(2,1)}) fusion(f32[128,1152]{1,0:T(8,128)S(1)} %convolution_add_fusion.1, f32[128]{0:T(128)S(1)} %fusion.22, f32[128,1152]{1,0:T(8,128)S(1)} %copy-done.5, f32[128,1152]{1,0:T(8,128)S(1)} %copy-done.3, ...), kind=kOutput, calls=%fused_computation.79 | convolution fusion | flops 2040791040 | bytes 20939264 | tf_op jit(solution)/shard_map/dot_general | solution.py:685
  494.8 36.3 %encoder_back.1 = (f32[128,1152]{1,0:T(8,128)}, bf16[128,6912]{1,0:T(8,128)(2,1)}, bf16[128,1152]{1,0:T(8,128)(2,1)}, bf16[128,6144]{1,0:T(8,128)(2,1)}, bf16[12...) custom-call(f32[128,1152]{1,0:T(8,128)} %get-tuple-element.140.grad_out, ...), custom_call_target="tpu_custom_call" | custom-call | tf_op jit(solution)/shard_map/encoder_back/pallas_call | solution.py:1214
  531.1 1.9 fusion.8
  536.8 2.1 slice_bitcast_fusion.3
  539.0 2.1 slice_bitcast_fusion
  541.1 0.9 add_bitcast_fusion
  543.4 340.3 %scatter.1 = (f32[72,36096]{1,0:T(8,128)}, bf16[16,16,1728]{2,1,0:T(8,128)(2,1)}) custom-call(bf16[16,80,128]{2,1,0:T(8,128)(2,1)} %pad.27.refs_0_, bf16[16,80,128]{2,1,0:T(8,128)(2,1)} %get-tuple-element.100.refs_1_, bf16[16,80,128]{2,1,0:T(8,128)(2,1)} %get-tuple-element.101.refs_2_, bf16[16,80,128]{2,1,0:T(8,128)(2,1)} %get-tuple-element.102.refs_3_, ...), custom_call_target="tpu_custom_call" | custom-call | tf_op jit(solution)/shard_map/scatter/pallas_call | solution.py:575
  883.7 2.4 fusion.31
  886.0 4.1 fusion.32
  890.1 3.0 fusion.34
  893.1 3.0 slice.109
  896.1 1.0 reshape.344
  897.1 1.8 fusion.29
  899.1 2.0 fusion.33
  905.0 2.0 pad_maximum_fusion.1
  907.0 1.0 pad_maximum_fusion
  (95 shorter events, 17.2 us)
Async XLA Ops:
  0.7 18.9 %copy-start = (bf16[72,6912]{1,0:T(8,128)(2,1)S(1)}, bf16[72,6912]{1,0:T(8,128)(2,1)}, u32[]{:S(2)}) copy-start(bf16[72,6912]{1,0:T(8,128)(2,1)} %param.28) | copy-start | bytes 2985988
  21.7 354.5 %copy-start.10 = (s32[1,256]{1,0:T(1,128)S(1)}, s32[1,256]{1,0:T(1,128)}, u32[]{:S(2)}) copy-start(s32[1,256]{1,0:T(1,128)} %seg_k.7) | copy-start | bytes 3076
  374.5 4.4 copy-start.8
  374.5 5.3 copy-start.11
  376.3 7.7 copy-start.9
  446.4 36.2 %copy-start.3 = (f32[128,1152]{1,0:T(8,128)S(1)}, f32[128,1152]{1,0:T(8,128)}, u32[]{:S(2)}) copy-start(f32[128,1152]{1,0:T(8,128)} %get-tuple-element.74) | copy-start | bytes 1769476
  446.4 36.2 %copy-start.5 = (f32[128,1152]{1,0:T(8,128)S(1)}, f32[128,1152]{1,0:T(8,128)}, u32[]{:S(2)}) copy-start(f32[128,1152]{1,0:T(8,128)} %get-tuple-element.80) | copy-start | bytes 1769476
  494.8 38.6 %copy-start.2 = (bf16[128,6912]{1,0:T(8,128)(2,1)S(1)}, bf16[128,6912]{1,0:T(8,128)(2,1)}, u32[]{:S(2)}) copy-start(bf16[128,6912]{1,0:T(8,128)(2,1)} %get-tuple-element.90.refs_15_) | copy-start | bytes 5308420
  531.0 2.7 copy-start.12
  531.1 3.8 copy-start.13
  533.0 9.6 %collective-permute-start = (f32[4,6912]{1,0:T(4,128)S(1)}, f32[4,6912]{1,0:T(4,128)S(1)}, u32[]{:S(2)}, u32[]{:S(2)}) collective-permute-start(f32[4,6912]{1,0:T(4,128)S(1)} %fusion.8), channel_id=1, source_target_pairs={{0,1},{1,0},{2,3},{3,2},{4,5},{5,4},{6,7},{7,6},{8,9},{9,8},{10,11... | collective-permute-start | bytes 331784 | tf_op jit(solution)/shard_map/ppermute | solution.py:1390
  533.6 7.5 copy-start.6
  533.6 7.5 copy-start.7
  890.1 6.0 copy-start.4
  897.1 10.9 %copy-start.1 = (bf16[72,6912]{1,0:T(8,128)(2,1)S(1)}, bf16[72,6912]{1,0:T(8,128)(2,1)}, u32[]{:S(2)}) copy-start(bf16[72,6912]{1,0:T(8,128)(2,1)} %param.28) | copy-start | bytes 2985988

commit v4 on v3

--- a/solution.py
+++ b/solution.py
@@ -45,13 +45,13 @@
 
 
 class Exchange:
-    def __init__(self, broadcast, in_ref, out_ref, ssem, rsem, lsem):
+    def __init__(self, same, in_ref, out_ref, ssem, rsem, lsem):
         self.refs = (in_ref, out_ref, ssem, rsem, lsem)
-        self.broadcast = broadcast
+        self.same = same
         self.me = lax.axis_index("dp")
 
     def source(self, target):
-        return self.refs[0] if self.broadcast else self.refs[0].at[target]
+        return self.refs[0] if self.same else self.refs[0].at[target]
 
     def copy(self, k, target, slot):
         return pltpu.make_async_remote_copy(
@@ -81,7 +81,61 @@
             self.copy(k, origin, origin).wait_recv()
 
 
-def gather_kernel(units, count, stride, group, lag, *refs):
+class Broadcast:
+    def __init__(self, in_ref, out_ref, ssem, rsem, lsem):
+        self.refs = (in_ref, out_ref, ssem, rsem, lsem)
+        self.z, self.y, self.x, self.c = coords()
+
+    def own(self):
+        return pltpu.make_async_copy(
+            self.refs[0], self.refs[1].at[self.z, self.y, self.x], self.refs[4].at[0]
+        )
+
+    def along(self, k, arrival):
+        there = lax.rem(self.z + (4 - k if arrival else k), 4)
+        slot = there if arrival else self.z
+        return pltpu.make_async_remote_copy(
+            self.refs[0],
+            self.refs[1].at[slot, self.y, self.x],
+            self.refs[2].at[k],
+            self.refs[3].at[k],
+            device_id=device(there, self.y, self.x, self.c),
+            device_id_type=MESH,
+        )
+
+    def across(self, k, arrival):
+        y = lax.rem(self.y + k // 2, 2)
+        x = lax.rem(self.x + k % 2, 2)
+        block = self.refs[1].at[:, y, x] if arrival else self.refs[1].at[:, self.y, self.x]
+        return pltpu.make_async_remote_copy(
+            block,
+            block,
+            self.refs[2].at[3 + k],
+            self.refs[3].at[3 + k],
+            device_id=device(self.z, y, x, self.c),
+            device_id_type=MESH,
+        )
+
+    def start(self):
+        for k in range(1, 4):
+            self.along(k, False).start()
+        self.own().start()
+
+    def forward(self):
+        self.own().wait()
+        for k in range(1, 4):
+            self.along(k, True).wait_recv()
+        for k in range(1, 4):
+            self.across(k, False).start()
+
+    def wait(self):
+        for k in range(1, 4):
+            self.along(k, False).wait_send()
+            self.across(k, False).wait_send()
+            self.across(k, True).wait_recv()
+
+
+def gather_kernel(units, turns, count, *refs):
     w = refs[:count]
     o = refs[count + 1 : 2 * count + 1]
     ssem, rsem, lsem, csem, crsem, es, er, el = refs[2 * count + 2 :]
@@ -94,7 +148,7 @@
     partner = {"y": device(z, 1 - y, x, c), "x": device(z, y, 1 - x, c)}
     every = slice(None)
 
-    def run(mine, other):
+    def run(mine, other, order):
         def view(u, index):
             m, first, cols, _ = mine[u]
             return o[m].at[index[0], index[1], index[2], :, pl.ds(first, cols)]
@@ -171,22 +225,16 @@
 
         for u in range(len(mine)):
             local_copy(u).start()
-        starts = [(u // group) * stride for u in range(len(mine))]
-        for turn in range(max(starts) + 6 + lag):
-            for u in range(len(mine)):
-                steps, pending, _ = plans[u]
-                s = turn - starts[u]
-                if 0 <= s < 5:
-                    if s == 1:
-                        local_copy(u).wait()
-                    for cond, make in steps[s][0]:
-                        when(cond, lambda make=make: make().wait_recv())
-                    for cond, make in steps[s][1]:
-                        when(cond, lambda make=make: make().start())
-                elif s == 5 + lag:
-                    for cond, make in pending:
-                        when(cond, lambda make=make: make().wait_recv())
-                    to_core(u, mine).start()
+        for u, s in order:
+            steps, pending, _ = plans[u]
+            if s == 1:
+                local_copy(u).wait()
+            for cond, make in steps[s][0] if s < 5 else pending:
+                when(cond, lambda make=make: make().wait_recv())
+            for cond, make in steps[s][1] if s < 5 else ():
+                when(cond, lambda make=make: make().start())
+            if s == 5:
+                to_core(u, mine).start()
         for u in range(len(mine)):
             for cond, make in plans[u][2]:
                 when(cond, lambda make=make: make().wait_send())
@@ -194,8 +242,8 @@
         for u in range(len(other)):
             to_core(u, other).wait_recv()
 
-    pl.when(c == 0)(lambda: run(units[0], units[1]))
-    pl.when(c == 1)(lambda: run(units[1], units[0]))
+    pl.when(c == 0)(lambda: run(units[0], units[1], turns[0]))
+    pl.when(c == 1)(lambda: run(units[1], units[0], turns[1]))
     side.wait()
 
 
@@ -206,12 +254,12 @@
 SIDE = [DMA((16,)), DMA((16,)), DMA((1,))]
 
 
-def gather(shards, rows, units, collective_id, stride, group, lag, name):
+def gather(shards, rows, units, turns, collective_id, name):
     count = len(shards)
     most = max(len(units[0]), len(units[1]))
     shapes = [jax.ShapeDtypeStruct(GRID + s.shape, s.dtype) for s in shards]
     return pl.pallas_call(
-        functools.partial(gather_kernel, units, count, stride, group, lag),
+        functools.partial(gather_kernel, units, turns, count),
         name=name,
         out_shape=shapes + [jax.ShapeDtypeStruct(rows.shape, rows.dtype)],
         in_specs=[ANY] * (count + 1),
@@ -222,26 +270,53 @@
     )(*shards, rows)
 
 
-def gather_units(shards, size):
-    orders = (
-        ("xzy", "yzx", "zyx", "yzx", "xzy", "zxy"),
-        ("yzx", "xzy", "zxy", "xzy", "yzx", "zyx"),
-    )
+ORDERS = (
+    ("zyx", "zxy", "xyz", "zxy", "zyx", "zxy", "zyx", "yxz", "zyx", "zxy"),
+    ("zxy", "zyx", "yxz", "zyx", "zxy", "zyx", "zxy", "xyz", "zxy", "zyx"),
+)
+AFTER_Z = (0.6165, 0.4168, 0.3474, 1.6339, 4.4601)
+AFTER_XY = (1.5672, 1.5028, 1.8589, 1.1737, 2.0677)
+PER_TURN = 2.2835
+SHIFT = 0.1931
+SIZE = 4
+TAIL = (0.1, 2)
+
+
+def gather_units(shards):
     units = ([], [])
     load = [0, 0]
+    whole = sum(s.size for s in shards) / (ROWS * 128)
+    done = 0
     for m, shard in enumerate(shards):
         rows, columns = shard.shape
         tiles = columns // 128
-        cuts = max(1, round(tiles * rows / 72 / size))
+        weight = rows / ROWS
         at = 0
-        for k in range(cuts):
-            n = tiles // cuts + (1 if k < tiles % cuts else 0)
+        while at < tiles:
+            size = SIZE if done < (1 - TAIL[0]) * whole else TAIL[1]
+            step = max(1, round(size / weight))
+            n = min(step, tiles - at)
+            if 0 < tiles - at - n < max(1, round(size / weight / 2)):
+                n = tiles - at
             core = 0 if load[0] <= load[1] else 1
-            order = orders[core][len(units[core]) % 6]
+            order = ORDERS[core][len(units[core]) % len(ORDERS[core])]
             units[core].append((m, at * 128, n * 128, order))
-            load[core] += n * rows
+            load[core] += n * weight
+            done += n * weight
             at += n
-    return tuple(units[0]), tuple(units[1])
+    turns = []
+    for core in range(2):
+        keys = []
+        place = 0.0
+        for u, (m, first, columns, order) in enumerate(units[core]):
+            at = place / PER_TURN + core * SHIFT
+            place += shards[m].shape[0] * columns / (ROWS * 128 * SIZE)
+            keys.append((at, u, 0))
+            for s, after in enumerate(AFTER_Z if order[0] == "z" else AFTER_XY):
+                at += after
+                keys.append((at, u, s + 1))
+        turns.append(tuple((u, s) for _, u, s in sorted(keys)))
+    return (tuple(units[0]), tuple(units[1])), tuple(turns)
 
 
 def exchange_kernel(in_ref, out_ref, *sems):
@@ -288,7 +363,7 @@
     up = device(z + 1, y, x, c)
     down = device(z - 1, y, x, c)
     greet()
-    side = Exchange(True, refs[nv + dy_count], refs[nv + dy_count + 2], es, er, el)
+    side = Broadcast(refs[nv + dy_count], refs[nv + dy_count + 2], es, er, el)
     lanes = pl.ds(pl.multiple_of(c * 128, 128), 128)
     offsets = []
     at = 0
@@ -485,25 +560,19 @@
         e_t[s] = part[:, :, 128:].reshape(4, 2, ROWS, 256) + e_b1[w].astype(F32)
         z_send(i, 0, True)
 
-    def stage2(i):
+    def a_second(i):
         f, s, w = slots(i)
         qb = axes(i)[2]
         second_copy(i).wait_recv()
         a_t[s, :, qb] = a_t[s, :, qb] + a_b2[w].astype(F32)
         z_send(i, 0, False)
-        z_wait(i, 0, True)
-        z_send(i, 1, True)
-
-    def stage3(i):
-        z_wait(i, 0, False)
-        z_send(i, 1, False)
-        z_wait(i, 1, True)
-        z_send(i, 2, True)
-
-    def stage4(i):
+
+    def z_step(i, k, e):
+        z_wait(i, k - 1, e)
+        z_send(i, k, e)
+
+    def e_fourth(i):
         f, s, w = slots(i)
-        z_wait(i, 1, False)
-        z_send(i, 2, False)
         z_wait(i, 2, True)
         z_close(i, True)
         e_sq[s] = e_t[s, z, 1 - axes(i)[2]].astype(BF16)
@@ -512,10 +581,12 @@
     def out_view(i):
         return out.at[:, pl.ds(pl.multiple_of((2 * i + c) * UNIT, 128), UNIT)]
 
-    def stage5(i):
-        f, s, w = slots(i)
+    def a_fifth(i):
         z_wait(i, 2, False)
         outs[i, :, :128] = z_close(i, False)[...]
+
+    def e_fifth(i):
+        f, s, w = slots(i)
         last_copy(i).wait_recv()
         outs[i, :, 128:] = e_t[s, z, axes(i)[2]] + e_bq[w].astype(F32)
         pltpu.make_async_copy(outs.at[i], out_view(i), ol.at[0]).start()
@@ -533,15 +604,27 @@
                 pl.when(up_sends(k))(lambda k=k, e=e: up_copy(i, k, e).wait_send())
                 pl.when(down_sends(k))(lambda k=k, e=e: down_copy(i, k, e).wait_send())
 
-    stages = (stage0, stage1, stage2, stage3, stage4, stage5)
+    stages = (
+        (a_fifth, LAG[5]),
+        (functools.partial(z_step, k=1, e=False), LAG[3]),
+        (functools.partial(z_step, k=2, e=True), LAG[3]),
+        (e_fourth, LAG[4]),
+        (stage0, LAG[0]),
+        (functools.partial(z_step, k=1, e=True), LAG[2]),
+        (a_second, LAG[2]),
+        (functools.partial(z_step, k=2, e=False), LAG[4]),
+        (e_fifth, LAG[5]),
+        (stage1, LAG[1]),
+    )
 
     def tick(t, carry):
         arrive(t)
+        pl.when(t == 4)(side.forward)
         pl.when((t >= SEND_SLOTS) & (t - SEND_SLOTS < total))(lambda: sent(t - SEND_SLOTS))
         pl.when((t >= FIRST_SLOTS) & (t - FIRST_SLOTS < total))(lambda: first_sent(t - FIRST_SLOTS))
-        for k in reversed(range(6)):
-            i = t - LAG[k]
-            pl.when((i >= 0) & (i < total))(functools.partial(stages[k], i))
+        for stage, lag in stages:
+            i = t - lag
+            pl.when((i >= 0) & (i < total))(functools.partial(stage, i))
         return carry
 
     lax.fori_loop(0, total + SEND_SLOTS, tick, 0)
@@ -577,7 +660,7 @@
         name=name,
         out_shape=[
             jax.ShapeDtypeStruct((ROWS, first[-1] * UNIT), F32),
-            jax.ShapeDtypeStruct((16,) + rows.shape, rows.dtype),
+            jax.ShapeDtypeStruct(GRID + rows.shape, rows.dtype),
         ],
         in_specs=[ANY] * (nv + len(dys) + 1),
         out_specs=[ANY] * 2,
@@ -1242,6 +1325,41 @@
     return jnp.pad(rows, ((0, 0), (0, PADDED - rows.shape[1]), (0, 0)))
 
 
+def split_kernel(pieces, in_ref, *refs):
+    *outs, held, arrived, left = refs
+    for k, (n, row, rows, columns, at) in enumerate(pieces):
+        span = (pl.ds(0, rows), pl.ds(at, columns))
+        pltpu.make_async_copy(in_ref.at[span], held.at[span], arrived.at[k]).start()
+
+    def leave(k):
+        n, row, rows, columns, at = pieces[k]
+        span = (pl.ds(0, rows), pl.ds(at, columns))
+        return pltpu.make_async_copy(held.at[span], outs[n].at[pl.ds(row, rows), :], left.at[k])
+
+    for k, (n, row, rows, columns, at) in enumerate(pieces):
+        span = (pl.ds(0, rows), pl.ds(at, columns))
+        pltpu.make_async_copy(in_ref.at[span], held.at[span], arrived.at[k]).wait()
+        leave(k).start()
+    for k in range(len(pieces)):
+        leave(k).wait()
+
+
+def split(values, shapes, pieces):
+    return pl.pallas_call(
+        functools.partial(split_kernel, tuple(pieces)),
+        name="split",
+        out_shape=[jax.ShapeDtypeStruct(shape, values.dtype) for shape in shapes],
+        in_specs=[ANY],
+        out_specs=[ANY] * len(shapes),
+        scratch_shapes=[
+            pltpu.VMEM(values.shape, values.dtype),
+            DMA((len(pieces),)),
+            DMA((len(pieces),)),
+        ],
+        compiler_params=pltpu.CompilerParams(vmem_limit_bytes=32 * 1024 * 1024),
+    )(values)
+
+
 def rope_lanes(cosine, sine):
     tokens = cosine.shape[0]
 
@@ -1269,21 +1387,28 @@
         source.append(len(dys))
         dys.append(jnp.eye(tokens, UNIT, dtype=BF16))
     out, rows = scatter(xts, dys, source, rows, collective_id, name)
-    results = []
+    shapes = []
+    pieces = []
+    smalls = []
     at = 0
     for factors, extra in blocks:
-        grads = []
         for lefts, right in factors[:-1]:
-            grads.append(out[:, at : at + right.shape[1]])
+            pieces.append((len(shapes), 0, ROWS, right.shape[1], at))
+            shapes.append((ROWS, right.shape[1]))
             at += right.shape[1]
         width = factors[-1][1].shape[1]
-        parts = [out[:64, at + g * width : at + (g + 1) * width] for g in range(3)]
-        grads.append(jnp.concatenate(parts, axis=0))
-        at += 3 * width
+        for g in range(3):
+            pieces.append((len(shapes), 64 * g, 64, width, at))
+            at += width
+        shapes.append((192, width))
         lines = -(-extra.shape[1] // tokens)
-        small = out[:lines, at : at + tokens].reshape(-1)[: extra.shape[1]]
+        smalls.append(out[:lines, at : at + tokens].reshape(-1)[: extra.shape[1]])
         at += UNIT
-        results.append((grads, small))
+    grads = split(out, shapes, pieces)
+    results = []
+    for (factors, extra), small in zip(blocks, smalls):
+        results.append((grads[: len(factors)], small))
+        grads = grads[len(factors) :]
     return results, rows
 
 
@@ -1324,15 +1449,25 @@
     me = lax.axis_index("dp")
     rows = encoder[0].shape[0]
     act_mine = lax.dynamic_slice_in_dim(act_rows, me * rows, rows, 1)
-    partial = dense(act_mine, encoder[0]).reshape(16, 8, -1)
+    core = lax.axis_index("ctx")
+    share = encoder[0].shape[1] // 2
+    partial = dense(act_mine, lax.dynamic_slice_in_dim(encoder[0], core * share, share, 1))
+    partial = partial.reshape(16, 8, -1)
     shards = (encoder[2], encoder[4], encoder[5], encoder[6])
     shards += (decoder[0], decoder[2], decoder[4], decoder[5], decoder[6])
-    *wholes, partial = gather(shards, partial, gather_units(shards, 7), 1, 1, 3, 1, "gather")
+    *wholes, partial = gather(shards, partial, *gather_units(shards), 1, "gather")
     wholes = [whole_rows(w) for w in wholes]
     encoder_weights = (*wholes[:4], encoder_gains)
     modulate = wholes[4]
     decoder_weights = (*wholes[5:], decoder_gains)
-    modulation_rows = jnp.sum(partial, axis=0).reshape(segments, -1) + encoder_offset
+    partial = jnp.sum(partial, axis=0).reshape(segments, -1)
+    others = lax.ppermute(partial, "ctx", [(0, 1), (1, 0)])
+    modulation_rows = jnp.where(
+        core == 0,
+        jnp.concatenate([partial, others], axis=1),
+        jnp.concatenate([others, partial], axis=1),
+    )
+    modulation_rows = modulation_rows + encoder_offset
     exact = lax.Precision.HIGHEST
     encoder_modulation = jnp.dot(picks, modulation_rows, precision=exact)
     cond_rows = lax.dynamic_slice_in_dim(all_cond, me * segments, segments, 0)

time: 914 us -> 856 us (0.937)
  Pallas kernels: 826 us -> 784 us
  local copies, waits for them, and re-layouts: 39.3 us -> 27.6 us
    pallas_call x1 -> x2, Pallas kernels: 353 us -> 328 us  [the longest x1 324 us: gather(): pl.pallas_call(functools.partial(gather_kernel, units, turns, count), nam...]
    pallas_call x1, Pallas kernels: 340 us -> 322 us  [scatter(): pl.pallas_call(functools.partial(scatter_kernel, tuple(first), tuple(cols...]
    slice x5 -> x0, local copies, waits for them, and re-layouts: 14.4 us -> none  [the longest x4 12 us: fast_reduce(): grads.append(out[:, at:at + right.shape[1]])]
  transfers between devices with their start and end apart: 1 -> 2, of which waited for: 0 -> 0; matrix products, arithmetic and copies ran while one was open for 1% -> 2% of each run, Pallas kernels for 0% -> 0%
where the time goes in v4:
time: 856 us; the launch traced here: 851 us
  Pallas kernels  784 us (92%)
  matrix products  31.2 us (4%)
  local copies, waits for them, and re-layouts  27.6 us (3%)
    pallas_call x1, Pallas kernels, gather(): pl.pallas_call(functools.partial(gather_kernel, units, turns, count), nam...  324 us
    pallas_call x1, Pallas kernels, scatter(): pl.pallas_call(functools.partial(scatter_kernel, tuple(first), tuple(cols...  322 us
    pallas_call x2, Pallas kernels, kernel_backward(): pl.pallas_call(backward_kernel, name=name, out_shape=out_shape, in_specs=...  72.6 us
    pallas_call x2, Pallas kernels, kernel_forward(): pl.pallas_call(forward_kernel, name=name, out_shape=out_shape, in_specs=[...  49.9 us
  transfers between devices with their start and end apart: 2, of which 0 were waited for; matrix products, arithmetic and copies ran while one was open for 2% of the time, Pallas kernels for 0%

profile of v4, /device:TPU:0, one launch (start us, length us, event | category | flops | bytes accessed | tf_op | source)
XLA Modules:
  0.0 850.7 jit_solution(9605176694236202535)
XLA Ops:
  0.7 0.8 reshape.296
  2.9 1.5 concatenate.21
  5.0 10.7 %small.1 = f32[16,16,128]{2,1,0:T(8,128)} custom-call(f32[16,128]{1,0:T(8,128)} %pad_bitcast_fusion.in_ref), custom_call_target="tpu_custom_call" | custom-call | tf_op jit(solution)/shard_map/small/pallas_call | solution.py:330
  15.7 0.9 copy.69
  17.7 1.2 reshape.261.refs_9_
  19.0 323.8 %gather.1 = (bf16[4,2,2,72,3456]{4,3,2,1,0:T(8,128)(2,1)}, bf16[4,2,2,72,1152]{4,3,2,1,0:T(8,128)(2,1)}, bf16[4,2,2,72,6144]{4,3,2,1,0:T(8,128)(2,1)}, bf16[4,2,...) custom-call(bf16[72,3456]{1,0:T(8,128)(2,1)} %refs_0_.1, ...), custom_call_target="tpu_custom_call" | custom-call | tf_op jit(solution)/shard_map/gather/pallas_call | solution.py:261
  342.7 1.2 reduce_sum.27
  345.5 0.9 bitcast_convert_fusion.flat
  346.3 0.9 convert_multiply_fusion.grad_out
  347.4 1.1 copy.50.sine
  348.5 1.1 copy.49.cosine
  349.6 0.7 copy.51.seg_q
  352.0 3.4 fusion.9.mod
  355.3 24.9 %encoder.1 = (f32[128,1152]{1,0:T(8,128)}, f32[128,2304]{1,0:T(8,128)}, bf16[128,1152]{1,0:T(8,128)(2,1)}, bf16[2,256,1152]{2,1,0:T(8,128)(2,1)}, f32[128,128]{1...) custom-call(f32[128,1152]{1,0:T(8,128)} %bitcast_convert_fusion.flat, ...), custom_call_target="tpu_custom_call" | custom-call | tf_op jit(solution)/shard_map/encoder/pallas_call | solution.py:1262
  380.2 1.5 convolution_add_fusion.1
  381.7 10.0 %convolution_add_fusion.mod = f32[128,6912]{1,0:T(8,128)} fusion(bf16[1152,6912]{1,0:T(8,128)(2,1)} %bitcast.80, f32[6912]{0:T(1024)S(1)} %add.79, f32[128,1152]{1,0:T(8,128)S(1)} %convolution_add_fusion.1), kind=kOutput, calls=%fused_computation | convolution fusion | flops 2040053760 | bytes 20081664 | tf_op jit(solution)/shard_map/dot_general | solution.py:764
  391.7 25.0 %decoder.1 = (f32[128,1152]{1,0:T(8,128)}, f32[128,2304]{1,0:T(8,128)}, bf16[128,1152]{1,0:T(8,128)(2,1)}, bf16[2,256,1152]{2,1,0:T(8,128)(2,1)}, f32[128,128]{1...) custom-call(f32[128,1152]{1,0:T(8,128)} %bitcast_convert_fusion.flat, ...), custom_call_target="tpu_custom_call" | custom-call | tf_op jit(solution)/shard_map/decoder/pallas_call | solution.py:1262
  416.8 36.1 %decoder_back.1 = (f32[128,1152]{1,0:T(8,128)}, bf16[128,6912]{1,0:T(8,128)(2,1)}, bf16[128,1152]{1,0:T(8,128)(2,1)}, bf16[128,6144]{1,0:T(8,128)(2,1)}, bf16[12...) custom-call(f32[128,1152]{1,0:T(8,128)} %convert_multiply_fusion.grad_out, ...), custom_call_target="tpu_custom_call" | custom-call | tf_op jit(solution)/shard_map/decoder_back/pallas_call | solution.py:1297
  452.9 12.1 %fusion.40 = (bf16[1152,128]{0,1:T(8,128)(2,1)S(1)}, f32[128,1152]{1,0:T(8,128)}, bf16[1,128,1152]{2,1,0:T(8,128)(2,1)}, bf16[1,128,1152]{2,1,0:T(8,128)(2,1)}) fusion(f32[128,1152]{1,0:T(8,128)S(1)} %convolution_add_fusion.1, f32[128]{0:T(128)S(1)} %fusion.32, f32[128,1152]{1,0:T(8,128)S(1)} %copy-done.5, f32[128,1152]{1,0:T(8,128)S(1)} %copy-done.4, ...), kind=kOutput, calls=%fused_computation.87 | convolution fusion | flops 2040791040 | bytes 20939264 | tf_op jit(solution)/shard_map/dot_general | solution.py:768
  465.0 36.5 %encoder_back.1 = (f32[128,1152]{1,0:T(8,128)}, bf16[128,6912]{1,0:T(8,128)(2,1)}, bf16[128,1152]{1,0:T(8,128)(2,1)}, bf16[128,6144]{1,0:T(8,128)(2,1)}, bf16[12...) custom-call(f32[128,1152]{1,0:T(8,128)} %get-tuple-element.146.grad_out, ...), custom_call_target="tpu_custom_call" | custom-call | tf_op jit(solution)/shard_map/encoder_back/pallas_call | solution.py:1297
  501.5 1.9 fusion.20
  504.3 2.1 slice_bitcast_fusion.3
  506.4 2.1 slice_bitcast_fusion
  508.6 0.9 add_bitcast_fusion
  509.6 0.8 pad.29.refs_7_
  510.6 0.8 pad.31.refs_14_
  511.6 0.8 pad.27.refs_0_
  513.1 322.0 %scatter.1 = (f32[72,36096]{1,0:T(8,128)}, bf16[4,2,2,16,1728]{4,3,2,1,0:T(8,128)(2,1)}) custom-call(bf16[16,80,128]{2,1,0:T(8,128)(2,1)} %pad.27.refs_0_, bf16[16,80,128]{2,1,0:T(8,128)(2,1)} %get-tuple-element.109.refs_1_, bf16[16,80,128]{2,1,0:T(8,128)(2,1)} %get-tuple-element.110.refs_2_, bf16[16,80,128]{2,1,0:T(8,128)(2,1)} %get-tuple-element.111.refs_3_, ...), custom_call_target="tpu_custom_call" | custom-call | tf_op jit(solution)/shard_map/scatter/pallas_call | solution.py:658
  835.1 2.1 reshape.289
  837.2 1.8 fusion.39
  839.2 4.0 copy-done.2
  843.2 4.7 split.1
  (92 shorter events, 11.4 us)
Async XLA Ops:
  0.7 16.7 %copy-start = (bf16[72,6912]{1,0:T(8,128)(2,1)S(1)}, bf16[72,6912]{1,0:T(8,128)(2,1)}, u32[]{:S(2)}) copy-start(bf16[72,6912]{1,0:T(8,128)(2,1)} %param.28) | copy-start | bytes 2985988
  18.9 326.3 %copy-start.14 = (s32[1,256]{1,0:T(1,128)S(1)}, s32[1,256]{1,0:T(1,128)}, u32[]{:S(2)}) copy-start(s32[1,256]{1,0:T(1,128)} %param.24) | copy-start | bytes 3076
  18.9 326.3 %copy-start.15 = (s32[1,256]{1,0:T(1,128)S(1)}, s32[1,256]{1,0:T(1,128)}, u32[]{:S(2)}) copy-start(s32[1,256]{1,0:T(1,128)} %param.25) | copy-start | bytes 3076
  18.9 326.5 %copy-start.8 = (bf16[1,128,1152]{2,1,0:T(8,128)(2,1)S(1)}, bf16[1,128,1152]{2,1,0:T(8,128)(2,1)}, u32[]{:S(2)}) copy-start(bf16[1,128,1152]{2,1,0:T(8,128)(2,1)} %param.21) | copy-start | bytes 884740
  18.9 327.4 %copy-start.11 = (s32[1,256]{1,0:T(1,128)S(1)}, s32[1,256]{1,0:T(1,128)}, u32[]{:S(2)}) copy-start(s32[1,256]{1,0:T(1,128)} %pad_k.7) | copy-start | bytes 3076
  18.9 327.4 %copy-start.9 = (bf16[1,128,1152]{2,1,0:T(8,128)(2,1)S(1)}, bf16[1,128,1152]{2,1,0:T(8,128)(2,1)}, u32[]{:S(2)}) copy-start(bf16[1,128,1152]{2,1,0:T(8,128)(2,1)} %param.22) | copy-start | bytes 884740
  342.7 4.5 copy-start.10
  344.1 7.9 collective-permute-start
  416.8 36.1 %copy-start.4 = (f32[128,1152]{1,0:T(8,128)S(1)}, f32[128,1152]{1,0:T(8,128)}, u32[]{:S(2)}) copy-start(f32[128,1152]{1,0:T(8,128)} %get-tuple-element.83) | copy-start | bytes 1769476
  416.8 36.1 %copy-start.5 = (f32[128,1152]{1,0:T(8,128)S(1)}, f32[128,1152]{1,0:T(8,128)}, u32[]{:S(2)}) copy-start(f32[128,1152]{1,0:T(8,128)} %get-tuple-element.89) | copy-start | bytes 1769476
  465.0 38.6 %copy-start.3 = (bf16[128,6912]{1,0:T(8,128)(2,1)S(1)}, bf16[128,6912]{1,0:T(8,128)(2,1)}, u32[]{:S(2)}) copy-start(bf16[128,6912]{1,0:T(8,128)(2,1)} %get-tuple-element.99.refs_15_) | copy-start | bytes 5308420
  501.5 2.6 copy-start.12
  503.5 5.1 copy-start.6
  503.5 8.9 %collective-permute-start.1 = (f32[4,6912]{1,0:T(4,128)S(1)}, f32[4,6912]{1,0:T(4,128)S(1)}, u32[]{:S(2)}, u32[]{:S(2)}) collective-permute-start(f32[4,6912]{1,0:T(4,128)S(1)} %fusion.20), channel_id=1, source_target_pairs={{0,1},{1,0},{2,3},{3,2},{4,5},{5,4},{6,7},{7,6},{8,9},{9,8},{10,11... | collective-permute-start | bytes 331784 | tf_op jit(solution)/shard_map/ppermute | solution.py:1525
  504.0 4.6 copy-start.7
  504.0 6.4 copy-start.13
  839.2 11.4 %copy-start.1 = (bf16[72,6912]{1,0:T(8,128)(2,1)S(1)}, bf16[72,6912]{1,0:T(8,128)(2,1)}, u32[]{:S(2)}) copy-start(bf16[72,6912]{1,0:T(8,128)(2,1)} %param.28) | copy-start | bytes 2985988
  839.2 4.0 copy-start.2

commit v5 on v4

--- a/solution.py
+++ b/solution.py
@@ -79,6 +79,67 @@
             self.copy(k, lax.rem(self.me + k, 16), self.me).wait_send()
             origin = lax.rem(self.me + 16 - k, 16)
             self.copy(k, origin, origin).wait_recv()
+
+
+class Sums:
+    def __init__(self, in_ref, out_ref, box, total, ssem, rsem, lsem):
+        self.refs = (in_ref, out_ref, box, total)
+        self.sems = (ssem, rsem, lsem)
+        self.z, self.y, self.x, self.c = coords()
+
+    def remote(self, src, dst, k, target):
+        return pltpu.make_async_remote_copy(
+            src,
+            dst,
+            self.sems[0].at[k],
+            self.sems[1].at[k],
+            device_id=target,
+            device_id_type=MESH,
+        )
+
+    def across(self, k):
+        y = lax.rem(self.y + k // 2, 2)
+        x = lax.rem(self.x + k % 2, 2)
+        target = device(self.z, y, x, self.c)
+        return self.remote(self.refs[0].at[:, y, x], self.refs[2].at[k], k, target)
+
+    def own(self):
+        return pltpu.make_async_copy(
+            self.refs[0].at[:, self.y, self.x], self.refs[2].at[0], self.sems[2].at[0]
+        )
+
+    def along(self, k, arrival):
+        there = lax.rem(self.z + (4 - k if arrival else k), 4)
+        slot = there if arrival else self.z
+        target = device(there, self.y, self.x, self.c)
+        return self.remote(self.refs[3].at[there], self.refs[1].at[slot], 3 + k, target)
+
+    def kept(self):
+        return pltpu.make_async_copy(
+            self.refs[3].at[self.z], self.refs[1].at[self.z], self.sems[2].at[1]
+        )
+
+    def start(self):
+        for k in range(1, 4):
+            self.across(k).start()
+        self.own().start()
+
+    def forward(self):
+        self.own().wait()
+        for k in range(1, 4):
+            self.across(k).wait_recv()
+        box = self.refs[2]
+        self.refs[3][...] = (box[0] + box[1]) + (box[2] + box[3])
+        for k in range(1, 4):
+            self.along(k, False).start()
+        self.kept().start()
+
+    def wait(self):
+        self.kept().wait()
+        for k in range(1, 4):
+            self.across(k).wait_send()
+            self.along(k, False).wait_send()
+            self.along(k, True).wait_recv()
 
 
 class Broadcast:
@@ -138,10 +199,10 @@
 def gather_kernel(units, turns, count, *refs):
     w = refs[:count]
     o = refs[count + 1 : 2 * count + 1]
-    ssem, rsem, lsem, csem, crsem, es, er, el = refs[2 * count + 2 :]
+    ssem, rsem, lsem, csem, crsem, box, sums, es, er, el = refs[2 * count + 2 :]
     z, y, x, c = coords()
     greet()
-    side = Exchange(False, refs[count], refs[2 * count + 1], es, er, el)
+    side = Sums(refs[count], refs[2 * count + 1], box, sums, es, er, el)
     side.start()
     up = device(z + 1, y, x, c)
     down = device(z - 1, y, x, c)
@@ -225,7 +286,9 @@
 
         for u in range(len(mine)):
             local_copy(u).start()
-        for u, s in order:
+        for at, (u, s) in enumerate(order):
+            if at == FORWARD_AT:
+                side.forward()
             steps, pending, _ = plans[u]
             if s == 1:
                 local_copy(u).wait()
@@ -261,11 +324,21 @@
     return pl.pallas_call(
         functools.partial(gather_kernel, units, turns, count),
         name=name,
-        out_shape=shapes + [jax.ShapeDtypeStruct(rows.shape, rows.dtype)],
+        out_shape=shapes + [jax.ShapeDtypeStruct(GRID[:1] + rows.shape[3:], rows.dtype)],
         in_specs=[ANY] * (count + 1),
         out_specs=[ANY] * (count + 1),
-        scratch_shapes=[DMA((most, 8)), DMA((most, 8)), DMA((most,)), DMA((most,)), DMA((most,))]
-        + SIDE,
+        scratch_shapes=[
+            DMA((most, 8)),
+            DMA((most, 8)),
+            DMA((most,)),
+            DMA((most,)),
+            DMA((most,)),
+            pltpu.VMEM((4,) + GRID[:1] + rows.shape[3:], rows.dtype),
+            pltpu.VMEM(GRID[:1] + rows.shape[3:], rows.dtype),
+            DMA((7,)),
+            DMA((7,)),
+            DMA((2,)),
+        ],
         compiler_params=pltpu.CompilerParams(collective_id=collective_id, has_side_effects=True),
     )(*shards, rows)
 
@@ -277,6 +350,7 @@
 AFTER_Z = (0.6165, 0.4168, 0.3474, 1.6339, 4.4601)
 AFTER_XY = (1.5672, 1.5028, 1.8589, 1.1737, 2.0677)
 PER_TURN = 2.2835
+FORWARD_AT = 40
 SHIFT = 0.1931
 SIZE = 4
 TAIL = (0.1, 2)
@@ -395,14 +469,17 @@
         return remote(*y_views(k), ys.at[k], yr.at[k], sibling)
 
     fresh = [source[v] not in source[:v] for v in range(nv)]
-    for v in range(nv):
+
+    def bring(v):
         x_local(v).start()
         x_remote(v).start()
         if fresh[v]:
             y_local(source[v]).start()
             y_remote(source[v]).start()
-        if v == 0:
-            side.start()
+
+    bring(0)
+    bring(1)
+    side.start()
 
     def arrive(tick):
         for v in range(nv):
@@ -413,6 +490,8 @@
                 if fresh[v]:
                     y_local(source[v]).wait()
                     y_remote(source[v]).wait_recv()
+                if v + 2 < nv:
+                    bring(v + 2)
 
             pl.when(tick == (first[v] - c + 1) // 2)(wait)
 
@@ -1001,323 +1080,399 @@
     return (seg_q[...] == seg_k[...]) & ((pad_k[...] == 0) | (place_q == place_k))
 
 
-def forward_kernel(
-    flat, mod, gains, cosine, sine, seg_q, seg_k, pad_k, triple_h, mixing_h, expand_h, reduce_h,
-    output, raw, queries, kv, lse, attended, resid, expanded, feed, xt1, xtm, xt2, xth,
-    triple, mixing, expand, reduce_w, mixed, wsem, ssem, rsem,
-):
-    half, width = flat.shape
-    loads = [
-        pltpu.make_async_copy(src, dst, wsem.at[k])
-        for k, (src, dst) in enumerate(
-            ((triple_h, triple), (mixing_h, mixing), (expand_h, expand), (reduce_h, reduce_w))
-        )
-    ]
-    for load in loads:
-        load.start()
-    sibling = meet_sibling()
+class Traffic:
+    def __init__(self, held, sources, targets, lsem, ssem):
+        self.held = held
+        names = [n for n in sources]
+        self.loads = {
+            n: pltpu.make_async_copy(sources[n], held[n], lsem.at[k]) for k, n in enumerate(names)
+        }
+        self.sources = sources
+        self.tiles = {}
+        self.stores = {
+            n: pltpu.make_async_copy(held[n], targets[n], ssem.at[k])
+            for k, n in enumerate(targets)
+        }
+        self.waiting = set(names)
+
+    def __getattr__(self, name):
+        return self.held[name]
+
+    def fetch(self, *names):
+        for n in names:
+            if n in self.loads:
+                self.loads[n].start()
+
+    def fetch_tile(self, t, size, rows, columns, sem):
+        spans = [(n, (pl.ds(t * size, size), slice(None))) for n in rows]
+        for n in columns:
+            for first in (0, self.held[n].shape[1] // 2):
+                spans.append((n, (slice(None), pl.ds(first + t * size, size))))
+        self.tiles[t] = [
+            pltpu.make_async_copy(self.sources[n].at[at], self.held[n].at[at], sem.at[t, k])
+            for k, (n, at) in enumerate(spans)
+        ]
+        for copy in self.tiles[t]:
+            copy.start()
+        self.waiting.difference_update(rows + columns)
+
+    def need_tile(self, t):
+        for copy in self.tiles.pop(t, ()):
+            copy.wait()
+
+    def need(self, *names):
+        for n in names:
+            if n in self.waiting:
+                self.loads[n].wait()
+                self.waiting.discard(n)
+
+    def emit(self, *names):
+        for n in names:
+            if n in self.stores:
+                self.stores[n].start()
+
+    def close(self):
+        for store in self.stores.values():
+            store.wait()
+
+
+def forward_body(r, sibling, ssem, rsem):
+    half, width = r.flat.shape
     c = lax.axis_index("ctx")
     mine = pl.ds(pl.multiple_of(c * half, 128), half)
+    theirs = pl.ds(pl.multiple_of((1 - c) * half, 128), half)
+    hidden_size = r.reduce.shape[0]
 
     def part(k):
-        return mod[:, k * width : (k + 1) * width]
-
-    normed, unused = normalize(flat[...])
-    lifted = normed * (1.0 + part(1)) + part(0)
-    lifted_low = lifted.astype(BF16)
-    xt1[...] = turned(lifted_low.astype(F32))
+        return r.mod[:, k * width : (k + 1) * width]
+
+    r.need("flat", "mod")
+    normed, unused = normalize(r.flat[...])
+    lifted_low = (normed * (1.0 + part(1)) + part(0)).astype(BF16)
+    r.need("triple")
+    r.fetch("mixing", "expand", "reduce")
     heads = head_sum_matrix(width)
-    loads[0].wait()
 
     def prepared(k):
-        values = raw[:, k * width : (k + 1) * width]
+        values = r.raw[:, k * width : (k + 1) * width]
         mean = exact_dot(values * values, heads) * (1.0 / HD)
-        scaled = values * spread_heads(lax.rsqrt(mean + 1e-06), heads) * gains[k : k + 1, :]
-        return scaled * cosine[...] + swap_pairs(scaled) * sine[...]
+        scaled = values * spread_heads(lax.rsqrt(mean + 1e-06), heads) * r.gains[k : k + 1, :]
+        return scaled * r.cosine[...] + swap_pairs(scaled) * r.sine[...]
 
     def project(k):
         return jnp.dot(
-            lifted_low, triple[:, k * width : (k + 1) * width], preferred_element_type=F32
+            lifted_low, r.triple[:, k * width : (k + 1) * width], preferred_element_type=F32
         )
 
-    raw[:, width:] = project(1)
-    kv[0, mine] = prepared(1).astype(BF16)
-    kv[1, mine] = project(2).astype(BF16)
+    r.raw[:, width:] = project(1)
+    r.need("gains", "cosine", "sine")
+    r.kv[0, mine] = prepared(1).astype(BF16)
+    r.kv[1, mine] = project(2).astype(BF16)
     share = pltpu.make_async_remote_copy(
-        kv.at[:, mine], kv.at[:, mine], ssem.at[0], rsem.at[0], device_id=sibling,
+        r.kv.at[:, mine], r.kv.at[:, mine], ssem.at[0], rsem.at[0], device_id=sibling,
         device_id_type=MESH,
     )
     share.start()
-    raw[:, :width] = project(0)
-    queries[...] = prepared(0).astype(BF16)
-    allowed = allowed_mask(seg_q, seg_k, pad_k, half)
-    mixed[...] = jnp.zeros_like(mixed)
+    r.raw[:, :width] = project(0)
+    r.emit("raw")
+    r.queries[...] = prepared(0).astype(BF16)
+    r.emit("queries")
+    r.xt1[...] = turned(lifted_low.astype(F32))
+    r.emit("xt1")
+    r.need("seg_q", "seg_k", "pad_k")
+    allowed = allowed_mask(r.seg_q, r.seg_k, r.pad_k, half)
+    r.lift[...] = jnp.zeros_like(r.lift)
     lane = lax.broadcasted_iota(jnp.int32, (half, 128), 1)
     sums = jnp.zeros((half, 128), F32)
-    theirs = pl.ds(pl.multiple_of((1 - c) * half, 128), half)
     pltpu.make_async_remote_copy(
-        kv.at[:, theirs], kv.at[:, theirs], ssem.at[0], rsem.at[0], device_id=sibling,
+        r.kv.at[:, theirs], r.kv.at[:, theirs], ssem.at[0], rsem.at[0], device_id=sibling,
         device_id_type=MESH,
     ).wait_recv()
+    r.emit("kv")
     for h in range(width // HD):
         first, unused = window(h, width)
         span = slice(first, first + 256)
         mask = head_mask(h, width, half)
-        query = jnp.where(mask, queries[:, span].astype(F32), 0.0).astype(BF16)
-        scores = dense_back(query, kv[0, :, span]) * (1.0 / math.sqrt(HD))
+        query = jnp.where(mask, r.queries[:, span].astype(F32), 0.0).astype(BF16)
+        scores = dense_back(query, r.kv[0, :, span]) * (1.0 / math.sqrt(HD))
         scores = jnp.where(allowed, scores, -1e30)
         top = jnp.max(scores, axis=1, keepdims=True)
         raised = jnp.exp(scores - top)
         total = jnp.sum(raised, axis=1, keepdims=True)
         low = (raised / total).astype(BF16)
-        out = jnp.dot(low, kv[1, :, span], preferred_element_type=F32)
-        mixed[:, span] = mixed[:, span] + jnp.where(mask, out, 0.0)
+        out = jnp.dot(low, r.kv[1, :, span], preferred_element_type=F32)
+        r.lift[:, span] = r.lift[:, span] + jnp.where(mask, out, 0.0)
         sums = jnp.where(lane == h, top + jnp.log(total), sums)
-    lse[...] = sums
-    mixed_low = mixed[...].astype(BF16)
-    xtm[...] = turned(mixed_low.astype(F32))
-    loads[1].wait()
-    attended[...] = jnp.dot(mixed_low, mixing[...], preferred_element_type=F32)
-    resid[...] = flat[...] + part(2) * attended[...]
-    normed, unused = normalize(resid[...])
+    r.lse[...] = sums
+    r.emit("lse")
+    mixed_low = r.lift[...].astype(BF16)
+    r.xtm[...] = turned(mixed_low.astype(F32))
+    r.emit("xtm")
+    r.need("mixing")
+    r.attended[...] = jnp.dot(mixed_low, r.mixing[...], preferred_element_type=F32)
+    r.emit("attended")
+    r.resid[...] = r.flat[...] + part(2) * r.attended[...]
+    r.emit("resid")
+    normed, unused = normalize(r.resid[...])
     lifted_low = (normed * (1.0 + part(4)) + part(3)).astype(BF16)
-    xt2[...] = turned(lifted_low.astype(F32))
-    feed[...] = jnp.zeros_like(feed)
-    loads[2].wait()
-    loads[3].wait()
-    hidden_size = reduce_w.shape[0]
-    xth[...] = jnp.zeros_like(xth)
+    r.xt2[...] = turned(lifted_low.astype(F32))
+    r.emit("xt2")
+    r.feed[...] = jnp.zeros_like(r.feed)
+    r.need("expand", "reduce")
+    xth = (r.xth0, r.xth1, r.xth2)
+    for g in range(3):
+        xth[g][...] = jnp.zeros_like(xth[g])
     for t in range(hidden_size // FF_TILE):
-        gate = jnp.dot(
-            lifted_low, expand[:, t * FF_TILE : (t + 1) * FF_TILE], preferred_element_type=F32
-        )
-        up = jnp.dot(
-            lifted_low,
-            expand[:, hidden_size + t * FF_TILE : hidden_size + (t + 1) * FF_TILE],
-            preferred_element_type=F32,
-        )
-        expanded[:, t * FF_TILE : (t + 1) * FF_TILE] = gate
-        expanded[:, hidden_size + t * FF_TILE : hidden_size + (t + 1) * FF_TILE] = up
+        one = slice(t * FF_TILE, (t + 1) * FF_TILE)
+        two = slice(hidden_size + t * FF_TILE, hidden_size + (t + 1) * FF_TILE)
+        gate = jnp.dot(lifted_low, r.expand[:, one], preferred_element_type=F32)
+        up = jnp.dot(lifted_low, r.expand[:, two], preferred_element_type=F32)
+        r.expanded[:, one] = gate
+        r.expanded[:, two] = up
         hidden = (gate * jax.nn.sigmoid(gate) * up).astype(BF16)
         pieces = hidden.astype(F32).T.astype(BF16).reshape(FF_TILE // 192, 3, 64, half)
         for g in range(3):
-            xth[g, t * (FF_TILE // 192) : (t + 1) * (FF_TILE // 192), :64] = pieces[:, g]
-        feed[...] = feed[...] + jnp.dot(
-            hidden, reduce_w[t * FF_TILE : (t + 1) * FF_TILE], preferred_element_type=F32
-        )
-    output[...] = resid[...] + part(5) * feed[...]
+            xth[g][t * (FF_TILE // 192) : (t + 1) * (FF_TILE // 192), :64] = pieces[:, g]
+        r.feed[...] = r.feed[...] + jnp.dot(hidden, r.reduce[one], preferred_element_type=F32)
+    r.emit("expanded", "feed", "xth0", "xth1", "xth2")
+    r.output[...] = r.resid[...] + part(5) * r.feed[...]
+    r.emit("output")
     share.wait_send()
 
 
-def backward_kernel(
-    grad_out, flat, mod, gains, cosine, sine, seg_q, seg_k, pad_k,
-    raw, queries, kv, lse, attended, resid, expanded, feed,
-    triple_h, mixing_h, expand_h, reduce_h,
-    grad_flat, grad_mod, grad_feed, grad_expanded, grad_attended, grad_projected, gains_grad,
-    triple, mixing, expand, reduce_w, grad_q, grad_k, grad_v, lift, outgoing, incoming,
-    wsem, ssem, rsem,
-):
-    half, width = flat.shape
-    loads = [
-        pltpu.make_async_copy(src, dst, wsem.at[k])
-        for k, (src, dst) in enumerate(
-            ((reduce_h, reduce_w), (expand_h, expand), (mixing_h, mixing), (triple_h, triple))
-        )
-    ]
-    for load in loads:
-        load.start()
-    sibling = meet_sibling()
+def backward_body(r, sibling, ssem, rsem):
+    half, width = r.flat.shape
     c = lax.axis_index("ctx")
     mine = pl.ds(pl.multiple_of(c * half, 128), half)
     theirs = pl.ds(pl.multiple_of((1 - c) * half, 128), half)
+    hidden_size = r.reduce.shape[0]
 
     def part(k):
-        return mod[:, k * width : (k + 1) * width]
+        return r.mod[:, k * width : (k + 1) * width]
 
     def keep(k, values):
-        grad_mod[:, k * width : (k + 1) * width] = values.astype(BF16)
-
-    keep(5, grad_out[...] * feed[...])
-    feed_low = (grad_out[...] * part(5)).astype(BF16)
-    grad_feed[...] = feed_low
-    hidden_size = reduce_w.shape[0]
-    lift[...] = jnp.zeros_like(lift)
-    loads[0].wait()
-    loads[1].wait()
+        r.grad_mod[:, k * width : (k + 1) * width] = values.astype(BF16)
+
+    r.need("grad_out", "feed", "mod")
+    keep(5, r.grad_out[...] * r.feed[...])
+    feed_low = (r.grad_out[...] * part(5)).astype(BF16)
+    r.grad_feed[...] = feed_low
+    r.emit("grad_feed")
+    r.lift[...] = jnp.zeros_like(r.lift)
     for t in range(hidden_size // FF_TILE):
+        r.need_tile(t)
+        if t == 1:
+            r.fetch("attended", "resid", "mixing", "queries", "kv", "lse", "raw", "flat", "triple")
         one = slice(t * FF_TILE, (t + 1) * FF_TILE)
         two = slice(hidden_size + t * FF_TILE, hidden_size + (t + 1) * FF_TILE)
-        grad_hidden = dense_back(feed_low, reduce_w[one])
-        gate = expanded[:, one]
-        up = expanded[:, two]
+        grad_hidden = dense_back(feed_low, r.reduce[one])
+        gate = r.expanded[:, one]
+        up = r.expanded[:, two]
         sig = jax.nn.sigmoid(gate)
         grad_gate = (grad_hidden * up * (sig * (1.0 + gate * (1.0 - sig)))).astype(BF16)
         grad_up = (grad_hidden * (gate * sig)).astype(BF16)
-        grad_expanded[:, one] = grad_gate
-        grad_expanded[:, two] = grad_up
-        lift[...] = lift[...] + dense_back(grad_gate, expand[:, one])
-        lift[...] = lift[...] + dense_back(grad_up, expand[:, two])
-    normed, inverse = normalize(resid[...])
-    keep(3, lift[...])
-    keep(4, lift[...] * normed)
-    grad_resid = grad_out[...] + norm_back(normed, inverse, lift[...] * (1.0 + part(4)))
-    keep(2, grad_resid * attended[...])
-    grad_flat[...] = grad_resid
+        r.grad_expanded[:, one] = grad_gate
+        r.grad_expanded[:, two] = grad_up
+        r.lift[...] = r.lift[...] + dense_back(grad_gate, r.expand[:, one])
+        r.lift[...] = r.lift[...] + dense_back(grad_up, r.expand[:, two])
+    r.emit("grad_expanded")
+    r.need("resid", "attended")
+    normed, inverse = normalize(r.resid[...])
+    keep(3, r.lift[...])
+    keep(4, r.lift[...] * normed)
+    grad_resid = r.grad_out[...] + norm_back(normed, inverse, r.lift[...] * (1.0 + part(4)))
+    keep(2, grad_resid * r.attended[...])
+    if "output" in r.stores:
+        r.stores.pop("output").wait()
+    r.grad_flat[...] = grad_resid
     attended_low = (grad_resid * part(2)).astype(BF16)
-    grad_attended[...] = attended_low
-    loads[2].wait()
-    lift[...] = dense_back(attended_low, mixing[...])
-    allowed = allowed_mask(seg_q, seg_k, pad_k, half)
-    grad_q[...] = jnp.zeros_like(grad_q)
-    grad_k[...] = jnp.zeros_like(grad_k)
-    grad_v[...] = jnp.zeros_like(grad_v)
+    r.grad_attended[...] = attended_low
+    r.emit("grad_attended")
+    r.need("mixing")
+    r.lift[...] = dense_back(attended_low, r.mixing[...])
+    r.need("seg_q", "seg_k", "pad_k", "queries", "kv", "lse")
+    allowed = allowed_mask(r.seg_q, r.seg_k, r.pad_k, half)
+    r.feed[...] = jnp.zeros_like(r.feed)
+    r.grad_k[...] = jnp.zeros_like(r.grad_k)
+    r.grad_v[...] = jnp.zeros_like(r.grad_v)
     scale = 1.0 / math.sqrt(HD)
     lane = lax.broadcasted_iota(jnp.int32, (half, 128), 1)
     for h in range(width // HD):
         first, unused = window(h, width)
         span = slice(first, first + 256)
         mask = head_mask(h, width, half)
-        query = jnp.where(mask, queries[:, span].astype(F32), 0.0).astype(BF16)
-        grad_mixed = jnp.where(mask, lift[:, span], 0.0).astype(BF16)
-        scores = dense_back(query, kv[0, :, span]) * scale
-        logsum = jnp.sum(jnp.where(lane == h, lse[...], 0.0), axis=1, keepdims=True)
+        query = jnp.where(mask, r.queries[:, span].astype(F32), 0.0).astype(BF16)
+        grad_mixed = jnp.where(mask, r.lift[:, span], 0.0).astype(BF16)
+        scores = dense_back(query, r.kv[0, :, span]) * scale
+        logsum = jnp.sum(jnp.where(lane == h, r.lse[...], 0.0), axis=1, keepdims=True)
         chances = jnp.exp(jnp.where(allowed, scores, -1e30) - logsum)
-        grad_chances = dense_back(grad_mixed, kv[1, :, span])
+        grad_chances = dense_back(grad_mixed, r.kv[1, :, span])
         along = jnp.sum(chances * grad_chances, axis=1, keepdims=True)
-        grad_scores = chances * (grad_chances - along)
-        scores_low = grad_scores.astype(BF16)
-        out = jnp.dot(scores_low, kv[0, :, span], preferred_element_type=F32)
-        grad_q[:, span] = grad_q[:, span] + jnp.where(mask, out, 0.0)
-        grad_k[:, span] = grad_k[:, span] + outer_sum(scores_low, query)
-        grad_v[:, span] = grad_v[:, span] + outer_sum(chances.astype(BF16), grad_mixed)
-    outgoing[0] = (grad_k[theirs, :] * scale).astype(BF16)
-    outgoing[1] = grad_v[theirs, :].astype(BF16)
+        scores_low = (chances * (grad_chances - along)).astype(BF16)
+        out = jnp.dot(scores_low, r.kv[0, :, span], preferred_element_type=F32)
+        r.feed[:, span] = r.feed[:, span] + jnp.where(mask, out, 0.0)
+        r.grad_k[:, span] = r.grad_k[:, span] + outer_sum(scores_low, query)
+        r.grad_v[:, span] = r.grad_v[:, span] + outer_sum(chances.astype(BF16), grad_mixed)
+    r.outgoing[0] = (r.grad_k[theirs, :] * scale).astype(BF16)
+    r.outgoing[1] = r.grad_v[theirs, :].astype(BF16)
     share = pltpu.make_async_remote_copy(
-        outgoing, incoming, ssem.at[0], rsem.at[0], device_id=sibling, device_id_type=MESH
+        r.outgoing, r.incoming, ssem.at[1], rsem.at[1], device_id=sibling, device_id_type=MESH
     )
     share.start()
     heads = head_sum_matrix(width)
+    r.need("raw", "gains", "cosine", "sine")
 
     def prepare_back(k, grad):
-        values = raw[:, k * width : (k + 1) * width]
-        gain = gains[k : k + 1, :]
+        values = r.raw[:, k * width : (k + 1) * width]
+        gain = r.gains[k : k + 1, :]
         mean = exact_dot(values * values, heads) * (1.0 / HD)
         inverse = spread_heads(lax.rsqrt(mean + 1e-06), heads)
         scaled = values * inverse
-        turned_back = grad * cosine[...] + swap_pairs(grad * sine[...])
-        gains_grad[k : k + 1, :] = jnp.sum(turned_back * scaled, axis=0, keepdims=True)
+        turned_back = grad * r.cosine[...] + swap_pairs(grad * r.sine[...])
+        r.gains_grad[k : k + 1, :] = jnp.sum(turned_back * scaled, axis=0, keepdims=True)
         turned_back = turned_back * gain
         along = spread_heads(exact_dot(turned_back * scaled, heads) * (1.0 / HD), heads)
         return (turned_back - scaled * along) * inverse
 
-    grad_projected[:, :width] = prepare_back(0, grad_q[...] * scale).astype(BF16)
+    r.grad_projected[:, :width] = prepare_back(0, r.feed[...] * scale).astype(BF16)
+    r.need("triple")
+    total = dense_back(r.grad_projected[:, :width], r.triple[:, :width])
     share.wait()
-    own_k = (grad_k[mine, :] * scale).astype(BF16).astype(F32) + incoming[0].astype(F32)
-    own_v = grad_v[mine, :].astype(BF16).astype(F32) + incoming[1].astype(F32)
-    grad_projected[:, width : 2 * width] = prepare_back(1, own_k).astype(BF16)
-    grad_projected[:, 2 * width :] = own_v.astype(BF16)
-    loads[3].wait()
-    total = dense_back(grad_projected[:, :width], triple[:, :width])
+    own_k = (r.grad_k[mine, :] * scale).astype(BF16).astype(F32) + r.incoming[0].astype(F32)
+    own_v = r.grad_v[mine, :].astype(BF16).astype(F32) + r.incoming[1].astype(F32)
+    r.grad_projected[:, width : 2 * width] = prepare_back(1, own_k).astype(BF16)
+    r.grad_projected[:, 2 * width :] = own_v.astype(BF16)
+    r.emit("grad_projected", "gains_grad")
     for k in (1, 2):
         span = slice(k * width, (k + 1) * width)
-        total = total + dense_back(grad_projected[:, span], triple[:, span])
-    normed, inverse = normalize(flat[...])
+        total = total + dense_back(r.grad_projected[:, span], r.triple[:, span])
+    r.need("flat")
+    normed, inverse = normalize(r.flat[...])
     keep(0, total)
     keep(1, total * normed)
-    grad_flat[...] = grad_flat[...] + norm_back(normed, inverse, total * (1.0 + part(1)))
-
-
-IN_VMEM = pl.BlockSpec(memory_space=pltpu.VMEM)
-
-
-def weight_scratch(weights):
-    return [pltpu.VMEM(w.shape, w.dtype) for w in weights]
-
-
-def kernel_forward(flat, modulation, weights, context, name):
-    cosine, sine, seg_q, seg_k, pad_k = context
-    *weights, gains = weights
-    half, width = flat.shape
-    hidden_size = weights[3].shape[0]
-
-    def struct(shape, dtype=F32):
-        return jax.ShapeDtypeStruct(shape, dtype)
-
-    rows = (16, PADDED, half)
-    out_shape = [
-        struct((half, width)),
-        struct((half, 2 * width)),
-        struct((half, width), BF16),
-        struct((2, 2 * half, width), BF16),
-        struct((half, 128)),
-        struct((half, width)),
-        struct((half, width)),
-        struct((half, 2 * hidden_size)),
-        struct((half, width)),
-        struct(rows, BF16),
-        struct(rows, BF16),
-        struct(rows, BF16),
-        struct((3,) + rows, BF16),
-    ]
-    output, *rest = pl.pallas_call(
-        forward_kernel,
+    r.emit("grad_mod")
+    r.grad_flat[...] = r.grad_flat[...] + norm_back(normed, inverse, total * (1.0 + part(1)))
+    r.emit("grad_flat")
+
+
+def block_shapes(half, width, hidden_size):
+    rows = ((16, PADDED, half), BF16)
+    token = ((half, width), F32)
+    low = ((half, width), BF16)
+    return {
+        "flat": token,
+        "mod": ((half, 6 * width), F32),
+        "gains": ((2, width), F32),
+        "cosine": token,
+        "sine": token,
+        "seg_q": ((half, 1), jnp.int32),
+        "seg_k": ((1, 2 * half), jnp.int32),
+        "pad_k": ((1, 2 * half), jnp.int32),
+        "triple": ((width, 3 * width), BF16),
+        "mixing": ((width, width), BF16),
+        "expand": ((width, 2 * hidden_size), BF16),
+        "reduce": ((hidden_size, width), BF16),
+        "output": token,
+        "raw": ((half, 2 * width), F32),
+        "queries": low,
+        "kv": ((2, 2 * half, width), BF16),
+        "lse": ((half, 128), F32),
+        "attended": token,
+        "resid": token,
+        "expanded": ((half, 2 * hidden_size), F32),
+        "feed": token,
+        "xt1": rows,
+        "xtm": rows,
+        "xt2": rows,
+        "xth0": rows,
+        "xth1": rows,
+        "xth2": rows,
+        "lift": token,
+        "grad_out": token,
+        "grad_flat": token,
+        "grad_mod": ((half, 6 * width), BF16),
+        "grad_feed": low,
+        "grad_expanded": ((half, 2 * hidden_size), BF16),
+        "grad_attended": low,
+        "grad_projected": ((half, 3 * width), BF16),
+        "gains_grad": ((2, width), F32),
+        "grad_k": ((2 * half, width), F32),
+        "grad_v": ((2 * half, width), F32),
+        "outgoing": ((2, half, width), BF16),
+        "incoming": ((2, half, width), BF16),
+    }
+
+
+WEIGHTS = ("triple", "mixing", "expand", "reduce")
+GIVEN = ("gains", "cosine", "sine", "seg_q", "seg_k", "pad_k") + WEIGHTS
+SAVED = ("raw", "queries", "kv", "lse", "attended", "resid", "expanded", "feed")
+LEFTS = ("xt1", "xtm", "xt2", "xth0", "xth1", "xth2")
+GRADS = (
+    "grad_flat", "grad_mod", "grad_feed", "grad_expanded", "grad_attended", "grad_projected",
+    "gains_grad",
+)
+WORK = ("grad_k", "grad_v", "outgoing", "incoming")
+EARLY = ("gains", "cosine", "sine", "seg_q", "seg_k", "pad_k")
+PLANS = {
+    "forward": (("flat", "mod") + GIVEN, ("output",) + SAVED + LEFTS, ("lift",)),
+    "backward": (("grad_out", "flat", "mod") + GIVEN + SAVED, GRADS, ("lift",) + WORK),
+    "both": (("grad_out", "flat", "mod") + GIVEN, ("output",) + LEFTS + GRADS, SAVED + ("lift",) + WORK),
+}
+
+
+def held_names(kind):
+    inputs, outputs, others = PLANS[kind]
+    names = inputs + outputs + others
+    return tuple(n for n in names if kind != "both" or n != "output")
+
+
+def block_kernel(kind, *refs):
+    inputs, outputs, others = PLANS[kind]
+    sources = dict(zip(inputs, refs))
+    targets = dict(zip(outputs, refs[len(inputs) :]))
+    names = held_names(kind)
+    held = dict(zip(names, refs[len(inputs) + len(outputs) :]))
+    if kind == "both":
+        held["output"] = held["grad_flat"]
+    lsem, wsem, tsem, ssem, rsem = refs[len(inputs) + len(outputs) + len(names) :]
+    r = Traffic(held, sources, targets, lsem, wsem)
+    if kind == "backward":
+        r.fetch("grad_out", "feed", "mod", *EARLY)
+        for t in range(r.reduce.shape[0] // FF_TILE):
+            r.fetch_tile(t, FF_TILE, ("reduce",), ("expanded", "expand"), tsem)
+    else:
+        r.fetch("flat", "mod", "triple", *EARLY)
+    sibling = meet_sibling()
+    if kind != "backward":
+        forward_body(r, sibling, ssem, rsem)
+    if kind == "both":
+        r.fetch("grad_out")
+        r.loads = {"grad_out": r.loads["grad_out"]}
+    if kind != "forward":
+        backward_body(r, sibling, ssem, rsem)
+    r.close()
+
+
+def run_block(kind, values, name):
+    inputs, outputs, others = PLANS[kind]
+    half, width = values["flat"].shape
+    table = block_shapes(half, width, values["reduce"].shape[0])
+    names = held_names(kind)
+    results = pl.pallas_call(
+        functools.partial(block_kernel, kind),
         name=name,
-        out_shape=out_shape,
-        in_specs=[IN_VMEM] * 8 + [ANY] * 4,
-        out_specs=[IN_VMEM] * len(out_shape),
-        scratch_shapes=weight_scratch(weights)
-        + [pltpu.VMEM((half, width), F32), DMA((4,)), DMA((1,)), DMA((1,))],
+        out_shape=[jax.ShapeDtypeStruct(*table[n]) for n in outputs],
+        in_specs=[ANY] * len(inputs),
+        out_specs=[ANY] * len(outputs),
+        scratch_shapes=[pltpu.VMEM(*table[n]) for n in names]
+        + [DMA((len(inputs),)), DMA((len(outputs),)), DMA((4, 5)), DMA((2,)), DMA((2,))],
         compiler_params=pltpu.CompilerParams(
-            collective_id=5, has_side_effects=True, vmem_limit_bytes=60 * 1024 * 1024
+            collective_id={"forward": 5, "backward": 6, "both": 7}[kind],
+            has_side_effects=True,
+            vmem_limit_bytes=63 * 1024 * 1024,
         ),
-    )(flat, modulation, gains, cosine, sine, seg_q, seg_k, pad_k, *weights)
-    return output, (flat, modulation, rest[:8]), rest[8:]
-
-
-def kernel_backward(grad_out, kept, weights, context, name):
-    cosine, sine, seg_q, seg_k, pad_k = context
-    flat, modulation, saved = kept
-    *weights, gains = weights
-    half, width = flat.shape
-    hidden_size = weights[3].shape[0]
-
-    def struct(columns, dtype=BF16):
-        return jax.ShapeDtypeStruct((half, columns), dtype)
-
-    out_shape = [
-        struct(width, F32),
-        struct(6 * width),
-        struct(width),
-        struct(2 * hidden_size),
-        struct(width),
-        struct(3 * width),
-        jax.ShapeDtypeStruct((2, width), F32),
-    ]
-    vmem = pltpu.VMEM
-    return pl.pallas_call(
-        backward_kernel,
-        name=name,
-        out_shape=out_shape,
-        in_specs=[IN_VMEM] * 17 + [ANY] * 4,
-        out_specs=[IN_VMEM] * len(out_shape),
-        scratch_shapes=weight_scratch(weights)
-        + [
-            vmem((half, width), F32),
-            vmem((2 * half, width), F32),
-            vmem((2 * half, width), F32),
-            vmem((half, width), F32),
-            vmem((2, half, width), BF16),
-            vmem((2, half, width), BF16),
-            DMA((4,)),
-            DMA((1,)),
-            DMA((1,)),
-        ],
-        compiler_params=pltpu.CompilerParams(
-            collective_id=6, has_side_effects=True, vmem_limit_bytes=60 * 1024 * 1024
-        ),
-    )(
-        grad_out, flat, modulation, gains, cosine, sine, seg_q, seg_k, pad_k, *saved, *weights
-    )
+    )(*[values[n] for n in inputs])
+    return dict(zip(outputs, results))
 
 
 def shard_rows(values):
@@ -1452,7 +1607,7 @@
     core = lax.axis_index("ctx")
     share = encoder[0].shape[1] // 2
     partial = dense(act_mine, lax.dynamic_slice_in_dim(encoder[0], core * share, share, 1))
-    partial = partial.reshape(16, 8, -1)
+    partial = partial.reshape(GRID + (8, -1))
     shards = (encoder[2], encoder[4], encoder[5], encoder[6])
     shards += (decoder[0], decoder[2], decoder[4], decoder[5], decoder[6])
     *wholes, partial = gather(shards, partial, *gather_units(shards), 1, "gather")
@@ -1468,39 +1623,42 @@
         jnp.concatenate([others, partial], axis=1),
     )
     modulation_rows = modulation_rows + encoder_offset
-    exact = lax.Precision.HIGHEST
-    encoder_modulation = jnp.dot(picks, modulation_rows, precision=exact)
+
+    def pick(rows):
+        return sum(jnp.where(picks[:, j : j + 1] > 0, rows[j], 0.0) for j in range(segments))
+
+    encoder_modulation = pick(modulation_rows)
     cond_rows = lax.dynamic_slice_in_dim(all_cond, me * segments, segments, 0)
-    cond = jnp.dot(picks, cond_rows, precision=exact)
-
-    encoder_out, encoder_kept, encoder_left = kernel_forward(
-        flat, encoder_modulation, encoder_weights, context, "encoder"
-    )
-    latent_full = valid * encoder_out
+    cond = pick(cond_rows)
+
+    shared = dict(zip(("cosine", "sine", "seg_q", "seg_k", "pad_k"), context), flat=flat)
+    encoder_in = dict(zip(WEIGHTS + ("gains",), encoder_weights), mod=encoder_modulation, **shared)
+    forward = run_block("forward", encoder_in, "encoder")
+    latent_full = valid * forward["output"]
     decoder_pre = latent_full + cond
     decoder_act = jax.nn.silu(decoder_pre).astype(BF16)
 
     decoder_modulation = dense(decoder_act, modulate) + decoder_offset
-    decoder_out, decoder_kept, decoder_left = kernel_forward(
-        flat, decoder_modulation, decoder_weights, context, "decoder"
-    )
-    velocity = valid * decoder_out
-
-    def pair_up(lefts, rights):
-        feed, expanded, attended, projected = rights
-        one, mixed, two, hidden = lefts
+    decoder_in = dict(
+        zip(WEIGHTS + ("gains",), decoder_weights),
+        mod=decoder_modulation,
+        grad_out=valid * cotangent,
+        **shared,
+    )
+    both = run_block("both", decoder_in, "decoder")
+    velocity = valid * both["output"]
+
+    def pair_up(lefts, grads):
         return (
-            ([one], projected),
-            ([mixed], attended),
-            ([two], expanded),
-            ([hidden[g] for g in range(3)], feed),
+            ([lefts["xt1"]], grads["grad_projected"]),
+            ([lefts["xtm"]], grads["grad_attended"]),
+            ([lefts["xt2"]], grads["grad_expanded"]),
+            ([lefts["xth0"], lefts["xth1"], lefts["xth2"]], grads["grad_feed"]),
         )
 
-    grad_out = valid * cotangent
-    decoder_flat, grad_modulation, *rights, gains_grad = kernel_backward(
-        grad_out, decoder_kept, decoder_weights, context, "decoder_back"
-    )
-    factors = pair_up(decoder_left, rights)
+    factors = pair_up(both, both)
+    grad_modulation = both["grad_mod"]
+    gains_grad = both["gains_grad"]
     grad_act = dense_back(grad_modulation, modulate)
     unused_silu, silu_pull = jax.vjp(jax.nn.silu, decoder_pre)
     grad_latent = valid * silu_pull(grad_act)[0]
@@ -1513,12 +1671,13 @@
         axis=1,
     )
     first = ([shard_rows(decoder_act)], grad_modulation)
-    decoder_block = ((first,) + factors, extra)
-
-    encoder_flat, grad_modulation, *rights, gains_grad = kernel_backward(
-        grad_latent, encoder_kept, encoder_weights, context, "encoder_back"
-    )
-    factors = pair_up(encoder_left, rights)
+    decoder_block = ((factors[1], factors[0], factors[2], first, factors[3]), extra)
+
+    encoder_in["grad_out"] = grad_latent
+    backward = run_block("backward", {**encoder_in, **forward}, "encoder_back")
+    factors = pair_up(forward, backward)
+    grad_modulation = backward["grad_mod"]
+    gains_grad = backward["gains_grad"]
     grad_rows = lax.dot_general(
         picks.astype(BF16), grad_modulation, (((0,), (0,)), ((), ())), preferred_element_type=F32
     )
@@ -1529,12 +1688,12 @@
     )
     (grads, small), (encoder_parts, encoder_small) = results
     decoder_grads = (
-        grads[0],
+        grads[3],
         small[:offset_size],
         grads[1],
         small[offset_size:].reshape(2, -1),
+        grads[0],
         grads[2],
-        grads[3],
         grads[4],
     )
     all_rows = all_rows.reshape(16 * segments, -1)
@@ -1551,7 +1710,8 @@
         encoder_parts[2],
         encoder_parts[3],
     )
-    return velocity, latent_full, decoder_flat + encoder_flat, encoder_grads, decoder_grads
+    token_grad = both["grad_flat"] + backward["grad_flat"]
+    return velocity, latent_full, token_grad, encoder_grads, decoder_grads
 
 
 def plain_gather(block):

time: 856 us -> 811 us (0.947)
  Pallas kernels: 784 us -> 741 us
    pallas_call x4 -> x3, Pallas kernels: 122 us -> 102 us  [run_block(): pl.pallas_call(functools.partial(block_kernel, kind), name=name, out_shap...]
    pallas_call x1, Pallas kernels: 324 us -> 305 us  [gather(): pl.pallas_call(functools.partial(gather_kernel, units, turns, count), nam...]
where the time goes in v5:
time: 811 us; the launch traced here: 806 us
  Pallas kernels  741 us (91%)
  matrix products  28.1 us (3%)
  local copies, waits for them, and re-layouts  23.5 us (3%)
  other arithmetic  11.3 us (1%)
    pallas_call x1, Pallas kernels, scatter(): pl.pallas_call(functools.partial(scatter_kernel, tuple(first), tuple(cols...  319 us
    pallas_call x1, Pallas kernels, gather(): pl.pallas_call(functools.partial(gather_kernel, units, turns, count), nam...  305 us
    pallas_call x3, Pallas kernels, run_block(): pl.pallas_call(functools.partial(block_kernel, kind), name=name, out_shap...  102 us
  transfers between devices with their start and end apart: 2, of which 0 were waited for; matrix products, arithmetic and copies ran while one was open for 2% of the time, Pallas kernels for 0%

profile of v5, /device:TPU:0, one launch (start us, length us, event | category | flops | bytes accessed | tf_op | source)
XLA Modules:
  0.0 806.0 jit_solution(16554642714511176660)
XLA Ops:
  0.7 0.7 reshape.285
  1.4 0.7 reshape.287
  2.8 1.5 concatenate.21
  4.9 10.7 %small.1 = f32[16,16,128]{2,1,0:T(8,128)} custom-call(f32[16,128]{1,0:T(8,128)} %pad_bitcast_fusion.in_ref), custom_call_target="tpu_custom_call" | custom-call | tf_op jit(solution)/shard_map/small/pallas_call | solution.py:404
  15.6 0.9 copy.65
  17.3 1.4 fusion.3
  18.7 1.2 reshape.249.refs_9_
  19.9 305.4 %gather.1 = (bf16[4,2,2,72,3456]{4,3,2,1,0:T(8,128)(2,1)}, bf16[4,2,2,72,1152]{4,3,2,1,0:T(8,128)(2,1)}, bf16[4,2,2,72,6144]{4,3,2,1,0:T(8,128)(2,1)}, bf16[4,2,...) custom-call(bf16[72,3456]{1,0:T(8,128)(2,1)} %refs_0_.1, ...), custom_call_target="tpu_custom_call" | custom-call | tf_op jit(solution)/shard_map/gather/pallas_call | solution.py:324
  325.3 1.0 reduce_sum.27
  327.8 0.9 bitcast_convert_fusion.refs_0_.refs_1_
  328.8 0.9 convert_multiply_fusion.refs_0_
  329.9 1.1 copy.49.refs_4_.refs_5_
  331.0 1.1 copy.48.refs_3_.refs_4_
  332.1 0.7 copy.50.refs_5_.refs_6_
  334.8 3.3 select_add_fusion.refs_1_.refs_2_
  338.1 22.8 %encoder.1 = (f32[128,1152]{1,0:T(8,128)}, f32[128,2304]{1,0:T(8,128)}, bf16[128,1152]{1,0:T(8,128)(2,1)}, bf16[2,256,1152]{2,1,0:T(8,128)(2,1)}, f32[128,128]{1...) custom-call(f32[128,1152]{1,0:T(8,128)} %bitcast_convert_fusion.refs, ...), custom_call_target="tpu_custom_call" | custom-call | tf_op jit(solution)/shard_map/encoder/pallas_call | solution.py:1461
  360.9 10.5 %convolution_add_fusion.refs_2_ = f32[128,6912]{1,0:T(8,128)} fusion(bf16[1152,6912]{1,0:T(8,128)(2,1)} %bitcast.100, f32[6912]{0:T(1024)S(1)} %add.103, f32[128,1152]{1,0:T(8,128)} %get-tuple-element.79, f32[1152]{0:T(1024)S(1)} %get-tuple-element.138, f32[1152]{0:T(1024)S(1)} %get-tuple-element.136, f32[1152]{0:T(1024)S(1)} %get-tuple-element.137, ...), kind=kOutput, calls=%fused_computation | convolution fusion | flops 2041380864 | bytes 20101120 | tf_op jit(solution)/shard_map/dot_general | solution.py:843
  371.4 45.3 %decoder.1 = (f32[128,1152]{1,0:T(8,128)}, bf16[16,80,128]{2,1,0:T(8,128)(2,1)}, bf16[16,80,128]{2,1,0:T(8,128)(2,1)}, bf16[16,80,128]{2,1,0:T(8,128)(2,1)}, bf1...) custom-call(f32[128,1152]{1,0:T(8,128)} %convert_multiply_fusion.ref, ...), custom_call_target="tpu_custom_call" | custom-call | tf_op jit(solution)/shard_map/decoder/pallas_call | solution.py:1461
  416.7 12.5 %fusion.27 = (bf16[1152,128]{0,1:T(8,128)(2,1)S(1)}, f32[128,1152]{1,0:T(8,128)}, bf16[1,128,1152]{2,1,0:T(8,128)(2,1)}, bf16[1,128,1152]{2,1,0:T(8,128)(2,1)}) fusion(f32[1152]{0:T(1024)S(1)} %get-tuple-element.138, pred[128]{0:T(512)(128)(4,1)S(1)} %get-tuple-element.149, f32[1152]{0:T(1024)S(1)} %get-tuple-element.136, ...), kind=kOutput, calls=%fused_computation.81 | convolution fusion | flops 2041970688 | bytes 20368384 | tf_op jit(solution)/shard_map/dot_general | solution.py:847
  429.2 33.5 %encoder_back.1 = (f32[128,1152]{1,0:T(8,128)}, bf16[128,6912]{1,0:T(8,128)(2,1)}, bf16[128,1152]{1,0:T(8,128)(2,1)}, bf16[128,6144]{1,0:T(8,128)(2,1)}, bf16[12...) custom-call(f32[128,1152]{1,0:T(8,128)} %get-tuple-element.140.refs_0_, ...), custom_call_target="tpu_custom_call" | custom-call | tf_op jit(solution)/shard_map/encoder_back/pallas_call | solution.py:1461
  462.8 1.9 fusion.16
  464.9 1.8 reduce
  467.0 0.9 add_bitcast_fusion
  468.0 0.8 pad.29.refs_7_
  469.0 0.8 pad.31.refs_14_
  470.0 0.8 pad.27.refs_3_
  470.8 0.7 reshape.276.refs_26_
  471.6 318.9 %scatter.1 = (f32[72,36096]{1,0:T(8,128)}, bf16[4,2,2,16,1728]{4,3,2,1,0:T(8,128)(2,1)}) custom-call(bf16[16,80,128]{2,1,0:T(8,128)(2,1)} %get-tuple-element.97.refs_0_, bf16[16,80,128]{2,1,0:T(8,128)(2,1)} %get-tuple-element.98.refs_1_, bf16[16,80,128]{2,1,0:T(8,128)(2,1)} %get-tuple-element.99.refs_2_, bf16[16,80,128]{2,1,0:T(8,128)(2,1)} %pad.27.refs_3_, ...), custom_call_target="tpu_custom_call" | custom-call | tf_op jit(solution)/shard_map/scatter/pallas_call | solution.py:737
  790.5 2.1 reshape.277
  792.6 1.9 fusion.26
  794.6 3.9 copy-done
  798.5 4.7 split.1
  (84 shorter events, 9.7 us)
Async XLA Ops:
  19.9 307.7 %copy-start.5 = (s32[1,256]{1,0:T(1,128)S(1)}, s32[1,256]{1,0:T(1,128)}, u32[]{:S(2)}) copy-start(s32[1,256]{1,0:T(1,128)} %refs_7_.7) | copy-start | bytes 3076
  19.9 307.7 %copy-start.9 = (s32[1,256]{1,0:T(1,128)S(1)}, s32[1,256]{1,0:T(1,128)}, u32[]{:S(2)}) copy-start(s32[1,256]{1,0:T(1,128)} %param.24) | copy-start | bytes 3076
  19.9 307.7 %copy-start.10 = (s32[1,256]{1,0:T(1,128)S(1)}, s32[1,256]{1,0:T(1,128)}, u32[]{:S(2)}) copy-start(s32[1,256]{1,0:T(1,128)} %param.25) | copy-start | bytes 3076
  19.9 307.9 %copy-start.3 = (bf16[1,128,1152]{2,1,0:T(8,128)(2,1)S(1)}, bf16[1,128,1152]{2,1,0:T(8,128)(2,1)}, u32[]{:S(2)}) copy-start(bf16[1,128,1152]{2,1,0:T(8,128)(2,1)} %param.21) | copy-start | bytes 884740
  19.9 308.9 %copy-start.6 = (s32[1,256]{1,0:T(1,128)S(1)}, s32[1,256]{1,0:T(1,128)}, u32[]{:S(2)}) copy-start(s32[1,256]{1,0:T(1,128)} %refs_8_.5) | copy-start | bytes 3076
  19.9 309.0 %copy-start.4 = (bf16[1,128,1152]{2,1,0:T(8,128)(2,1)S(1)}, bf16[1,128,1152]{2,1,0:T(8,128)(2,1)}, u32[]{:S(2)}) copy-start(bf16[1,128,1152]{2,1,0:T(8,128)(2,1)} %param.22) | copy-start | bytes 884740
  326.4 8.1 %collective-permute-start = (f32[4,3456]{1,0:T(4,128)S(1)}, f32[4,3456]{1,0:T(4,128)S(1)}, u32[]{:S(2)}, u32[]{:S(2)}) collective-permute-start(f32[4,3456]{1,0:T(4,128)S(1)} %reshape.250), channel_id=1, source_target_pairs={{0,1},{1,0},{2,3},{3,2},{4,5},{5,4},{6,7},{7,6},{8,9},{9,8},{10,11... | collective-permute-start | bytes 165896 | tf_op jit(solution)/shard_map/ppermute | solution.py:1619
  462.7 4.1 copy-start.7
  462.7 4.3 copy-start.1
  462.8 4.3 copy-start.2
  462.8 6.0 copy-start.8
  464.7 6.1 collective-permute-start.1
  794.6 4.0 copy-start

commit v6 on v5

--- a/solution.py
+++ b/solution.py
@@ -1,3 +1,4 @@
+import enum
 import functools
 import math
 
@@ -1080,6 +1081,123 @@
     return (seg_q[...] == seg_k[...]) & ((pad_k[...] == 0) | (place_q == place_k))
 
 
+MOD_TILE = 768
+
+
+def weight_tiles(weight, held, sem):
+    tiles = []
+    for t in range(weight.shape[1] // MOD_TILE):
+        span = slice(t * MOD_TILE, (t + 1) * MOD_TILE)
+        copy = pltpu.make_async_copy(
+            weight.at[:, pl.ds(t * MOD_TILE, MOD_TILE)],
+            held.at[:, pl.ds(t * MOD_TILE, MOD_TILE)],
+            sem.at[t],
+        )
+        copy.start()
+        tiles.append((span, copy))
+    return tiles
+
+
+def modulation_kernel(block, valid, cond, offset, weight, mod, before, latent, xt, held, sem):
+    tiles = weight_tiles(weight, held, sem)
+    kept = block[...] * valid[...]
+    latent[...] = kept.astype(BF16)
+    total = kept + cond[...]
+    before[...] = total
+    act = (total * jax.nn.sigmoid(total)).astype(BF16)
+    xt[...] = turned(act.astype(F32))
+    for span, copy in tiles:
+        copy.wait()
+        part = jnp.dot(act, held[:, span], preferred_element_type=F32)
+        mod[:, span] = part + offset[:, span]
+
+
+def modulation_back_kernel(grad, valid, before, weight, out, held, sem):
+    tiles = weight_tiles(weight, held, sem)
+    out[...] = jnp.zeros_like(out)
+    for span, copy in tiles:
+        copy.wait()
+        out[...] = out[...] + dense_back(grad[:, span], held[:, span])
+    sig = jax.nn.sigmoid(before[...])
+    out[...] = valid[...] * (out[...] * (sig * (1.0 + before[...] * (1.0 - sig))))
+
+
+def modulation_call(kernel, name, inputs, weight, outs):
+    in_vmem = pl.BlockSpec(memory_space=pltpu.VMEM)
+    return pl.pallas_call(
+        kernel,
+        name=name,
+        out_shape=outs,
+        in_specs=[in_vmem] * len(inputs) + [ANY],
+        out_specs=[in_vmem] * len(outs),
+        scratch_shapes=[pltpu.VMEM(weight.shape, BF16), DMA((weight.shape[1] // MOD_TILE,))],
+        compiler_params=pltpu.CompilerParams(vmem_limit_bytes=62 * 1024 * 1024),
+    )(*inputs, weight)
+
+
+def decoder_modulation_of(block, valid, cond, offset, weight):
+    rows, width = block.shape
+    outs = [
+        jax.ShapeDtypeStruct((rows, weight.shape[1]), F32),
+        jax.ShapeDtypeStruct((rows, width), F32),
+        jax.ShapeDtypeStruct((rows, width), BF16),
+        jax.ShapeDtypeStruct((16, PADDED, rows), BF16),
+    ]
+    inputs = (block, valid, cond, offset.reshape(1, -1))
+    return modulation_call(modulation_kernel, "modulation", inputs, weight, outs)
+
+
+def modulation_back(grad, valid, before, weight):
+    outs = [jax.ShapeDtypeStruct(before.shape, F32)]
+    return modulation_call(
+        modulation_back_kernel, "modulation_back", (grad, valid, before), weight, outs
+    )[0]
+
+
+class A(enum.IntEnum):
+    flat = 1
+    mod = 2
+    gains = 3
+    cosine = 4
+    sine = 5
+    seg_q = 6
+    seg_k = 7
+    pad_k = 8
+    triple = 9
+    mixing = 10
+    expand = 11
+    reduce = 12
+    output = 13
+    raw = 14
+    queries = 15
+    kv = 16
+    lse = 17
+    attended = 18
+    resid = 19
+    expanded = 20
+    feed = 21
+    xt1 = 22
+    xtm = 23
+    xt2 = 24
+    xth0 = 25
+    xth1 = 26
+    xth2 = 27
+    lift = 28
+    grad_out = 29
+    grad_flat = 30
+    grad_mod = 31
+    grad_feed = 32
+    grad_expanded = 33
+    grad_attended = 34
+    grad_projected = 35
+    gains_grad = 36
+    grad_v = 38
+    outgoing = 39
+    incoming = 40
+    marks = 41
+    mark_sums = 42
+
+
 class Traffic:
     def __init__(self, held, sources, targets, lsem, ssem):
         self.held = held
@@ -1089,6 +1207,7 @@
         }
         self.sources = sources
         self.tiles = {}
+        self.more = None
         self.stores = {
             n: pltpu.make_async_copy(held[n], targets[n], ssem.at[k])
             for k, n in enumerate(targets)
@@ -1096,14 +1215,14 @@
         self.waiting = set(names)
 
     def __getattr__(self, name):
-        return self.held[name]
+        return self.held[A[name]]
 
     def fetch(self, *names):
         for n in names:
             if n in self.loads:
                 self.loads[n].start()
 
-    def fetch_tile(self, t, size, rows, columns, sem):
+    def fetch_tile(self, size, rows, columns, sem, t):
         spans = [(n, (pl.ds(t * size, size), slice(None))) for n in rows]
         for n in columns:
             for first in (0, self.held[n].shape[1] // 2):
@@ -1146,11 +1265,11 @@
     def part(k):
         return r.mod[:, k * width : (k + 1) * width]
 
-    r.need("flat", "mod")
+    r.need(A.flat, A.mod)
     normed, unused = normalize(r.flat[...])
     lifted_low = (normed * (1.0 + part(1)) + part(0)).astype(BF16)
-    r.need("triple")
-    r.fetch("mixing", "expand", "reduce")
+    r.need(A.triple)
+    r.fetch(A.mixing, A.expand, A.reduce)
     heads = head_sum_matrix(width)
 
     def prepared(k):
@@ -1165,7 +1284,7 @@
         )
 
     r.raw[:, width:] = project(1)
-    r.need("gains", "cosine", "sine")
+    r.need(A.gains, A.cosine, A.sine)
     r.kv[0, mine] = prepared(1).astype(BF16)
     r.kv[1, mine] = project(2).astype(BF16)
     share = pltpu.make_async_remote_copy(
@@ -1174,12 +1293,12 @@
     )
     share.start()
     r.raw[:, :width] = project(0)
-    r.emit("raw")
+    r.emit(A.raw)
     r.queries[...] = prepared(0).astype(BF16)
-    r.emit("queries")
+    r.emit(A.queries)
     r.xt1[...] = turned(lifted_low.astype(F32))
-    r.emit("xt1")
-    r.need("seg_q", "seg_k", "pad_k")
+    r.emit(A.xt1)
+    r.need(A.seg_q, A.seg_k, A.pad_k)
     allowed = allowed_mask(r.seg_q, r.seg_k, r.pad_k, half)
     r.lift[...] = jnp.zeros_like(r.lift)
     lane = lax.broadcasted_iota(jnp.int32, (half, 128), 1)
@@ -1188,7 +1307,7 @@
         r.kv.at[:, theirs], r.kv.at[:, theirs], ssem.at[0], rsem.at[0], device_id=sibling,
         device_id_type=MESH,
     ).wait_recv()
-    r.emit("kv")
+    r.emit(A.kv)
     for h in range(width // HD):
         first, unused = window(h, width)
         span = slice(first, first + 256)
@@ -1204,21 +1323,21 @@
         r.lift[:, span] = r.lift[:, span] + jnp.where(mask, out, 0.0)
         sums = jnp.where(lane == h, top + jnp.log(total), sums)
     r.lse[...] = sums
-    r.emit("lse")
+    r.emit(A.lse)
     mixed_low = r.lift[...].astype(BF16)
     r.xtm[...] = turned(mixed_low.astype(F32))
-    r.emit("xtm")
-    r.need("mixing")
+    r.emit(A.xtm)
+    r.need(A.mixing)
     r.attended[...] = jnp.dot(mixed_low, r.mixing[...], preferred_element_type=F32)
-    r.emit("attended")
+    r.emit(A.attended)
     r.resid[...] = r.flat[...] + part(2) * r.attended[...]
-    r.emit("resid")
+    r.emit(A.resid)
     normed, unused = normalize(r.resid[...])
     lifted_low = (normed * (1.0 + part(4)) + part(3)).astype(BF16)
     r.xt2[...] = turned(lifted_low.astype(F32))
-    r.emit("xt2")
+    r.emit(A.xt2)
     r.feed[...] = jnp.zeros_like(r.feed)
-    r.need("expand", "reduce")
+    r.need(A.expand, A.reduce)
     xth = (r.xth0, r.xth1, r.xth2)
     for g in range(3):
         xth[g][...] = jnp.zeros_like(xth[g])
@@ -1234,9 +1353,9 @@
         for g in range(3):
             xth[g][t * (FF_TILE // 192) : (t + 1) * (FF_TILE // 192), :64] = pieces[:, g]
         r.feed[...] = r.feed[...] + jnp.dot(hidden, r.reduce[one], preferred_element_type=F32)
-    r.emit("expanded", "feed", "xth0", "xth1", "xth2")
+    r.emit(A.expanded, A.feed, A.xth0, A.xth1, A.xth2)
     r.output[...] = r.resid[...] + part(5) * r.feed[...]
-    r.emit("output")
+    r.emit(A.output)
     share.wait_send()
 
 
@@ -1253,16 +1372,18 @@
     def keep(k, values):
         r.grad_mod[:, k * width : (k + 1) * width] = values.astype(BF16)
 
-    r.need("grad_out", "feed", "mod")
+    r.need(A.grad_out, A.feed, A.mod)
     keep(5, r.grad_out[...] * r.feed[...])
     feed_low = (r.grad_out[...] * part(5)).astype(BF16)
     r.grad_feed[...] = feed_low
-    r.emit("grad_feed")
+    r.emit(A.grad_feed)
     r.lift[...] = jnp.zeros_like(r.lift)
     for t in range(hidden_size // FF_TILE):
         r.need_tile(t)
-        if t == 1:
-            r.fetch("attended", "resid", "mixing", "queries", "kv", "lse", "raw", "flat", "triple")
+        if r.more and t + 2 < hidden_size // FF_TILE:
+            r.more(t + 2)
+        if t == 2:
+            r.fetch(A.attended, A.resid, A.mixing, A.queries, A.kv, A.lse, A.raw, A.flat, A.triple)
         one = slice(t * FF_TILE, (t + 1) * FF_TILE)
         two = slice(hidden_size + t * FF_TILE, hidden_size + (t + 1) * FF_TILE)
         grad_hidden = dense_back(feed_low, r.reduce[one])
@@ -1275,25 +1396,26 @@
         r.grad_expanded[:, two] = grad_up
         r.lift[...] = r.lift[...] + dense_back(grad_gate, r.expand[:, one])
         r.lift[...] = r.lift[...] + dense_back(grad_up, r.expand[:, two])
-    r.emit("grad_expanded")
-    r.need("resid", "attended")
+    r.emit(A.grad_expanded)
+    r.need(A.resid, A.attended)
     normed, inverse = normalize(r.resid[...])
     keep(3, r.lift[...])
     keep(4, r.lift[...] * normed)
     grad_resid = r.grad_out[...] + norm_back(normed, inverse, r.lift[...] * (1.0 + part(4)))
     keep(2, grad_resid * r.attended[...])
-    if "output" in r.stores:
-        r.stores.pop("output").wait()
+    if A.output in r.stores:
+        r.stores.pop(A.output).wait()
     r.grad_flat[...] = grad_resid
     attended_low = (grad_resid * part(2)).astype(BF16)
     r.grad_attended[...] = attended_low
-    r.emit("grad_attended")
-    r.need("mixing")
+    r.emit(A.grad_attended)
+    r.need(A.mixing)
     r.lift[...] = dense_back(attended_low, r.mixing[...])
-    r.need("seg_q", "seg_k", "pad_k", "queries", "kv", "lse")
+    r.need(A.seg_q, A.seg_k, A.pad_k, A.queries, A.kv, A.lse)
     allowed = allowed_mask(r.seg_q, r.seg_k, r.pad_k, half)
     r.feed[...] = jnp.zeros_like(r.feed)
-    r.grad_k[...] = jnp.zeros_like(r.grad_k)
+    r.resid[...] = jnp.zeros_like(r.resid)
+    r.attended[...] = jnp.zeros_like(r.attended)
     r.grad_v[...] = jnp.zeros_like(r.grad_v)
     scale = 1.0 / math.sqrt(HD)
     lane = lax.broadcasted_iota(jnp.int32, (half, 128), 1)
@@ -1311,16 +1433,19 @@
         scores_low = (chances * (grad_chances - along)).astype(BF16)
         out = jnp.dot(scores_low, r.kv[0, :, span], preferred_element_type=F32)
         r.feed[:, span] = r.feed[:, span] + jnp.where(mask, out, 0.0)
-        r.grad_k[:, span] = r.grad_k[:, span] + outer_sum(scores_low, query)
+        part_k = outer_sum(scores_low, query)
+        r.resid[:, span] = r.resid[:, span] + part_k[:half]
+        r.attended[:, span] = r.attended[:, span] + part_k[half:]
         r.grad_v[:, span] = r.grad_v[:, span] + outer_sum(chances.astype(BF16), grad_mixed)
-    r.outgoing[0] = (r.grad_k[theirs, :] * scale).astype(BF16)
+    their_k = jnp.where(c == 0, r.attended[...], r.resid[...])
+    r.outgoing[0] = (their_k * scale).astype(BF16)
     r.outgoing[1] = r.grad_v[theirs, :].astype(BF16)
     share = pltpu.make_async_remote_copy(
         r.outgoing, r.incoming, ssem.at[1], rsem.at[1], device_id=sibling, device_id_type=MESH
     )
     share.start()
     heads = head_sum_matrix(width)
-    r.need("raw", "gains", "cosine", "sine")
+    r.need(A.raw, A.gains, A.cosine, A.sine)
 
     def prepare_back(k, grad):
         values = r.raw[:, k * width : (k + 1) * width]
@@ -1335,24 +1460,32 @@
         return (turned_back - scaled * along) * inverse
 
     r.grad_projected[:, :width] = prepare_back(0, r.feed[...] * scale).astype(BF16)
-    r.need("triple")
+    r.need(A.triple)
     total = dense_back(r.grad_projected[:, :width], r.triple[:, :width])
     share.wait()
-    own_k = (r.grad_k[mine, :] * scale).astype(BF16).astype(F32) + r.incoming[0].astype(F32)
+    own_k = jnp.where(c == 0, r.resid[...], r.attended[...]) * scale
+    own_k = own_k.astype(BF16).astype(F32) + r.incoming[0].astype(F32)
     own_v = r.grad_v[mine, :].astype(BF16).astype(F32) + r.incoming[1].astype(F32)
     r.grad_projected[:, width : 2 * width] = prepare_back(1, own_k).astype(BF16)
     r.grad_projected[:, 2 * width :] = own_v.astype(BF16)
-    r.emit("grad_projected", "gains_grad")
+    r.emit(A.grad_projected, A.gains_grad)
     for k in (1, 2):
         span = slice(k * width, (k + 1) * width)
         total = total + dense_back(r.grad_projected[:, span], r.triple[:, span])
-    r.need("flat")
+    r.need(A.flat)
     normed, inverse = normalize(r.flat[...])
     keep(0, total)
     keep(1, total * normed)
-    r.emit("grad_mod")
+    r.emit(A.grad_mod)
+    r.need(A.marks)
+    for k in range(6):
+        span = slice(k * width, (k + 1) * width)
+        r.mark_sums[:, span] = jnp.dot(
+            r.marks[...], r.grad_mod[:, span], preferred_element_type=F32
+        )
+    r.emit(A.mark_sums)
     r.grad_flat[...] = r.grad_flat[...] + norm_back(normed, inverse, total * (1.0 + part(1)))
-    r.emit("grad_flat")
+    r.emit(A.grad_flat)
 
 
 def block_shapes(half, width, hidden_size):
@@ -1360,70 +1493,71 @@
     token = ((half, width), F32)
     low = ((half, width), BF16)
     return {
-        "flat": token,
-        "mod": ((half, 6 * width), F32),
-        "gains": ((2, width), F32),
-        "cosine": token,
-        "sine": token,
-        "seg_q": ((half, 1), jnp.int32),
-        "seg_k": ((1, 2 * half), jnp.int32),
-        "pad_k": ((1, 2 * half), jnp.int32),
-        "triple": ((width, 3 * width), BF16),
-        "mixing": ((width, width), BF16),
-        "expand": ((width, 2 * hidden_size), BF16),
-        "reduce": ((hidden_size, width), BF16),
-        "output": token,
-        "raw": ((half, 2 * width), F32),
-        "queries": low,
-        "kv": ((2, 2 * half, width), BF16),
-        "lse": ((half, 128), F32),
-        "attended": token,
-        "resid": token,
-        "expanded": ((half, 2 * hidden_size), F32),
-        "feed": token,
-        "xt1": rows,
-        "xtm": rows,
-        "xt2": rows,
-        "xth0": rows,
-        "xth1": rows,
-        "xth2": rows,
-        "lift": token,
-        "grad_out": token,
-        "grad_flat": token,
-        "grad_mod": ((half, 6 * width), BF16),
-        "grad_feed": low,
-        "grad_expanded": ((half, 2 * hidden_size), BF16),
-        "grad_attended": low,
-        "grad_projected": ((half, 3 * width), BF16),
-        "gains_grad": ((2, width), F32),
-        "grad_k": ((2 * half, width), F32),
-        "grad_v": ((2 * half, width), F32),
-        "outgoing": ((2, half, width), BF16),
-        "incoming": ((2, half, width), BF16),
+        A.flat: token,
+        A.mod: ((half, 6 * width), F32),
+        A.gains: ((2, width), F32),
+        A.cosine: token,
+        A.sine: token,
+        A.seg_q: ((half, 1), jnp.int32),
+        A.seg_k: ((1, 2 * half), jnp.int32),
+        A.pad_k: ((1, 2 * half), jnp.int32),
+        A.triple: ((width, 3 * width), BF16),
+        A.mixing: ((width, width), BF16),
+        A.expand: ((width, 2 * hidden_size), BF16),
+        A.reduce: ((hidden_size, width), BF16),
+        A.output: token,
+        A.raw: ((half, 2 * width), F32),
+        A.queries: low,
+        A.kv: ((2, 2 * half, width), BF16),
+        A.lse: ((half, 128), F32),
+        A.attended: token,
+        A.resid: token,
+        A.expanded: ((half, 2 * hidden_size), F32),
+        A.feed: token,
+        A.xt1: rows,
+        A.xtm: rows,
+        A.xt2: rows,
+        A.xth0: rows,
+        A.xth1: rows,
+        A.xth2: rows,
+        A.lift: token,
+        A.grad_out: token,
+        A.grad_flat: token,
+        A.grad_mod: ((half, 6 * width), BF16),
+        A.grad_feed: low,
+        A.grad_expanded: ((half, 2 * hidden_size), BF16),
+        A.grad_attended: low,
+        A.grad_projected: ((half, 3 * width), BF16),
+        A.gains_grad: ((2, width), F32),
+        A.grad_v: ((2 * half, width), F32),
+        A.outgoing: ((2, half, width), BF16),
+        A.incoming: ((2, half, width), BF16),
+        A.marks: ((8, half), BF16),
+        A.mark_sums: ((8, 6 * width), F32),
     }
 
 
-WEIGHTS = ("triple", "mixing", "expand", "reduce")
-GIVEN = ("gains", "cosine", "sine", "seg_q", "seg_k", "pad_k") + WEIGHTS
-SAVED = ("raw", "queries", "kv", "lse", "attended", "resid", "expanded", "feed")
-LEFTS = ("xt1", "xtm", "xt2", "xth0", "xth1", "xth2")
+WEIGHTS = (A.triple, A.mixing, A.expand, A.reduce)
+GIVEN = (A.gains, A.cosine, A.sine, A.seg_q, A.seg_k, A.pad_k) + WEIGHTS
+SAVED = (A.raw, A.queries, A.kv, A.lse, A.attended, A.resid, A.expanded, A.feed)
+LEFTS = (A.xt1, A.xtm, A.xt2, A.xth0, A.xth1, A.xth2)
 GRADS = (
-    "grad_flat", "grad_mod", "grad_feed", "grad_expanded", "grad_attended", "grad_projected",
-    "gains_grad",
+    A.grad_flat, A.grad_mod, A.grad_feed, A.grad_expanded, A.grad_attended, A.grad_projected,
+    A.gains_grad, A.mark_sums,
 )
-WORK = ("grad_k", "grad_v", "outgoing", "incoming")
-EARLY = ("gains", "cosine", "sine", "seg_q", "seg_k", "pad_k")
+WORK = (A.grad_v, A.outgoing, A.incoming)
+EARLY = (A.gains, A.cosine, A.sine, A.seg_q, A.seg_k, A.pad_k)
 PLANS = {
-    "forward": (("flat", "mod") + GIVEN, ("output",) + SAVED + LEFTS, ("lift",)),
-    "backward": (("grad_out", "flat", "mod") + GIVEN + SAVED, GRADS, ("lift",) + WORK),
-    "both": (("grad_out", "flat", "mod") + GIVEN, ("output",) + LEFTS + GRADS, SAVED + ("lift",) + WORK),
+    "forward": ((A.flat, A.mod) + GIVEN, (A.output,) + SAVED + LEFTS, (A.lift,)),
+    "backward": ((A.grad_out, A.marks, A.flat, A.mod) + GIVEN + SAVED, GRADS, (A.lift,) + WORK),
+    "both": ((A.grad_out, A.marks, A.flat, A.mod) + GIVEN, (A.output,) + LEFTS + GRADS, SAVED + (A.lift,) + WORK),
 }
 
 
 def held_names(kind):
     inputs, outputs, others = PLANS[kind]
     names = inputs + outputs + others
-    return tuple(n for n in names if kind != "both" or n != "output")
+    return tuple(n for n in names if kind != "both" or n != A.output)
 
 
 def block_kernel(kind, *refs):
@@ -1433,21 +1567,22 @@
     names = held_names(kind)
     held = dict(zip(names, refs[len(inputs) + len(outputs) :]))
     if kind == "both":
-        held["output"] = held["grad_flat"]
+        held[A.output] = held[A.grad_flat]
     lsem, wsem, tsem, ssem, rsem = refs[len(inputs) + len(outputs) + len(names) :]
     r = Traffic(held, sources, targets, lsem, wsem)
     if kind == "backward":
-        r.fetch("grad_out", "feed", "mod", *EARLY)
-        for t in range(r.reduce.shape[0] // FF_TILE):
-            r.fetch_tile(t, FF_TILE, ("reduce",), ("expanded", "expand"), tsem)
+        r.fetch(A.grad_out, A.feed, A.mod, A.marks, *EARLY)
+        r.more = functools.partial(r.fetch_tile, FF_TILE, (A.reduce,), (A.expanded, A.expand), tsem)
+        r.more(0)
+        r.more(1)
     else:
-        r.fetch("flat", "mod", "triple", *EARLY)
+        r.fetch(A.flat, A.mod, A.triple, *EARLY)
     sibling = meet_sibling()
     if kind != "backward":
         forward_body(r, sibling, ssem, rsem)
     if kind == "both":
-        r.fetch("grad_out")
-        r.loads = {"grad_out": r.loads["grad_out"]}
+        r.fetch(A.grad_out, A.marks)
+        r.loads = {n: r.loads[n] for n in (A.grad_out, A.marks)}
     if kind != "forward":
         backward_body(r, sibling, ssem, rsem)
     r.close()
@@ -1455,8 +1590,8 @@
 
 def run_block(kind, values, name):
     inputs, outputs, others = PLANS[kind]
-    half, width = values["flat"].shape
-    table = block_shapes(half, width, values["reduce"].shape[0])
+    half, width = values[A.flat].shape
+    table = block_shapes(half, width, values[A.reduce].shape[0])
     names = held_names(kind)
     results = pl.pallas_call(
         functools.partial(block_kernel, kind),
@@ -1475,11 +1610,6 @@
     return dict(zip(outputs, results))
 
 
-def shard_rows(values):
-    rows = values.T.reshape(16, -1, values.shape[0])
-    return jnp.pad(rows, ((0, 0), (0, PADDED - rows.shape[1]), (0, 0)))
-
-
 def split_kernel(pieces, in_ref, *refs):
     *outs, held, arrived, left = refs
     for k, (n, row, rows, columns, at) in enumerate(pieces):
@@ -1511,7 +1641,7 @@
             DMA((len(pieces),)),
             DMA((len(pieces),)),
         ],
-        compiler_params=pltpu.CompilerParams(vmem_limit_bytes=32 * 1024 * 1024),
+        compiler_params=pltpu.CompilerParams(vmem_limit_bytes=62 * 1024 * 1024),
     )(values)
 
 
@@ -1631,38 +1761,33 @@
     cond_rows = lax.dynamic_slice_in_dim(all_cond, me * segments, segments, 0)
     cond = pick(cond_rows)
 
-    shared = dict(zip(("cosine", "sine", "seg_q", "seg_k", "pad_k"), context), flat=flat)
-    encoder_in = dict(zip(WEIGHTS + ("gains",), encoder_weights), mod=encoder_modulation, **shared)
+    shared = {**dict(zip(EARLY[1:], context)), A.flat: flat}
+    encoder_in = {**dict(zip(WEIGHTS + EARLY[:1], encoder_weights)), **shared}
+    encoder_in[A.mod] = encoder_modulation
     forward = run_block("forward", encoder_in, "encoder")
-    latent_full = valid * forward["output"]
-    decoder_pre = latent_full + cond
-    decoder_act = jax.nn.silu(decoder_pre).astype(BF16)
-
-    decoder_modulation = dense(decoder_act, modulate) + decoder_offset
-    decoder_in = dict(
-        zip(WEIGHTS + ("gains",), decoder_weights),
-        mod=decoder_modulation,
-        grad_out=valid * cotangent,
-        **shared,
-    )
+    decoder_modulation, decoder_pre, latent, act_xt = decoder_modulation_of(
+        forward[A.output], valid, cond, decoder_offset, modulate
+    )
+    decoder_in = {**dict(zip(WEIGHTS + EARLY[:1], decoder_weights)), **shared}
+    decoder_in[A.mod] = decoder_modulation
+    decoder_in[A.grad_out] = valid * cotangent
+    decoder_in[A.marks] = jnp.ones((8, flat.shape[0]), BF16)
     both = run_block("both", decoder_in, "decoder")
-    velocity = valid * both["output"]
+    velocity = valid * both[A.output]
 
     def pair_up(lefts, grads):
         return (
-            ([lefts["xt1"]], grads["grad_projected"]),
-            ([lefts["xtm"]], grads["grad_attended"]),
-            ([lefts["xt2"]], grads["grad_expanded"]),
-            ([lefts["xth0"], lefts["xth1"], lefts["xth2"]], grads["grad_feed"]),
+            ([lefts[A.xt1]], grads[A.grad_projected]),
+            ([lefts[A.xtm]], grads[A.grad_attended]),
+            ([lefts[A.xt2]], grads[A.grad_expanded]),
+            ([lefts[A.xth0], lefts[A.xth1], lefts[A.xth2]], grads[A.grad_feed]),
         )
 
     factors = pair_up(both, both)
-    grad_modulation = both["grad_mod"]
-    gains_grad = both["gains_grad"]
-    grad_act = dense_back(grad_modulation, modulate)
-    unused_silu, silu_pull = jax.vjp(jax.nn.silu, decoder_pre)
-    grad_latent = valid * silu_pull(grad_act)[0]
-    offset_grad = jnp.sum(grad_modulation, axis=0, dtype=F32)
+    grad_modulation = both[A.grad_mod]
+    gains_grad = both[A.gains_grad]
+    grad_latent = modulation_back(grad_modulation, valid, decoder_pre, modulate)
+    offset_grad = both[A.mark_sums][0]
     extra = jnp.concatenate(
         [
             offset_grad.reshape(16, -1),
@@ -1670,17 +1795,16 @@
         ],
         axis=1,
     )
-    first = ([shard_rows(decoder_act)], grad_modulation)
+    first = ([act_xt], grad_modulation)
     decoder_block = ((factors[1], factors[0], factors[2], first, factors[3]), extra)
 
-    encoder_in["grad_out"] = grad_latent
+    encoder_in[A.grad_out] = grad_latent
+    encoder_in[A.marks] = jnp.pad(picks.T, ((0, 8 - segments), (0, 0))).astype(BF16)
     backward = run_block("backward", {**encoder_in, **forward}, "encoder_back")
     factors = pair_up(forward, backward)
-    grad_modulation = backward["grad_mod"]
-    gains_grad = backward["gains_grad"]
-    grad_rows = lax.dot_general(
-        picks.astype(BF16), grad_modulation, (((0,), (0,)), ((), ())), preferred_element_type=F32
-    )
+    grad_modulation = backward[A.grad_mod]
+    gains_grad = backward[A.gains_grad]
+    grad_rows = backward[A.mark_sums][:segments]
     grad_rows = grad_rows + lax.ppermute(grad_rows, "ctx", [(0, 1), (1, 0)])
     extra = gains_grad.reshape(2, 16, -1).swapaxes(0, 1).reshape(16, -1)
     results, all_rows = fast_reduce(
@@ -1710,8 +1834,8 @@
         encoder_parts[2],
         encoder_parts[3],
     )
-    token_grad = both["grad_flat"] + backward["grad_flat"]
-    return velocity, latent_full, token_grad, encoder_grads, decoder_grads
+    token_grad = both[A.grad_flat] + backward[A.grad_flat]
+    return velocity, latent, token_grad, encoder_grads, decoder_grads
 
 
 def plain_gather(block):

time: 811 us -> 811 us (level)
  matrix products: 28.1 us -> 3.25 us
  Pallas kernels: 741 us -> 762 us
    pallas_call x0 -> x2, Pallas kernels: none -> 19.5 us  [modulation_call(): pl.pallas_call(kernel, name=name, out_shape=outs, in_specs=[in_vmem] * le...]
    dot_general x2 -> x0, matrix products: 14.4 us -> none  [the longest x1 12.5 us: dense_back(): lax.dot_general(grads, weight, (((1,), (1,)), ((), ())), preferred_elemen...]
    dot_general x2 -> x1, matrix products: 11.9 us -> 1.4 us  [dense(): return jnp.dot(values, weight, preferred_element_type=F32)]
where the time goes in v6:
time: 811 us; the launch traced here: 806 us
  Pallas kernels  762 us (94%)
  local copies, waits for them, and re-layouts  23.9 us (3%)
  other arithmetic  14.8 us (2%)
    pallas_call x1, Pallas kernels, scatter(): pl.pallas_call(functools.partial(scatter_kernel, tuple(first), tuple(cols...  319 us
    pallas_call x1, Pallas kernels, gather(): pl.pallas_call(functools.partial(gather_kernel, units, turns, count), nam...  305 us
    pallas_call x3, Pallas kernels, run_block(): pl.pallas_call(functools.partial(block_kernel, kind), name=name, out_shap...  99.1 us
    pallas_call x2, Pallas kernels, modulation_call(): pl.pallas_call(kernel, name=name, out_shape=outs, in_specs=[in_vmem] * le...  19.5 us
  transfers between devices with their start and end apart: 2, of which 0 were waited for; matrix products, arithmetic and copies ran while one was open for 2% of the time, Pallas kernels for 0%

profile of v6, /device:TPU:0, one launch (start us, length us, event | category | flops | bytes accessed | tf_op | source)
XLA Modules:
  0.0 805.7 jit_solution(4145589028663726632)
XLA Ops:
  0.7 0.7 reshape.278
  2.8 1.5 concatenate.21
  4.9 10.7 %small.1 = f32[16,16,128]{2,1,0:T(8,128)} custom-call(f32[16,128]{1,0:T(8,128)} %pad_bitcast_fusion.in_ref), custom_call_target="tpu_custom_call" | custom-call | tf_op jit(solution)/shard_map/small/pallas_call | solution.py:405
  15.6 0.9 copy.67
  17.3 1.4 fusion
  18.7 1.2 reshape.243.refs_9_
  19.9 305.4 %gather.1 = (bf16[4,2,2,72,3456]{4,3,2,1,0:T(8,128)(2,1)}, bf16[4,2,2,72,1152]{4,3,2,1,0:T(8,128)(2,1)}, bf16[4,2,2,72,6144]{4,3,2,1,0:T(8,128)(2,1)}, bf16[4,2,...) custom-call(bf16[72,3456]{1,0:T(8,128)(2,1)} %refs_0_.1, ...), custom_call_target="tpu_custom_call" | custom-call | tf_op jit(solution)/shard_map/gather/pallas_call | solution.py:325
  325.3 1.0 reduce_sum.18
  327.8 0.9 bitcast_convert_fusion.refs_0_.refs_2_
  328.8 0.9 convert_multiply_fusion.refs_0_
  329.8 1.0 select_add_fusion.1.cond
  331.5 1.1 copy.50.refs_4_.refs_6_
  332.6 1.1 copy.49.refs_3_.refs_5_
  333.7 0.7 copy.51.refs_5_.refs_7_
  335.2 0.7 copy.52.valid
  337.8 3.3 select_add_fusion.refs_1_.refs_3_
  341.1 22.9 %encoder.1 = (f32[128,1152]{1,0:T(8,128)}, f32[128,2304]{1,0:T(8,128)}, bf16[128,1152]{1,0:T(8,128)(2,1)}, bf16[2,256,1152]{2,1,0:T(8,128)(2,1)}, f32[128,128]{1...) custom-call(f32[128,1152]{1,0:T(8,128)} %bitcast_convert_fusion.refs, ...), custom_call_target="tpu_custom_call" | custom-call | tf_op jit(solution)/shard_map/encoder/pallas_call | solution.py:1596
  364.0 9.5 %modulation.1 = (f32[128,6912]{1,0:T(8,128)}, f32[128,1152]{1,0:T(8,128)}, bf16[128,1152]{1,0:T(8,128)(2,1)}, bf16[16,80,128]{2,1,0:T(8,128)(2,1)}) custom-call(f32[128,1152]{1,0:T(8,128)} %get-tuple-element.84.block, f32[128,1]{1,0:T(8,128)} %copy.52.valid, f32[128,1152]{1,0:T(8,128)} %select_add_fusion.1.cond, f32[1,6912]{1,0:T(1,128)} %reshape_reshape.3.offset, ...), custom_call_target="tpu_custom_call" | custom-call | tf_op jit(solution)/shard_map/modulation/pallas_call | solution.py:1127
  374.1 45.3 %decoder.1 = (f32[128,1152]{1,0:T(8,128)}, bf16[16,80,128]{2,1,0:T(8,128)(2,1)}, bf16[16,80,128]{2,1,0:T(8,128)(2,1)}, bf16[16,80,128]{2,1,0:T(8,128)(2,1)}, bf1...) custom-call(f32[128,1152]{1,0:T(8,128)} %convert_multiply_fusion.ref, ...), custom_call_target="tpu_custom_call" | custom-call | tf_op jit(solution)/shard_map/decoder/pallas_call | solution.py:1596
  419.4 10.0 %modulation_back.1.refs_0_ = f32[128,1152]{1,0:T(8,128)} custom-call(bf16[128,6912]{1,0:T(8,128)(2,1)} %get-tuple-element.94.grad.refs_18_, f32[128,1]{1,0:T(8,128)} %copy.52.valid, f32[128,1152]{1,0:T(8,128)} %get-tuple-element.95.before, bf16[1152,6912]{1,0:T(8,128)(2,1)} %bitcast.71), custom_call_target="tpu_custom_call" | custom-call | tf_op jit(solution)/shard_map/modulation_back/pallas_call | solution.py:1127
  429.5 30.9 %encoder_back.1 = (f32[128,1152]{1,0:T(8,128)}, bf16[128,6912]{1,0:T(8,128)(2,1)}, bf16[128,1152]{1,0:T(8,128)(2,1)}, bf16[128,6144]{1,0:T(8,128)(2,1)}, bf16[12...) custom-call(f32[128,1152]{1,0:T(8,128)} %modulation_back.1.refs_0_, ...), custom_call_target="tpu_custom_call" | custom-call | tf_op jit(solution)/shard_map/encoder_back/pallas_call | solution.py:1596
  460.4 1.0 slice.98
  461.7 1.0 fusion.8
  463.1 1.9 fusion.2
  464.9 1.9 add_bitcast_fusion
  467.9 0.8 pad.33.refs_7_
  468.7 0.8 pad.35.refs_14_
  469.5 0.7 reshape.269.refs_26_
  470.3 319.3 %scatter.1 = (f32[72,36096]{1,0:T(8,128)}, bf16[4,2,2,16,1728]{4,3,2,1,0:T(8,128)(2,1)}) custom-call(bf16[16,80,128]{2,1,0:T(8,128)(2,1)} %get-tuple-element.105.refs_0_, bf16[16,80,128]{2,1,0:T(8,128)(2,1)} %get-tuple-element.106.refs_1_, bf16[16,80,128]{2,1,0:T(8,128)(2,1)} %get-tuple-element.107.refs_2_, bf16[16,80,128]{2,1,0:T(8,128)(2,1)} %get-tuple-element.108.refs_3_, ...), custom_call_target="tpu_custom_call" | custom-call | tf_op jit(solution)/shard_map/scatter/pallas_call | solution.py:738
  789.6 2.1 reshape.270
  791.7 1.8 fusion.21
  793.7 7.9 split.1
  (83 shorter events, 14.1 us)
Async XLA Ops:
  19.9 307.0 %copy-start.4 = (s32[1,256]{1,0:T(1,128)S(1)}, s32[1,256]{1,0:T(1,128)}, u32[]{:S(2)}) copy-start(s32[1,256]{1,0:T(1,128)} %refs_8_.5) | copy-start | bytes 3076
  19.9 307.0 %copy-start.5 = (s32[1,256]{1,0:T(1,128)S(1)}, s32[1,256]{1,0:T(1,128)}, u32[]{:S(2)}) copy-start(s32[1,256]{1,0:T(1,128)} %refs_9_.3) | copy-start | bytes 3076
  19.9 307.7 %copy-start.7 = (s32[1,256]{1,0:T(1,128)S(1)}, s32[1,256]{1,0:T(1,128)}, u32[]{:S(2)}) copy-start(s32[1,256]{1,0:T(1,128)} %param.24) | copy-start | bytes 3076
  19.9 307.7 %copy-start.8 = (s32[1,256]{1,0:T(1,128)S(1)}, s32[1,256]{1,0:T(1,128)}, u32[]{:S(2)}) copy-start(s32[1,256]{1,0:T(1,128)} %param.25) | copy-start | bytes 3076
  19.9 308.0 %copy-start.1 = (bf16[1,128,1152]{2,1,0:T(8,128)(2,1)S(1)}, bf16[1,128,1152]{2,1,0:T(8,128)(2,1)}, u32[]{:S(2)}) copy-start(bf16[1,128,1152]{2,1,0:T(8,128)(2,1)} %param.21) | copy-start | bytes 884740
  19.9 309.0 %copy-start.2 = (bf16[1,128,1152]{2,1,0:T(8,128)(2,1)S(1)}, bf16[1,128,1152]{2,1,0:T(8,128)(2,1)}, u32[]{:S(2)}) copy-start(bf16[1,128,1152]{2,1,0:T(8,128)(2,1)} %param.22) | copy-start | bytes 884740
  326.4 11.1 %collective-permute-start = (f32[4,3456]{1,0:T(4,128)S(1)}, f32[4,3456]{1,0:T(4,128)S(1)}, u32[]{:S(2)}, u32[]{:S(2)}) collective-permute-start(f32[4,3456]{1,0:T(4,128)S(1)} %reshape.244), channel_id=1, source_target_pairs={{0,1},{1,0},{2,3},{3,2},{4,5},{5,4},{6,7},{7,6},{8,9},{9,8},{10,11... | collective-permute-start | bytes 165896 | tf_op jit(solution)/shard_map/ppermute | solution.py:1749
  429.5 33.4 %copy-start.6 = (f32[2,1152]{1,0:T(2,128)S(1)}, f32[2,1152]{1,0:T(2,128)}, u32[]{:S(2)}) copy-start(f32[2,1152]{1,0:T(2,128)} %get-tuple-element.113) | copy-start | bytes 27652
  429.5 35.5 %copy-start = (f32[128,1152]{1,0:T(8,128)S(1)}, f32[128,1152]{1,0:T(8,128)}, u32[]{:S(2)}) copy-start(f32[128,1152]{1,0:T(8,128)} %get-tuple-element.93) | copy-start | bytes 1769476
  460.4 9.1 %copy-start.3 = (f32[8,6912]{1,0:T(8,128)S(1)}, f32[8,6912]{1,0:T(8,128)}, u32[]{:S(2)}) copy-start(f32[8,6912]{1,0:T(8,128)} %get-tuple-element.129) | copy-start | bytes 663556
  461.5 8.0 collective-permute-start.1

commit v7 on v6

--- a/solution.py
+++ b/solution.py
@@ -345,14 +345,14 @@
 
 
 ORDERS = (
-    ("zyx", "zxy", "xyz", "zxy", "zyx", "zxy", "zyx", "yxz", "zyx", "zxy"),
-    ("zxy", "zyx", "yxz", "zyx", "zxy", "zyx", "zxy", "xyz", "zxy", "zyx"),
+    ("zyx", "zxy", "xyz", "zxy", "zyx", "zyx", "yxz", "zxy", "zyx"),
+    ("zxy", "zyx", "yxz", "zyx", "zxy", "zxy", "xyz", "zyx", "zxy"),
 )
-AFTER_Z = (0.6165, 0.4168, 0.3474, 1.6339, 4.4601)
+AFTER_Z = (0.6165, 0.5838, 0.5725, 1.6339, 4.1589)
 AFTER_XY = (1.5672, 1.5028, 1.8589, 1.1737, 2.0677)
-PER_TURN = 2.2835
+PER_TURN = 2.2146
 FORWARD_AT = 40
-SHIFT = 0.1931
+SHIFT = 0.5711
 SIZE = 4
 TAIL = (0.1, 2)
 
@@ -413,8 +413,7 @@
     )(values)
 
 
-LAG = (0, 2, 3, 4, 5, 6)
-RECV_SLOTS = 9
+RECV_SLOTS = 10
 SEND_SLOTS = 8
 FIRST_SLOTS = 4
 UNIT = 384
@@ -685,16 +684,16 @@
                 pl.when(down_sends(k))(lambda k=k, e=e: down_copy(i, k, e).wait_send())
 
     stages = (
-        (a_fifth, LAG[5]),
-        (functools.partial(z_step, k=1, e=False), LAG[3]),
-        (functools.partial(z_step, k=2, e=True), LAG[3]),
-        (e_fourth, LAG[4]),
-        (stage0, LAG[0]),
-        (functools.partial(z_step, k=1, e=True), LAG[2]),
-        (a_second, LAG[2]),
-        (functools.partial(z_step, k=2, e=False), LAG[4]),
-        (e_fifth, LAG[5]),
-        (stage1, LAG[1]),
+        (a_second, 4),
+        (functools.partial(z_step, k=2, e=False), 5),
+        (e_fourth, 5),
+        (functools.partial(z_step, k=1, e=False), 4),
+        (a_fifth, 6),
+        (functools.partial(z_step, k=1, e=True), 3),
+        (stage0, 0),
+        (e_fifth, 7),
+        (functools.partial(z_step, k=2, e=True), 3),
+        (stage1, 2),
     )
 
     def tick(t, carry):

time: 811 us -> 802 us (0.989)
  Pallas kernels: 762 us -> 753 us
where the time goes in v7:
time: 802 us; the launch traced here: 797 us
  Pallas kernels  753 us (94%)
  local copies, waits for them, and re-layouts  23.9 us (3%)
  other arithmetic  14.8 us (2%)
    pallas_call x1, Pallas kernels, scatter(): pl.pallas_call(functools.partial(scatter_kernel, tuple(first), tuple(cols...  316 us
    pallas_call x1, Pallas kernels, gather(): pl.pallas_call(functools.partial(gather_kernel, units, turns, count), nam...  300 us
    pallas_call x3, Pallas kernels, run_block(): pl.pallas_call(functools.partial(block_kernel, kind), name=name, out_shap...  99.1 us
    pallas_call x2, Pallas kernels, modulation_call(): pl.pallas_call(kernel, name=name, out_shape=outs, in_specs=[in_vmem] * le...  19.5 us
  transfers between devices with their start and end apart: 2, of which 0 were waited for; matrix products, arithmetic and copies ran while one was open for 2% of the time, Pallas kernels for 0%

profile of v7, /device:TPU:0, one launch (start us, length us, event | category | flops | bytes accessed | tf_op | source)
XLA Modules:
  0.0 797.1 jit_solution(271155594716728347)
XLA Ops:
  0.7 0.7 reshape.278
  2.8 1.5 concatenate.21
  4.9 10.7 %small.1 = f32[16,16,128]{2,1,0:T(8,128)} custom-call(f32[16,128]{1,0:T(8,128)} %pad_bitcast_fusion.in_ref), custom_call_target="tpu_custom_call" | custom-call | tf_op jit(solution)/shard_map/small/pallas_call | solution.py:405
  15.6 0.9 copy.67
  17.3 1.4 fusion
  18.7 1.2 reshape.243.refs_9_
  19.9 299.7 %gather.1 = (bf16[4,2,2,72,3456]{4,3,2,1,0:T(8,128)(2,1)}, bf16[4,2,2,72,1152]{4,3,2,1,0:T(8,128)(2,1)}, bf16[4,2,2,72,6144]{4,3,2,1,0:T(8,128)(2,1)}, bf16[4,2,...) custom-call(bf16[72,3456]{1,0:T(8,128)(2,1)} %refs_0_.1, ...), custom_call_target="tpu_custom_call" | custom-call | tf_op jit(solution)/shard_map/gather/pallas_call | solution.py:325
  319.6 1.0 reduce_sum.18
  322.1 0.9 bitcast_convert_fusion.refs_0_.refs_2_
  323.2 0.9 convert_multiply_fusion.refs_0_
  324.1 1.0 select_add_fusion.1.cond
  325.9 1.1 copy.50.refs_4_.refs_6_
  327.0 1.1 copy.49.refs_3_.refs_5_
  328.0 0.7 copy.51.refs_5_.refs_7_
  329.5 0.7 copy.52.valid
  332.1 3.3 select_add_fusion.refs_1_.refs_3_
  335.4 22.9 %encoder.1 = (f32[128,1152]{1,0:T(8,128)}, f32[128,2304]{1,0:T(8,128)}, bf16[128,1152]{1,0:T(8,128)(2,1)}, bf16[2,256,1152]{2,1,0:T(8,128)(2,1)}, f32[128,128]{1...) custom-call(f32[128,1152]{1,0:T(8,128)} %bitcast_convert_fusion.refs, ...), custom_call_target="tpu_custom_call" | custom-call | tf_op jit(solution)/shard_map/encoder/pallas_call | solution.py:1595
  358.3 9.5 %modulation.1 = (f32[128,6912]{1,0:T(8,128)}, f32[128,1152]{1,0:T(8,128)}, bf16[128,1152]{1,0:T(8,128)(2,1)}, bf16[16,80,128]{2,1,0:T(8,128)(2,1)}) custom-call(f32[128,1152]{1,0:T(8,128)} %get-tuple-element.84.block, f32[128,1]{1,0:T(8,128)} %copy.52.valid, f32[128,1152]{1,0:T(8,128)} %select_add_fusion.1.cond, f32[1,6912]{1,0:T(1,128)} %reshape_reshape.3.offset, ...), custom_call_target="tpu_custom_call" | custom-call | tf_op jit(solution)/shard_map/modulation/pallas_call | solution.py:1126
  368.4 45.3 %decoder.1 = (f32[128,1152]{1,0:T(8,128)}, bf16[16,80,128]{2,1,0:T(8,128)(2,1)}, bf16[16,80,128]{2,1,0:T(8,128)(2,1)}, bf16[16,80,128]{2,1,0:T(8,128)(2,1)}, bf1...) custom-call(f32[128,1152]{1,0:T(8,128)} %convert_multiply_fusion.ref, ...), custom_call_target="tpu_custom_call" | custom-call | tf_op jit(solution)/shard_map/decoder/pallas_call | solution.py:1595
  413.7 10.0 %modulation_back.1.refs_0_ = f32[128,1152]{1,0:T(8,128)} custom-call(bf16[128,6912]{1,0:T(8,128)(2,1)} %get-tuple-element.94.grad.refs_18_, f32[128,1]{1,0:T(8,128)} %copy.52.valid, f32[128,1152]{1,0:T(8,128)} %get-tuple-element.95.before, bf16[1152,6912]{1,0:T(8,128)(2,1)} %bitcast.71), custom_call_target="tpu_custom_call" | custom-call | tf_op jit(solution)/shard_map/modulation_back/pallas_call | solution.py:1126
  423.8 30.9 %encoder_back.1 = (f32[128,1152]{1,0:T(8,128)}, bf16[128,6912]{1,0:T(8,128)(2,1)}, bf16[128,1152]{1,0:T(8,128)(2,1)}, bf16[128,6144]{1,0:T(8,128)(2,1)}, bf16[12...) custom-call(f32[128,1152]{1,0:T(8,128)} %modulation_back.1.refs_0_, ...), custom_call_target="tpu_custom_call" | custom-call | tf_op jit(solution)/shard_map/encoder_back/pallas_call | solution.py:1595
  454.7 1.0 slice.98
  456.0 1.0 fusion.8
  457.4 1.9 fusion.2
  459.2 1.9 add_bitcast_fusion
  462.2 0.8 pad.33.refs_7_
  463.0 0.8 pad.35.refs_14_
  463.8 0.7 reshape.269.refs_26_
  464.6 316.4 %scatter.1 = (f32[72,36096]{1,0:T(8,128)}, bf16[4,2,2,16,1728]{4,3,2,1,0:T(8,128)(2,1)}) custom-call(bf16[16,80,128]{2,1,0:T(8,128)(2,1)} %get-tuple-element.105.refs_0_, bf16[16,80,128]{2,1,0:T(8,128)(2,1)} %get-tuple-element.106.refs_1_, bf16[16,80,128]{2,1,0:T(8,128)(2,1)} %get-tuple-element.107.refs_2_, bf16[16,80,128]{2,1,0:T(8,128)(2,1)} %get-tuple-element.108.refs_3_, ...), custom_call_target="tpu_custom_call" | custom-call | tf_op jit(solution)/shard_map/scatter/pallas_call | solution.py:737
  781.0 2.1 reshape.270
  783.1 1.8 fusion.21
  785.1 7.9 split.1
  (83 shorter events, 14.1 us)
Async XLA Ops:
  19.9 301.3 %copy-start.4 = (s32[1,256]{1,0:T(1,128)S(1)}, s32[1,256]{1,0:T(1,128)}, u32[]{:S(2)}) copy-start(s32[1,256]{1,0:T(1,128)} %refs_8_.5) | copy-start | bytes 3076
  19.9 301.3 %copy-start.5 = (s32[1,256]{1,0:T(1,128)S(1)}, s32[1,256]{1,0:T(1,128)}, u32[]{:S(2)}) copy-start(s32[1,256]{1,0:T(1,128)} %refs_9_.3) | copy-start | bytes 3076
  19.9 302.0 %copy-start.7 = (s32[1,256]{1,0:T(1,128)S(1)}, s32[1,256]{1,0:T(1,128)}, u32[]{:S(2)}) copy-start(s32[1,256]{1,0:T(1,128)} %param.24) | copy-start | bytes 3076
  19.9 302.0 %copy-start.8 = (s32[1,256]{1,0:T(1,128)S(1)}, s32[1,256]{1,0:T(1,128)}, u32[]{:S(2)}) copy-start(s32[1,256]{1,0:T(1,128)} %param.25) | copy-start | bytes 3076
  19.9 302.3 %copy-start.1 = (bf16[1,128,1152]{2,1,0:T(8,128)(2,1)S(1)}, bf16[1,128,1152]{2,1,0:T(8,128)(2,1)}, u32[]{:S(2)}) copy-start(bf16[1,128,1152]{2,1,0:T(8,128)(2,1)} %param.21) | copy-start | bytes 884740
  19.9 303.3 %copy-start.2 = (bf16[1,128,1152]{2,1,0:T(8,128)(2,1)S(1)}, bf16[1,128,1152]{2,1,0:T(8,128)(2,1)}, u32[]{:S(2)}) copy-start(bf16[1,128,1152]{2,1,0:T(8,128)(2,1)} %param.22) | copy-start | bytes 884740
  320.7 11.1 %collective-permute-start = (f32[4,3456]{1,0:T(4,128)S(1)}, f32[4,3456]{1,0:T(4,128)S(1)}, u32[]{:S(2)}, u32[]{:S(2)}) collective-permute-start(f32[4,3456]{1,0:T(4,128)S(1)} %reshape.244), channel_id=1, source_target_pairs={{0,1},{1,0},{2,3},{3,2},{4,5},{5,4},{6,7},{7,6},{8,9},{9,8},{10,11... | collective-permute-start | bytes 165896 | tf_op jit(solution)/shard_map/ppermute | solution.py:1748
  423.8 33.4 %copy-start.6 = (f32[2,1152]{1,0:T(2,128)S(1)}, f32[2,1152]{1,0:T(2,128)}, u32[]{:S(2)}) copy-start(f32[2,1152]{1,0:T(2,128)} %get-tuple-element.113) | copy-start | bytes 27652
  423.8 35.5 %copy-start = (f32[128,1152]{1,0:T(8,128)S(1)}, f32[128,1152]{1,0:T(8,128)}, u32[]{:S(2)}) copy-start(f32[128,1152]{1,0:T(8,128)} %get-tuple-element.93) | copy-start | bytes 1769476
  454.7 9.1 %copy-start.3 = (f32[8,6912]{1,0:T(8,128)S(1)}, f32[8,6912]{1,0:T(8,128)}, u32[]{:S(2)}) copy-start(f32[8,6912]{1,0:T(8,128)} %get-tuple-element.129) | copy-start | bytes 663556
  455.8 8.0 %collective-permute-start.1 = (f32[4,6912]{1,0:T(4,128)S(1)}, f32[4,6912]{1,0:T(4,128)S(1)}, u32[]{:S(2)}, u32[]{:S(2)}) collective-permute-start(f32[4,6912]{1,0:T(4,128)S(1)} %slice.98), channel_id=1, source_target_pairs={{0,1},{1,0},{2,3},{3,2},{4,5},{5,4},{6,7},{7,6},{8,9},{9,8},{10,11... | collective-permute-start | bytes 331784 | tf_op jit(solution)/shard_map/ppermute | solution.py:1807

commit v8 on v7

--- a/solution.py
+++ b/solution.py
@@ -698,7 +698,7 @@
 
     def tick(t, carry):
         arrive(t)
-        pl.when(t == 4)(side.forward)
+        pl.when(t == 14)(side.forward)
         pl.when((t >= SEND_SLOTS) & (t - SEND_SLOTS < total))(lambda: sent(t - SEND_SLOTS))
         pl.when((t >= FIRST_SLOTS) & (t - FIRST_SLOTS < total))(lambda: first_sent(t - FIRST_SLOTS))
         for stage, lag in stages:
@@ -1234,6 +1234,16 @@
             copy.start()
         self.waiting.difference_update(rows + columns)
 
+    def fetch_parts(self, n, width, order, sem):
+        for k in order:
+            at = (slice(None), pl.ds(k * width, width))
+            copy = pltpu.make_async_copy(
+                self.sources[n].at[at], self.held[n].at[at], sem.at[0, k]
+            )
+            copy.start()
+            self.tiles[n, k] = [copy]
+        self.waiting.discard(n)
+
     def need_tile(self, t):
         for copy in self.tiles.pop(t, ()):
             copy.wait()
@@ -1267,8 +1277,6 @@
     r.need(A.flat, A.mod)
     normed, unused = normalize(r.flat[...])
     lifted_low = (normed * (1.0 + part(1)) + part(0)).astype(BF16)
-    r.need(A.triple)
-    r.fetch(A.mixing, A.expand, A.reduce)
     heads = head_sum_matrix(width)
 
     def prepared(k):
@@ -1278,11 +1286,13 @@
         return scaled * r.cosine[...] + swap_pairs(scaled) * r.sine[...]
 
     def project(k):
+        r.need_tile((A.triple, k))
         return jnp.dot(
             lifted_low, r.triple[:, k * width : (k + 1) * width], preferred_element_type=F32
         )
 
     r.raw[:, width:] = project(1)
+    r.fetch(A.mixing, A.expand, A.reduce)
     r.need(A.gains, A.cosine, A.sine)
     r.kv[0, mine] = prepared(1).astype(BF16)
     r.kv[1, mine] = project(2).astype(BF16)
@@ -1575,7 +1585,8 @@
         r.more(0)
         r.more(1)
     else:
-        r.fetch(A.flat, A.mod, A.triple, *EARLY)
+        r.fetch(A.flat, A.mod, *EARLY)
+        r.fetch_parts(A.triple, r.flat.shape[1], (1, 2, 0), tsem)
     sibling = meet_sibling()
     if kind != "backward":
         forward_body(r, sibling, ssem, rsem)

time: 802 us -> 800 us (level)
  no operation moved by 1% of the time
where the time goes in v8:
time: 800 us; the launch traced here: 795 us
  Pallas kernels  751 us (94%)
  local copies, waits for them, and re-layouts  23.9 us (3%)
  other arithmetic  14.8 us (2%)
    pallas_call x1, Pallas kernels, scatter(): pl.pallas_call(functools.partial(scatter_kernel, tuple(first), tuple(cols...  316 us
    pallas_call x1, Pallas kernels, gather(): pl.pallas_call(functools.partial(gather_kernel, units, turns, count), nam...  300 us
    pallas_call x3, Pallas kernels, run_block(): pl.pallas_call(functools.partial(block_kernel, kind), name=name, out_shap...  97.1 us
    pallas_call x2, Pallas kernels, modulation_call(): pl.pallas_call(kernel, name=name, out_shape=outs, in_specs=[in_vmem] * le...  19.5 us
  transfers between devices with their start and end apart: 2, of which 0 were waited for; matrix products, arithmetic and copies ran while one was open for 2% of the time, Pallas kernels for 0%

profile of v8, /device:TPU:0, one launch (start us, length us, event | category | flops | bytes accessed | tf_op | source)
XLA Modules:
  0.0 795.0 jit_solution(654378992592879963)
XLA Ops:
  0.7 0.7 reshape.278
  2.8 1.5 concatenate.21
  4.9 10.7 %small.1 = f32[16,16,128]{2,1,0:T(8,128)} custom-call(f32[16,128]{1,0:T(8,128)} %pad_bitcast_fusion.in_ref), custom_call_target="tpu_custom_call" | custom-call | tf_op jit(solution)/shard_map/small/pallas_call | solution.py:405
  15.6 0.9 copy.67
  17.3 1.4 fusion
  18.7 1.2 reshape.243.refs_9_
  19.9 299.7 %gather.1 = (bf16[4,2,2,72,3456]{4,3,2,1,0:T(8,128)(2,1)}, bf16[4,2,2,72,1152]{4,3,2,1,0:T(8,128)(2,1)}, bf16[4,2,2,72,6144]{4,3,2,1,0:T(8,128)(2,1)}, bf16[4,2,...) custom-call(bf16[72,3456]{1,0:T(8,128)(2,1)} %refs_0_.1, ...), custom_call_target="tpu_custom_call" | custom-call | tf_op jit(solution)/shard_map/gather/pallas_call | solution.py:325
  319.6 1.0 reduce_sum.18
  322.1 0.9 bitcast_convert_fusion.refs_0_.refs_2_
  323.2 0.9 convert_multiply_fusion.refs_0_
  324.1 1.0 select_add_fusion.1.cond
  325.9 1.1 copy.50.refs_4_.refs_6_
  327.0 1.1 copy.49.refs_3_.refs_5_
  328.0 0.7 copy.51.refs_5_.refs_7_
  329.5 0.7 copy.52.valid
  332.1 3.3 select_add_fusion.refs_1_.refs_3_
  335.4 21.8 %encoder.1 = (f32[128,1152]{1,0:T(8,128)}, f32[128,2304]{1,0:T(8,128)}, bf16[128,1152]{1,0:T(8,128)(2,1)}, bf16[2,256,1152]{2,1,0:T(8,128)(2,1)}, f32[128,128]{1...) custom-call(f32[128,1152]{1,0:T(8,128)} %bitcast_convert_fusion.refs, ...), custom_call_target="tpu_custom_call" | custom-call | tf_op jit(solution)/shard_map/encoder/pallas_call | solution.py:1606
  357.3 9.5 %modulation.1 = (f32[128,6912]{1,0:T(8,128)}, f32[128,1152]{1,0:T(8,128)}, bf16[128,1152]{1,0:T(8,128)(2,1)}, bf16[16,80,128]{2,1,0:T(8,128)(2,1)}) custom-call(f32[128,1152]{1,0:T(8,128)} %get-tuple-element.84.block, f32[128,1]{1,0:T(8,128)} %copy.52.valid, f32[128,1152]{1,0:T(8,128)} %select_add_fusion.1.cond, f32[1,6912]{1,0:T(1,128)} %reshape_reshape.3.offset, ...), custom_call_target="tpu_custom_call" | custom-call | tf_op jit(solution)/shard_map/modulation/pallas_call | solution.py:1126
  367.3 44.3 %decoder.1 = (f32[128,1152]{1,0:T(8,128)}, bf16[16,80,128]{2,1,0:T(8,128)(2,1)}, bf16[16,80,128]{2,1,0:T(8,128)(2,1)}, bf16[16,80,128]{2,1,0:T(8,128)(2,1)}, bf1...) custom-call(f32[128,1152]{1,0:T(8,128)} %convert_multiply_fusion.ref, ...), custom_call_target="tpu_custom_call" | custom-call | tf_op jit(solution)/shard_map/decoder/pallas_call | solution.py:1606
  411.6 10.1 %modulation_back.1.refs_0_ = f32[128,1152]{1,0:T(8,128)} custom-call(bf16[128,6912]{1,0:T(8,128)(2,1)} %get-tuple-element.94.grad.refs_18_, f32[128,1]{1,0:T(8,128)} %copy.52.valid, f32[128,1152]{1,0:T(8,128)} %get-tuple-element.95.before, bf16[1152,6912]{1,0:T(8,128)(2,1)} %bitcast.71), custom_call_target="tpu_custom_call" | custom-call | tf_op jit(solution)/shard_map/modulation_back/pallas_call | solution.py:1126
  421.7 31.0 %encoder_back.1 = (f32[128,1152]{1,0:T(8,128)}, bf16[128,6912]{1,0:T(8,128)(2,1)}, bf16[128,1152]{1,0:T(8,128)(2,1)}, bf16[128,6144]{1,0:T(8,128)(2,1)}, bf16[12...) custom-call(f32[128,1152]{1,0:T(8,128)} %modulation_back.1.refs_0_, ...), custom_call_target="tpu_custom_call" | custom-call | tf_op jit(solution)/shard_map/encoder_back/pallas_call | solution.py:1606
  452.7 1.0 slice.98
  453.9 1.0 fusion.8
  455.2 1.9 fusion.2
  457.1 1.9 add_bitcast_fusion
  460.1 0.8 pad.33.refs_7_
  460.9 0.8 pad.35.refs_14_
  461.7 0.7 reshape.269.refs_26_
  462.5 316.4 %scatter.1 = (f32[72,36096]{1,0:T(8,128)}, bf16[4,2,2,16,1728]{4,3,2,1,0:T(8,128)(2,1)}) custom-call(bf16[16,80,128]{2,1,0:T(8,128)(2,1)} %get-tuple-element.105.refs_0_, bf16[16,80,128]{2,1,0:T(8,128)(2,1)} %get-tuple-element.106.refs_1_, bf16[16,80,128]{2,1,0:T(8,128)(2,1)} %get-tuple-element.107.refs_2_, bf16[16,80,128]{2,1,0:T(8,128)(2,1)} %get-tuple-element.108.refs_3_, ...), custom_call_target="tpu_custom_call" | custom-call | tf_op jit(solution)/shard_map/scatter/pallas_call | solution.py:737
  778.9 2.1 reshape.270
  781.0 1.9 fusion.21
  783.0 7.9 split.1
  (83 shorter events, 14.1 us)
Async XLA Ops:
  19.9 301.3 %copy-start.4 = (s32[1,256]{1,0:T(1,128)S(1)}, s32[1,256]{1,0:T(1,128)}, u32[]{:S(2)}) copy-start(s32[1,256]{1,0:T(1,128)} %refs_8_.5) | copy-start | bytes 3076
  19.9 301.3 %copy-start.5 = (s32[1,256]{1,0:T(1,128)S(1)}, s32[1,256]{1,0:T(1,128)}, u32[]{:S(2)}) copy-start(s32[1,256]{1,0:T(1,128)} %refs_9_.3) | copy-start | bytes 3076
  19.9 302.0 %copy-start.7 = (s32[1,256]{1,0:T(1,128)S(1)}, s32[1,256]{1,0:T(1,128)}, u32[]{:S(2)}) copy-start(s32[1,256]{1,0:T(1,128)} %param.24) | copy-start | bytes 3076
  19.9 302.0 %copy-start.8 = (s32[1,256]{1,0:T(1,128)S(1)}, s32[1,256]{1,0:T(1,128)}, u32[]{:S(2)}) copy-start(s32[1,256]{1,0:T(1,128)} %param.25) | copy-start | bytes 3076
  19.9 302.3 %copy-start.1 = (bf16[1,128,1152]{2,1,0:T(8,128)(2,1)S(1)}, bf16[1,128,1152]{2,1,0:T(8,128)(2,1)}, u32[]{:S(2)}) copy-start(bf16[1,128,1152]{2,1,0:T(8,128)(2,1)} %param.21) | copy-start | bytes 884740
  19.9 303.3 %copy-start.2 = (bf16[1,128,1152]{2,1,0:T(8,128)(2,1)S(1)}, bf16[1,128,1152]{2,1,0:T(8,128)(2,1)}, u32[]{:S(2)}) copy-start(bf16[1,128,1152]{2,1,0:T(8,128)(2,1)} %param.22) | copy-start | bytes 884740
  320.7 11.1 %collective-permute-start = (f32[4,3456]{1,0:T(4,128)S(1)}, f32[4,3456]{1,0:T(4,128)S(1)}, u32[]{:S(2)}, u32[]{:S(2)}) collective-permute-start(f32[4,3456]{1,0:T(4,128)S(1)} %reshape.244), channel_id=1, source_target_pairs={{0,1},{1,0},{2,3},{3,2},{4,5},{5,4},{6,7},{7,6},{8,9},{9,8},{10,11... | collective-permute-start | bytes 165896 | tf_op jit(solution)/shard_map/ppermute | solution.py:1759
  421.6 33.4 %copy-start.6 = (f32[2,1152]{1,0:T(2,128)S(1)}, f32[2,1152]{1,0:T(2,128)}, u32[]{:S(2)}) copy-start(f32[2,1152]{1,0:T(2,128)} %get-tuple-element.113) | copy-start | bytes 27652
  421.7 35.5 %copy-start = (f32[128,1152]{1,0:T(8,128)S(1)}, f32[128,1152]{1,0:T(8,128)}, u32[]{:S(2)}) copy-start(f32[128,1152]{1,0:T(8,128)} %get-tuple-element.93) | copy-start | bytes 1769476
  452.6 9.0 %copy-start.3 = (f32[8,6912]{1,0:T(8,128)S(1)}, f32[8,6912]{1,0:T(8,128)}, u32[]{:S(2)}) copy-start(f32[8,6912]{1,0:T(8,128)} %get-tuple-element.129) | copy-start | bytes 663556
  453.7 8.0 %collective-permute-start.1 = (f32[4,6912]{1,0:T(4,128)S(1)}, f32[4,6912]{1,0:T(4,128)S(1)}, u32[]{:S(2)}, u32[]{:S(2)}) collective-permute-start(f32[4,6912]{1,0:T(4,128)S(1)} %slice.98), channel_id=1, source_target_pairs={{0,1},{1,0},{2,3},{3,2},{4,5},{5,4},{6,7},{7,6},{8,9},{9,8},{10,11... | collective-permute-start | bytes 331784 | tf_op jit(solution)/shard_map/ppermute | solution.py:1818
